TPU v7x, 512 devices: a whole 4x8x8 slice. The times are simulated.
512 devices in a mesh: section: 2 (over x_hi), ep: 128 (over y, z, core), tp: 2 (over x_lo).
Axes of the slice: x: 4 (x_hi: 2, x_lo: 2; x = x_hi * 2 + x_lo), y: 8, z: 8, core: 2. Of those that a mesh axis runs over, the one named last changes fastest.
Arguments:
- section_rows: bfloat16 [2, 512, 7168], P('section', 'ep', 'tp'), may hold values from -6 to 6
- routes: int32 [2, 512, 4], P('section', 'ep'), may hold values from 0 to 7, all different within a row; in each aligned block of 4 rows (0 to 3, 4 to 7, ..., all dimensions but the last counted through in order) at most 3 rows name the same one
- route_weights: float32 [2, 512, 4], P('section', 'ep'), may hold values from 0.1 to 0.5
- in_gain: bfloat16 [2, 7168], P('section', 'tp'), may hold values from 0.099609375 to 1.8984375
- gate_up: bfloat16 [2, 128, 7168, 256], P('section', 'ep', 'tp'), may hold values from -0.0625 to 0.0625
- down: bfloat16 [2, 128, 128, 7168], P('section', 'ep', None, 'tp'), may hold values from -0.125 to 0.125
- out_gain: bfloat16 [2, 7168], P('section', 'tp'), may hold values from 0.099609375 to 1.8984375
Outputs:
- layer_out: bfloat16 [2, 512, 7168], P('section', 'ep', 'tp')
- handed: bfloat16 [2, 512, 7168], P('section', 'ep', 'tp')
Inputs may be any that keep to these rules, and one draw needn't show every extreme that they name: `routes`: each row names 4 different experts. Among the 4 rows of one index of ep (aligned blocks of rows, both groups counted in order), no expert is named by more than 3 rows, a bound that some block reaches.
All inputs are finite; a program needn't handle non-finite values.
Results may differ from a plain program's by a relative error of at most 0.012.
Values may be sent and summed in bfloat16 or wider, within the bound.
No kernel may reach another device: no remote copies, remote signals or barrier semaphores. Data moves between devices by JAX's collectives and lax.ppermute only.
A program may use at most 64 MiB of HBM per device.

v0:
```python
import jax
import jax.numpy as jnp
from jax import lax
from jax.sharding import PartitionSpec as P


def swapped(block, axis, bit):
    count = lax.axis_size(axis)
    route = []
    for low in range(count):
        high = low | 1 << bit
        if high != low and high < count:
            route += [(low, high), (high, low)]
    return lax.ppermute(block, axis, route)


def rms_scale(values):
    totals = lax.psum(jnp.sum(values * values, axis=1), "tp")
    return lax.rsqrt(totals / (values.shape[1] * lax.axis_size("tp")) + 1e-06)


def expert_block(received, gate_block, down_block):
    hidden_units = down_block.shape[0]
    partial_sums = jnp.einsum(
        "smd,dh->smh", received, gate_block, preferred_element_type=jnp.float32
    )
    totals = lax.psum(partial_sums, "tp")
    hidden = (jax.nn.silu(totals[..., :hidden_units]) * totals[..., hidden_units:]).astype(
        jnp.bfloat16
    )
    return jnp.einsum("smh,hd->smd", hidden, down_block, preferred_element_type=jnp.float32).astype(
        jnp.bfloat16
    )


def body(section_rows, routes, route_weights, in_gain, gate_up, down, out_gain):
    inputs = section_rows[0]
    row_count, half_width = inputs.shape
    topk = routes.shape[2]
    ep_size = lax.axis_size("ep")
    share_count = min(16, ep_size // 4)
    expert_count = ep_size // share_count
    capacity = min(row_count, 3 * row_count * topk // (2 * expert_count))
    values = inputs.astype(jnp.float32)
    normed = (values * rms_scale(values)[:, None] * in_gain[0].astype(jnp.float32)[None, :]).astype(
        jnp.bfloat16
    )
    flat_ids = routes[0].reshape(-1)
    onehot = (flat_ids[:, None] == jnp.arange(expert_count, dtype=jnp.int32)[None, :]).astype(
        jnp.int32
    )
    slot_rank = jnp.sum((jnp.cumsum(onehot, axis=0) - 1) * onehot, axis=1)
    slot_ids = flat_ids * capacity + slot_rank
    source_rows = jnp.full((expert_count * capacity,), row_count, jnp.int32)
    source_rows = source_rows.at[slot_ids].set(
        jnp.arange(row_count * topk, dtype=jnp.int32) // topk
    )
    padded = jnp.concatenate([normed, jnp.zeros((1, half_width), jnp.bfloat16)], axis=0)
    per_expert = padded[source_rows].reshape(expert_count, capacity, half_width)
    outgoing = jnp.repeat(per_expert, share_count, axis=0)
    gate_block = gate_up[0, 0]
    down_block = down[0, 0]
    received = lax.all_to_all(outgoing, "ep", split_axis=0, concat_axis=0, tiled=True)
    returned = lax.all_to_all(
        expert_block(received, gate_block, down_block),
        "ep",
        split_axis=0,
        concat_axis=0,
        tiled=True,
    )
    grouped = returned.reshape(expert_count, share_count, capacity, half_width)
    summed = jnp.sum(grouped.astype(jnp.float32), axis=1).reshape(
        expert_count * capacity, half_width
    )
    picked = summed[slot_ids]
    weighted = picked * route_weights[0].reshape(-1)[:, None]
    mixture = jnp.sum(weighted.reshape(row_count, topk, half_width), axis=1)
    layer_out = (values + mixture).astype(jnp.bfloat16)
    residual = layer_out.astype(jnp.float32)
    closing = (
        residual * rms_scale(residual)[:, None] * out_gain[0].astype(jnp.float32)[None, :]
    ).astype(jnp.bfloat16)
    handed = swapped(closing, "section", 0)
    return (layer_out[None], handed[None])


def solution(mesh):
    return jax.shard_map(
        body,
        mesh=mesh,
        in_specs=(
            P("section", "ep", "tp"),
            P("section", "ep", None),
            P("section", "ep", None),
            P("section", "tp"),
            P("section", "ep", "tp", None),
            P("section", "ep", None, "tp"),
            P("section", "tp"),
        ),
        out_specs=(P("section", "ep", "tp"), P("section", "ep", "tp")),
        check_vma=False,
    )
```

profile of v0, /device:TPU:24, one launch (start us, length us, event | category | flops | bytes accessed | tf_op | source)
XLA Modules:
  0.0 295.1 jit_solution(13091304797155299446)
XLA Ops:
  7.2 0.9 eq.15
  8.1 0.7 broadcast_multiply_fusion
  9.2 0.6 scatter_custom_fusion
  9.8 0.8 convert_reduce_fusion.2
  10.6 0.9 fusion.10
  11.5 4.9 %psum.21 = f32[4]{0:T(128)S(1)} all-reduce(f32[4]{0:T(128)S(1)} %fusion.10), channel_id=1, replica_groups=mesh['section'=2,'ep'=128,'tp'=2] {'tp'}, use_global_device_ids=true, to_apply=%region_1.0 | all-reduce | flops 4 | bytes 32 | tf_op jit(solution)/shard_map/psum | solution.py:18
  16.4 0.8 fusion.12
  17.3 0.7 gather_fusion
  18.1 0.9 broadcast_in_dim.7
  19.0 103.9 %all_to_all.10 = bf16[128,3,3584]{2,1,0:T(4,128)(2,1)S(1)} all-to-all(bf16[128,3,3584]{2,1,0:T(4,128)(2,1)S(1)} %bitcast.44), channel_id=1, replica_groups=mesh['section'=2,'ep'=128,'tp'=2] {'ep'}, dimensions={0} | all-to-all | bytes 5505024 | tf_op jit(solution)/shard_map/all_to_all | solution.py:63
  122.9 1.6 fusion
  124.6 38.5 %all-reduce.3.cloned.1.call-done = f32[128,3,256]{2,0,1:T(8,128)} async-done(((f32[128,3,256]{2,0,1:T(8,128)}), f32[128,3,256]{2,0,1:T(8,128)}) %all-reduce.3.cloned.1.call-update) | async-done | bytes 393232 | tf_op jit(solution)/shard_map/psum | solution.py:27
  163.1 1.9 convolution_convert_fusion
  165.0 4.2 %copy.12 = bf16[128,3,3584]{2,1,0:T(4,128)(2,1)} copy(bf16[128,3,3584]{2,0,1:T(8,128)(2,1)S(1)} %convolution_convert_fusion) | data formatting | bytes 5505024 | tf_op jit(solution)/shard_map/convert_element_type | solution.py:31
  169.2 14.7 %all-to-all-start.1 = ((bf16[128,3,3584]{2,1,0:T(4,128)(2,1)}), bf16[128,3,3584]{2,1,0:T(4,128)(2,1)}, u32[]{:S(2)}, u32[]{:S(2)}) async-start(bf16[128,3,3584]{2,1,0:T(4,128)(2,1)} %copy.12), calls=%async_computation.1 | async-start | bytes 7340032 | tf_op jit(solution)/shard_map/all_to_all | solution.py:64
  184.0 86.4 %all-to-all-done.1 = bf16[128,3,3584]{2,1,0:T(4,128)(2,1)} async-done(((bf16[128,3,3584]{2,1,0:T(4,128)(2,1)}), bf16[128,3,3584]{2,1,0:T(4,128)(2,1)}, u32[]{:S(2)}, u32[]{:S(2)}) %all-to-all-start.1) | async-done | bytes 2752544 | tf_op jit(solution)/shard_map/all_to_all | solution.py:64
  270.4 3.6 %convert_reduce_fusion = f32[8,3,3584]{2,1,0:T(4,128)S(1)} fusion(bf16[128,3,3584]{2,1,0:T(4,128)(2,1)} %all-to-all-done.1), kind=kLoop, calls=%fused_computation.3 | loop fusion | flops 2666496 | bytes 3096576 | tf_op jit(solution)/shard_map/reduce_sum | solution.py:72
  274.2 0.6 gather_fusion.1
  274.9 0.2 multiply_reduce_fusion
  275.3 4.9 %psum.23 = f32[4]{0:T(128)S(1)} all-reduce(f32[4]{0:T(128)S(1)} %fusion.15), channel_id=1, replica_groups=mesh['section'=2,'ep'=128,'tp'=2] {'tp'}, use_global_device_ids=true, to_apply=%region_9.10 | all-reduce | flops 4 | bytes 32 | tf_op jit(solution)/shard_map/psum | solution.py:18
  280.4 4.6 %collective-permute-start = (bf16[4,3584]{1,0:T(4,128)(2,1)S(1)}, bf16[4,3584]{1,0:T(4,128)(2,1)S(1)}, u32[]{:S(2)}, u32[]{:S(2)}) collective-permute-start(bf16[4,3584]{1,0:T(4,128)(2,1)S(1)} %fusion.17), channel_id=1, source_target_pairs={{0,256},{256,0},{1,257},{257,1},{2,258},{258,2},{3,259},{259,3},{4... | collective-permute-start | bytes 86024 | tf_op jit(solution)/shard_map/ppermute | solution.py:14
  285.0 0.6 fusion.14
  285.6 2.0 collective-permute-done
  287.7 0.6 copy.20
  (30 shorter events, 1.1 us)
Async XLA Ops:
  7.2 115.8 %copy-start = (bf16[1,1,3584,256]{3,2,1,0:T(8,128)(2,1)S(1)}, bf16[1,1,3584,256]{3,2,1,0:T(8,128)(2,1)}, u32[]{:S(2)}) copy-start(bf16[1,1,3584,256]{3,2,1,0:T(8,128)(2,1)} %param.11) | copy-start | bytes 5505028
  7.2 155.9 %all-reduce.3.cloned.1.call-start = ((), (), s32[]{:S(2)}) async-start(), calls=%async_computation.2 | async-start | bytes 786432 | tf_op jit(solution)/shard_map/psum | solution.py:27
  122.9 40.1 %copy-start.1 = (bf16[1,1,128,3584]{3,2,1,0:T(8,128)(2,1)S(1)}, bf16[1,1,128,3584]{3,2,1,0:T(8,128)(2,1)}, u32[]{:S(2)}) copy-start(bf16[1,1,128,3584]{3,2,1,0:T(8,128)(2,1)} %param.12) | copy-start | bytes 2752516
  169.2 101.2 %all-to-all-start.1 = ((bf16[128,3,3584]{2,1,0:T(4,128)(2,1)}), bf16[128,3,3584]{2,1,0:T(4,128)(2,1)}, u32[]{:S(2)}, u32[]{:S(2)}) async-start(bf16[128,3,3584]{2,1,0:T(4,128)(2,1)} %copy.12), calls=%async_computation.1 | async-start | bytes 7340032 | tf_op jit(solution)/shard_map/all_to_all | solution.py:64
  183.9 91.0 %copy-start.4 = (f32[1,4,4]{2,1,0:T(4,128)S(1)}, f32[1,4,4]{2,1,0:T(4,128)}, u32[]{:S(2)}) copy-start(f32[1,4,4]{2,1,0:T(4,128)} %param.9) | copy-start | bytes 196
  183.9 91.2 %copy-start.2 = (bf16[1,4,3584]{2,1,0:T(4,128)(2,1)S(1)}, bf16[1,4,3584]{2,1,0:T(4,128)(2,1)}, u32[]{:S(2)}) copy-start(bf16[1,4,3584]{2,1,0:T(4,128)(2,1)} %param.7) | copy-start | bytes 86020
  184.0 91.3 %copy-start.3 = (bf16[1,3584]{1,0:T(2,128)(2,1)S(1)}, bf16[1,3584]{1,0:T(2,128)(2,1)}, u32[]{:S(2)}) copy-start(bf16[1,3584]{1,0:T(2,128)(2,1)} %param.13) | copy-start | bytes 21508
  280.4 7.3 %collective-permute-start = (bf16[4,3584]{1,0:T(4,128)(2,1)S(1)}, bf16[4,3584]{1,0:T(4,128)(2,1)S(1)}, u32[]{:S(2)}, u32[]{:S(2)}) collective-permute-start(bf16[4,3584]{1,0:T(4,128)(2,1)S(1)} %fusion.17), channel_id=1, source_target_pairs={{0,256},{256,0},{1,257},{257,1},{2,258},{258,2},{3,259},{259,3},{4... | collective-permute-start | bytes 86024 | tf_op jit(solution)/shard_map/ppermute | solution.py:14
Sparse Core Ops, SparseCore 0:
  124.7 38.3 all-reduce.2
where the time goes:
time: 296 us; the launch traced here: 295 us
  waiting for transfers between devices  127 us (43%)
  blocking collectives  114 us (39%)
  starting transfers between devices  19.4 us (7%)
  between operations  14.2 us (5%)
  local copies, waits for them, and re-layouts  9.02 us (3%)
  other arithmetic  8.27 us (3%)
  matrix products  3.53 us (1%)
    all_to_all x1, blocking collectives, body(): lax.all_to_all(outgoing, 'ep', split_axis=0, concat_axis=0, tiled=True)  104 us
    all_to_all x1, waiting for transfers between devices, body(): lax.all_to_all(expert_block(received, gate_block, down_block), 'ep', spli...  86.4 us
    psum x1, waiting for transfers between devices, expert_block(): totals = lax.psum(partial_sums, 'tp')  38.5 us
    all_to_all x1, starting transfers between devices, body(): lax.all_to_all(expert_block(received, gate_block, down_block), 'ep', spli...  14.7 us
    psum x2, blocking collectives, rms_scale(): totals = lax.psum(jnp.sum(values * values, axis=1), 'tp')  9.88 us
  transfers between devices with their start and end apart: 3, of which 3 were waited for; matrix products, arithmetic and copies ran while one was open for 0% of the time, Pallas kernels for 0%

commit v1 on v0

v1 whole, which is shorter than its diff:
```python
import jax
import jax.numpy as jnp
from jax import lax
from jax.sharding import PartitionSpec as P

EXTRA = 128


def crossed_groups(ep, span, first):
    along_y = [[y * span + i for y in range(ep // span)] for i in range(span)]
    along_z = [
        [y * span + z * 2 + c for z in range(span // 2)] for y in range(ep // span) for c in range(2)
    ]
    return [g for g in along_z if g[0] % 2 == first] + [g for g in along_y if g[0] % 2 != first]


def traded(block, groups):
    return lax.all_to_all(block, "ep", 0, 0, axis_index_groups=groups, tiled=True)


def spread(block, groups):
    count = len(groups[0])
    copies = jnp.broadcast_to(block[None], (count,) + block.shape)
    got = traded(copies, groups)
    return got.reshape((-1,) + block.shape[1:])


def collected(block, groups):
    count = len(groups[0])
    parts = block.reshape((count, block.shape[0] // count) + block.shape[1:])
    got = traded(parts, groups)
    return jnp.sum(got.astype(jnp.float32), axis=0)


def body(section_rows, routes, route_weights, in_gain, gate_up, down, out_gain):
    bf16, f32 = jnp.bfloat16, jnp.float32
    rows = section_rows[0]
    row_count, half_width = rows.shape
    ep = lax.axis_size("ep")
    width = half_width * lax.axis_size("tp")
    hidden_units = down.shape[2]
    span = 16
    expert_count = ep // span
    near, far = crossed_groups(ep, span, 0), crossed_groups(ep, span, 1)
    expert = lax.axis_index("ep") // span
    other_core = [(i, i ^ 1) for i in range(ep)]
    swap = [(0, 1), (1, 0)]

    gate_own, down_own = gate_up[0, 0], down[0, 0]
    gate_other = lax.ppermute(gate_own, "ep", other_core)
    down_other = lax.ppermute(down_own, "ep", other_core)
    gain_other = lax.ppermute(out_gain, "section", swap)[0].astype(f32)

    named = routes[0][:, :, None] == jnp.arange(expert_count, dtype=jnp.int32)[None, None, :]
    dense = jnp.sum(jnp.where(named, route_weights[0][:, :, None], 0.0), axis=1)
    high = lax.reduce_precision(dense, 8, 7)
    low = dense - high
    extra = jnp.concatenate(
        [high, low, jnp.zeros((row_count, EXTRA - 2 * expert_count), f32)], axis=1
    ).astype(bf16)
    payload = jnp.concatenate([rows, extra], axis=1)

    gathered = spread(spread(payload, near), far)
    values = gathered[:, :half_width].astype(f32)
    tail = gathered[:, half_width:].astype(f32)
    lane = jnp.arange(EXTRA, dtype=jnp.int32)[None, :]
    mine = (lane == expert) | (lane == expert + expert_count)
    weight = jnp.sum(jnp.where(mine, tail, 0.0), axis=1)
    squares = jnp.sum(values * values, axis=1)
    squares = squares + lax.ppermute(squares, "tp", swap)
    scale = lax.rsqrt(squares / width + 1e-06)
    scaled = (values * in_gain[0].astype(f32)[None, :]).astype(bf16)
    partial = jnp.concatenate(
        [
            jnp.dot(scaled, gate_own, preferred_element_type=f32),
            jnp.dot(scaled, gate_other, preferred_element_type=f32),
        ],
        axis=1,
    )
    totals = partial + lax.ppermute(partial.astype(bf16), "tp", swap).astype(f32)
    totals = totals * scale[:, None]
    hu = hidden_units
    hidden = [
        (jax.nn.silu(totals[:, at : at + hu]) * totals[:, at + hu : at + 2 * hu] * weight[:, None]).astype(bf16)
        for at in (0, 2 * hu)
    ]
    parts = (
        jnp.dot(hidden[0], down_own, preferred_element_type=f32)
        + jnp.dot(hidden[1], down_other, preferred_element_type=f32)
    ).astype(bf16)
    mixture = collected(collected(parts, far).astype(bf16), near)
    layer_out = (rows.astype(f32) + mixture).astype(bf16)
    mine_out = layer_out.astype(f32)
    my_squares = jnp.sum(mine_out * mine_out, axis=1)
    far_squares = lax.ppermute(my_squares, ("section", "tp"), [(0, 3), (3, 0), (1, 2), (2, 1)])
    theirs = lax.ppermute(layer_out, "section", swap).astype(f32)
    total = jnp.sum(theirs * theirs, axis=1) + far_squares
    handed = (theirs * lax.rsqrt(total / width + 1e-06)[:, None] * gain_other[None, :]).astype(bf16)
    return (layer_out[None], handed[None])


def solution(mesh):
    return jax.shard_map(
        body,
        mesh=mesh,
        in_specs=(
            P("section", "ep", "tp"),
            P("section", "ep", None),
            P("section", "ep", None),
            P("section", "tp"),
            P("section", "ep", "tp", None),
            P("section", "ep", None, "tp"),
            P("section", "tp"),
        ),
        out_specs=(P("section", "ep", "tp"), P("section", "ep", "tp")),
        check_vma=False,
    )
```

time: 296 us -> 133 us (0.45)
  the two profiles are of different devices: /device:TPU:24 before, /device:TPU:8 now
where the time goes in v1:
time: 133 us; the launch traced here: 132 us
  blocking collectives  50.2 us (38%)
  waiting for transfers between devices  34.1 us (26%)
  starting transfers between devices  33.3 us (25%)
  matrix products  7.3 us (5%)
  other arithmetic  3.63 us (3%)
  local copies, waits for them, and re-layouts  3.13 us (2%)
    all_to_all x2, blocking collectives, traded(): lax.all_to_all(block, 'ep', 0, 0, axis_index_groups=groups, tiled=True)  50.2 us
    all_to_all x2, waiting for transfers between devices, traded(): lax.all_to_all(block, 'ep', 0, 0, axis_index_groups=groups, tiled=True)  25 us
    all_to_all x2, starting transfers between devices, traded(): lax.all_to_all(block, 'ep', 0, 0, axis_index_groups=groups, tiled=True)  11.1 us
    ppermute x1, starting transfers between devices, body(): gain_other = lax.ppermute(out_gain, 'section', swap)[0].astype(f32)  4.64 us
    ppermute x1, starting transfers between devices, body(): theirs = lax.ppermute(layer_out, 'section', swap).astype(f32)  4.63 us
    ppermute x1, waiting for transfers between devices, body(): lax.ppermute(my_squares, ('section', 'tp'), [(0, 3), (3, 0), (1, 2), (2,...  3.7 us
    ppermute x1, starting transfers between devices, body(): lax.ppermute(partial.astype(bf16), 'tp', swap).astype(f32)  3.4 us
    ppermute x1, waiting for transfers between devices, body(): squares = squares + lax.ppermute(squares, 'tp', swap)  2.9 us
  transfers between devices with their start and end apart: 9, of which 5 were waited for; matrix products, arithmetic and copies ran while one was open for 5% of the time, Pallas kernels for 0%

profile of v1, /device:TPU:8, one launch (start us, length us, event | category | flops | bytes accessed | tf_op | source)
XLA Modules:
  0.0 132.5 jit_solution(9336619079188295808)
XLA Ops:
  0.6 0.8 select_reduce_fusion.1
  1.4 0.8 concatenate.9
  2.4 20.3 %all_to_all.20 = bf16[8,4,3712]{2,1,0:T(4,128)(2,1)S(1)} all-to-all(bf16[8,4,3712]{2,1,0:T(4,128)(2,1)S(1)} %broadcast_in_dim.58), channel_id=1, replica_groups={{0,4,8,12,16,20,24,28},{32,36,40,44,48,52,56,60},{64,68,72,76,80,84,88,..., dimensions={0} | all-to-all | bytes 475136 | tf_op jit(solution)/shard_map/all_to_all | solution.py:18
  22.7 1.4 %broadcast_in_dim.60 = bf16[8,32,3712]{2,1,0:T(8,128)(2,1)} broadcast(bf16[32,3712]{1,0:T(8,128)(2,1)S(1)} %broadcast_in_dim.59), dimensions={1,2} | broadcast | bytes 2138112 | tf_op jit(solution)/shard_map/broadcast_in_dim | solution.py:23
  24.2 7.7 %all-to-all-start.1 = ((bf16[8,32,3712]{2,1,0:T(8,128)(2,1)}), bf16[8,32,3712]{2,1,0:T(8,128)(2,1)S(1)}, u32[]{:S(2)}, u32[]{:S(2)}) async-start(bf16[8,32,3712]{2,1,0:T(8,128)(2,1)} %broadcast_in_dim.60), calls=%async_computation.1 | async-start | bytes 3801088 | tf_op jit(solution)/shard_map/all_to_all | solution.py:18
  31.8 1.9 %collective-permute-start = (bf16[3584,256]{1,0:T(8,128)(2,1)}, bf16[3584,256]{1,0:T(8,128)(2,1)}, u32[]{:S(2)}, u32[]{:S(2)}) collective-permute-start(bf16[3584,256]{1,0:T(8,128)(2,1)} %bitcast.30), channel_id=1, source_target_pairs={{0,2},{2,0},{4,6},{6,4},{8,10},{10,8},{12,14},{14,12},{16,18},{18,... | collective-permute-start | bytes 5505032 | tf_op jit(solution)/shard_map/ppermute | solution.py:50
  33.8 2.4 %collective-permute-start.3 = (bf16[128,3584]{1,0:T(8,128)(2,1)S(1)}, bf16[128,3584]{1,0:T(8,128)(2,1)}, u32[]{:S(2)}, u32[]{:S(2)}) collective-permute-start(bf16[128,3584]{1,0:T(8,128)(2,1)S(1)} %bitcast.26), channel_id=1, source_target_pairs={{0,2},{2,0},{4,6},{6,4},{8,10},{10,8},{12,14},{14,12},{16,18},{18,... | collective-permute-start | bytes 2752520 | tf_op jit(solution)/shard_map/ppermute | solution.py:51
  36.3 22.1 %all-to-all-done.1 = bf16[8,32,3712]{2,1,0:T(8,128)(2,1)S(1)} async-done(((bf16[8,32,3712]{2,1,0:T(8,128)(2,1)}), bf16[8,32,3712]{2,1,0:T(8,128)(2,1)S(1)}, u32[]{:S(2)}, u32[]{:S(2)}) %all-to-all-start.1) | async-done | bytes 1900576 | tf_op jit(solution)/shard_map/all_to_all | solution.py:18
  58.9 2.4 %fusion.5 = f32[256,256]{0,1:T(8,128)S(1)} fusion(f32[3584]{0:T(1024)S(1)} %convert_reduce_fusion.2, bf16[256,3712]{1,0:T(8,128)(2,1)S(1)} %bitcast.22, bf16[1,1,3584,256]{3,2,1,0:T(8,128)(2,1)} %param.11), kind=kOutput, calls=%fused_computation.7 | convolution fusion | flops 472514560 | bytes 3948544 | tf_op jit(solution)/shard_map/dot_general | solution.py:75
  61.3 2.4 %fusion.3 = f32[256,256]{0,1:T(8,128)S(1)} fusion(bf16[3584,256]{1,0:T(8,128)(2,1)} %collective-permute-done, f32[3584]{0:T(1024)S(1)} %convert_reduce_fusion.2, bf16[256,3712]{1,0:T(8,128)(2,1)S(1)} %bitcast.23), kind=kOutput, calls=%fused_computation.6 | convolution fusion | flops 472514560 | bytes 3948544 | tf_op jit(solution)/shard_map/dot_general | solution.py:76
  63.7 3.4 %collective-permute-start.1 = (bf16[256,512]{0,1:T(8,128)(2,1)S(1)}, bf16[256,512]{0,1:T(8,128)(2,1)S(1)}, u32[]{:S(2)}, u32[]{:S(2)}) collective-permute-start(bf16[256,512]{0,1:T(8,128)(2,1)S(1)} %fusion.7), channel_id=1, source_target_pairs={{0,1},{1,0},{2,3},{3,2},{4,5},{5,4},{6,7},{7,6},{8,9},{9,8},{10,11... | collective-permute-start | bytes 786440 | tf_op jit(solution)/shard_map/ppermute | solution.py:80
  67.1 2.4 %collective-permute-start.2 = (f32[256]{0:T(256)S(1)}, f32[256]{0:T(256)S(1)}, u32[]{:S(2)}, u32[]{:S(2)}) collective-permute-start(f32[256]{0:T(256)S(1)} %fusion.2), channel_id=1, source_target_pairs={{0,1},{1,0},{2,3},{3,2},{4,5},{5,4},{6,7},{7,6},{8,9},{9,8},{10,11... | collective-permute-start | bytes 3080 | tf_op jit(solution)/shard_map/ppermute | solution.py:70
  69.7 2.9 %collective-permute-done.2 = f32[256]{0:T(256)S(1)} collective-permute-done((f32[256]{0:T(256)S(1)}, f32[256]{0:T(256)S(1)}, u32[]{:S(2)}, u32[]{:S(2)}) %collective-permute-start.2) | collective-permute-done | bytes 1056 | tf_op jit(solution)/shard_map/ppermute | solution.py:70
  73.3 1.9 %fusion = bf16[256,3584]{1,0:T(8,128)(2,1)S(1)} fusion(f32[256,3584]{1,0:T(8,128)S(1)} %fusion.12, bf16[128,3584]{1,0:T(8,128)(2,1)} %collective-permute-done.3, f32[256,512]{0,1:T(8,128)S(1)} %add_multiply_fusion, f32[256]{0:T(256)S(1)} %select_reduce_fusion), kind=kOutput, calls=%fused_computation.1 | convolution fusion | flops 236945408 | bytes 6685696 | tf_op jit(solution)/shard_map/dot_general | solution.py:89
  75.2 29.9 %all_to_all.21 = bf16[8,32,3584]{2,1,0:T(8,128)(2,1)S(1)} all-to-all(bf16[8,32,3584]{2,1,0:T(8,128)(2,1)S(1)} %bitcast.25), channel_id=1, replica_groups={{2,6,10,14,18,22,26,30},{34,38,42,46,50,54,58,62},{66,70,74,78,82,86,90..., dimensions={0} | all-to-all | bytes 3670016 | tf_op jit(solution)/shard_map/all_to_all | solution.py:18
  105.4 0.7 reshape.34
  106.1 3.4 %all-to-all-start.3 = ((bf16[8,4,3584]{2,1,0:T(4,128)(2,1)}), bf16[8,4,3584]{2,1,0:T(4,128)(2,1)S(1)}, u32[]{:S(2)}, u32[]{:S(2)}) async-start(bf16[8,4,3584]{2,1,0:T(4,128)(2,1)} %reshape.34), calls=%async_computation.3 | async-start | bytes 458752 | tf_op jit(solution)/shard_map/all_to_all | solution.py:18
  109.5 4.6 %collective-permute-start.6 = (bf16[1,3584]{1,0:T(2,128)(2,1)S(1)}, bf16[1,3584]{1,0:T(2,128)(2,1)S(1)}, u32[]{:S(2)}, u32[]{:S(2)}) collective-permute-start(bf16[1,3584]{1,0:T(2,128)(2,1)S(1)} %copy-done.3), channel_id=1, source_target_pairs={{0,256},{256,0},{1,257},{257,1},{2,258},{258,2},{3,259},{259,3},{4... | collective-permute-start | bytes 21512 | tf_op jit(solution)/shard_map/ppermute | solution.py:52
  114.2 2.5 %collective-permute-done.6 = bf16[1,3584]{1,0:T(2,128)(2,1)S(1)} collective-permute-done((bf16[1,3584]{1,0:T(2,128)(2,1)S(1)}, bf16[1,3584]{1,0:T(2,128)(2,1)S(1)}, u32[]{:S(2)}, u32[]{:S(2)}) %collective-permute-start.6) | collective-permute-done | bytes 7200 | tf_op jit(solution)/shard_map/ppermute | solution.py:52
  116.7 2.9 %all-to-all-done.3 = bf16[8,4,3584]{2,1,0:T(4,128)(2,1)S(1)} async-done(((bf16[8,4,3584]{2,1,0:T(4,128)(2,1)}), bf16[8,4,3584]{2,1,0:T(4,128)(2,1)S(1)}, u32[]{:S(2)}, u32[]{:S(2)}) %all-to-all-start.3) | async-done | bytes 229408 | tf_op jit(solution)/shard_map/all_to_all | solution.py:18
  119.9 4.6 %collective-permute-start.4 = (bf16[4,3584]{1,0:T(4,128)(2,1)S(1)}, bf16[4,3584]{1,0:T(4,128)(2,1)S(1)}, u32[]{:S(2)}, u32[]{:S(2)}) collective-permute-start(bf16[4,3584]{1,0:T(4,128)(2,1)S(1)} %get-tuple-element.3), channel_id=1, source_target_pairs={{0,256},{256,0},{1,257},{257,1},{2,258},{258,2},{3,259},{259,3},{4... | collective-permute-start | bytes 86024 | tf_op jit(solution)/shard_map/ppermute | solution.py:96
  125.1 2.8 %collective-permute-start.5 = (f32[4]{0:T(128)S(1)}, f32[4]{0:T(128)S(1)}, u32[]{:S(2)}, u32[]{:S(2)}) collective-permute-start(f32[4]{0:T(128)S(1)} %get-tuple-element.2), channel_id=1, source_target_pairs={{0,257},{257,0},{1,256},{256,1},{2,259},{259,2},{3,258},{258,3},{4... | collective-permute-start | bytes 56 | tf_op jit(solution)/shard_map/ppermute | solution.py:95
  128.1 3.7 %collective-permute-done.5 = f32[4]{0:T(128)S(1)} collective-permute-done((f32[4]{0:T(128)S(1)}, f32[4]{0:T(128)S(1)}, u32[]{:S(2)}, u32[]{:S(2)}) %collective-permute-start.5) | collective-permute-done | bytes 48 | tf_op jit(solution)/shard_map/ppermute | solution.py:95
  131.8 0.7 fusion.23
  (31 shorter events, 3.0 us)
Async XLA Ops:
  24.2 9.6 %copy-start = (bf16[1,1,128,3584]{3,2,1,0:T(8,128)(2,1)S(1)}, bf16[1,1,128,3584]{3,2,1,0:T(8,128)(2,1)}, u32[]{:S(2)}) copy-start(bf16[1,1,128,3584]{3,2,1,0:T(8,128)(2,1)} %param.12) | copy-start | bytes 2752516
  24.2 12.1 %copy-start.2 = (bf16[1,3584]{1,0:T(2,128)(2,1)S(1)}, bf16[1,3584]{1,0:T(2,128)(2,1)}, u32[]{:S(2)}) copy-start(bf16[1,3584]{1,0:T(2,128)(2,1)} %param.10) | copy-start | bytes 21508
  24.2 34.3 %all-to-all-start.1 = ((bf16[8,32,3712]{2,1,0:T(8,128)(2,1)}), bf16[8,32,3712]{2,1,0:T(8,128)(2,1)S(1)}, u32[]{:S(2)}, u32[]{:S(2)}) async-start(bf16[8,32,3712]{2,1,0:T(8,128)(2,1)} %broadcast_in_dim.60), calls=%async_computation.1 | async-start | bytes 3801088 | tf_op jit(solution)/shard_map/all_to_all | solution.py:18
  31.8 29.4 %collective-permute-start = (bf16[3584,256]{1,0:T(8,128)(2,1)}, bf16[3584,256]{1,0:T(8,128)(2,1)}, u32[]{:S(2)}, u32[]{:S(2)}) collective-permute-start(bf16[3584,256]{1,0:T(8,128)(2,1)} %bitcast.30), channel_id=1, source_target_pairs={{0,2},{2,0},{4,6},{6,4},{8,10},{10,8},{12,14},{14,12},{16,18},{18,... | collective-permute-start | bytes 5505032 | tf_op jit(solution)/shard_map/ppermute | solution.py:50
  33.8 39.6 %collective-permute-start.3 = (bf16[128,3584]{1,0:T(8,128)(2,1)S(1)}, bf16[128,3584]{1,0:T(8,128)(2,1)}, u32[]{:S(2)}, u32[]{:S(2)}) collective-permute-start(bf16[128,3584]{1,0:T(8,128)(2,1)S(1)} %bitcast.26), channel_id=1, source_target_pairs={{0,2},{2,0},{4,6},{6,4},{8,10},{10,8},{12,14},{14,12},{16,18},{18,... | collective-permute-start | bytes 2752520 | tf_op jit(solution)/shard_map/ppermute | solution.py:51
  63.7 8.9 %collective-permute-start.1 = (bf16[256,512]{0,1:T(8,128)(2,1)S(1)}, bf16[256,512]{0,1:T(8,128)(2,1)S(1)}, u32[]{:S(2)}, u32[]{:S(2)}) collective-permute-start(bf16[256,512]{0,1:T(8,128)(2,1)S(1)} %fusion.7), channel_id=1, source_target_pairs={{0,1},{1,0},{2,3},{3,2},{4,5},{5,4},{6,7},{7,6},{8,9},{9,8},{10,11... | collective-permute-start | bytes 786440 | tf_op jit(solution)/shard_map/ppermute | solution.py:80
  67.1 5.5 %collective-permute-start.2 = (f32[256]{0:T(256)S(1)}, f32[256]{0:T(256)S(1)}, u32[]{:S(2)}, u32[]{:S(2)}) collective-permute-start(f32[256]{0:T(256)S(1)} %fusion.2), channel_id=1, source_target_pairs={{0,1},{1,0},{2,3},{3,2},{4,5},{5,4},{6,7},{7,6},{8,9},{9,8},{10,11... | collective-permute-start | bytes 3080 | tf_op jit(solution)/shard_map/ppermute | solution.py:70
  105.1 4.4 %copy-start.3 = (bf16[1,3584]{1,0:T(2,128)(2,1)S(1)}, bf16[1,3584]{1,0:T(2,128)(2,1)}, u32[]{:S(2)}) copy-start(bf16[1,3584]{1,0:T(2,128)(2,1)} %param.13) | copy-start | bytes 21508
  105.1 14.7 %copy-start.1 = (bf16[1,4,3584]{2,1,0:T(4,128)(2,1)S(1)}, bf16[1,4,3584]{2,1,0:T(4,128)(2,1)}, u32[]{:S(2)}) copy-start(bf16[1,4,3584]{2,1,0:T(4,128)(2,1)} %param.7) | copy-start | bytes 86020
  106.1 13.4 %all-to-all-start.3 = ((bf16[8,4,3584]{2,1,0:T(4,128)(2,1)}), bf16[8,4,3584]{2,1,0:T(4,128)(2,1)S(1)}, u32[]{:S(2)}, u32[]{:S(2)}) async-start(bf16[8,4,3584]{2,1,0:T(4,128)(2,1)} %reshape.34), calls=%async_computation.3 | async-start | bytes 458752 | tf_op jit(solution)/shard_map/all_to_all | solution.py:18
  109.5 7.1 %collective-permute-start.6 = (bf16[1,3584]{1,0:T(2,128)(2,1)S(1)}, bf16[1,3584]{1,0:T(2,128)(2,1)S(1)}, u32[]{:S(2)}, u32[]{:S(2)}) collective-permute-start(bf16[1,3584]{1,0:T(2,128)(2,1)S(1)} %copy-done.3), channel_id=1, source_target_pairs={{0,256},{256,0},{1,257},{257,1},{2,258},{258,2},{3,259},{259,3},{4... | collective-permute-start | bytes 21512 | tf_op jit(solution)/shard_map/ppermute | solution.py:52
  119.9 8.0 %collective-permute-start.4 = (bf16[4,3584]{1,0:T(4,128)(2,1)S(1)}, bf16[4,3584]{1,0:T(4,128)(2,1)S(1)}, u32[]{:S(2)}, u32[]{:S(2)}) collective-permute-start(bf16[4,3584]{1,0:T(4,128)(2,1)S(1)} %get-tuple-element.3), channel_id=1, source_target_pairs={{0,256},{256,0},{1,257},{257,1},{2,258},{258,2},{3,259},{259,3},{4... | collective-permute-start | bytes 86024 | tf_op jit(solution)/shard_map/ppermute | solution.py:96
  125.1 6.6 %collective-permute-start.5 = (f32[4]{0:T(128)S(1)}, f32[4]{0:T(128)S(1)}, u32[]{:S(2)}, u32[]{:S(2)}) collective-permute-start(f32[4]{0:T(128)S(1)} %get-tuple-element.2), channel_id=1, source_target_pairs={{0,257},{257,0},{1,256},{256,1},{2,259},{259,2},{3,258},{258,3},{4... | collective-permute-start | bytes 56 | tf_op jit(solution)/shard_map/ppermute | solution.py:95

commit v2 on v1

v2 whole, which is shorter than its diff:
```python
import functools

import jax
import jax.numpy as jnp
from jax import lax
from jax.experimental import pallas as pl
from jax.experimental.pallas import tpu as pltpu
from jax.sharding import PartitionSpec as P

BF16, F32 = jnp.bfloat16, jnp.float32
SPAN = 16
ALONG = 8
ROWS = 4
MOST = 3
EXPERTS = 8
EXTRA = 128
WIDE = ALONG * ROWS
TIGHT = ALONG * MOST
PARAMS = dict(compiler_params=pltpu.CompilerParams(vmem_limit_bytes=24 * 1024 * 1024))


def crossed_groups(ep, first):
    along_y = [[y * SPAN + i for y in range(ep // SPAN)] for i in range(SPAN)]
    along_z = [
        [y * SPAN + z * 2 + c for z in range(SPAN // 2)] for y in range(ep // SPAN) for c in range(2)
    ]
    return [g for g in along_z if g[0] % 2 == first] + [g for g in along_y if g[0] % 2 != first]


def traded(block, groups):
    return lax.all_to_all(block, "ep", 0, 0, axis_index_groups=groups, tiled=True)


def index(shape, axis):
    return lax.broadcasted_iota(jnp.int32, shape, axis).astype(F32)


def split(at, count):
    whole = jnp.floor((at + 0.5) * (1.0 / count))
    return whole, at - whole * count


def announce(info_ref, rows_ref, routes_ref, weights_ref, out_ref, back_ref):
    crossing = info_ref[0] == 0
    half_width = rows_ref.shape[1]
    lane = lax.broadcasted_iota(jnp.int32, (ROWS, EXTRA), 1)
    routes, weights = routes_ref[...], weights_ref[...]
    dense = jnp.zeros((ROWS, EXTRA), F32)
    later = jnp.zeros((ROWS, EXTRA), F32)
    for k in range(routes.shape[1]):
        dense += jnp.where(lane == routes[:, k : k + 1], weights[:, k : k + 1], 0.0)
        later += jnp.where(lane == routes[:, k : k + 1] + EXPERTS, weights[:, k : k + 1], 0.0)
    high = dense.astype(BF16).astype(F32)
    low = later - later.astype(BF16).astype(F32)
    extra = jnp.where(lane < EXPERTS, high, low)
    named = jnp.where(dense > 0.0, 1.0, 0.0)
    codes, before = [], jnp.zeros((1, EXTRA), F32)
    for r in range(ROWS):
        codes.append(jnp.where(named[r : r + 1] > 0.5, before, -1.0))
        before = before + named[r : r + 1]
    rows = rows_ref[...].astype(F32)
    target, slot = split(index((WIDE, 1), 0), ROWS)
    pick = jnp.where(index((WIDE, EXTRA), 1) == target, 1.0, 0.0)
    body = jnp.zeros((WIDE, half_width), F32)
    tail = jnp.zeros((WIDE, EXTRA), F32)
    for r in range(ROWS):
        code = jnp.sum(pick * codes[r], axis=1, keepdims=True)
        here = jnp.where(jnp.where(crossing, r * 1.0, code) == slot, 1.0, 0.0)
        body += here * rows[r : r + 1]
        tail += here * extra[r : r + 1]
    out_ref[:, :half_width] = body.astype(BF16)
    out_ref[:, half_width:] = tail.astype(BF16)
    table = jnp.concatenate(codes + [jnp.full((8 - ROWS, EXTRA), -1.0, F32)], axis=0)
    target, slot = split(index((EXTRA, WIDE), 1), ROWS)
    spread = jnp.where(index((EXTRA, WIDE), 0) == target, 1.0, 0.0).astype(BF16)
    found = jnp.dot(table.astype(BF16), spread, preferred_element_type=F32)
    found = jnp.where(crossing, index((8, WIDE), 0), found)
    back_ref[...] = jnp.where(found == slot[:8], 1.0, 0.0).astype(BF16)


def sort_rows(info_ref, rows_ref, out_ref, back_ref):
    crossing = info_ref[0] == 0
    half_width = rows_ref.shape[1] - EXTRA
    total = ALONG * TIGHT
    tail = rows_ref[:, half_width:].astype(F32)
    named = jnp.where((tail > 0.0) & (index((WIDE, EXTRA), 1) < EXPERTS - 0.5), 1.0, 0.0)
    one, two = index((WIDE, WIDE), 0), index((WIDE, WIDE), 1)
    ahead = jnp.where((split(one, ROWS)[0] == split(two, ROWS)[0]) & (two < one), 1.0, 0.0)
    rank = jnp.dot(ahead.astype(BF16), named.astype(BF16), preferred_element_type=F32)
    code = jnp.where(named > 0.5, rank, -1.0).astype(BF16)

    def matrix(found, at, to):
        source, slot = split(split(at, TIGHT)[1], MOST)
        block, row = split(to, ROWS)
        found = jnp.where(crossing, found, row)
        return jnp.where((block == source) & (found == slot), 1.0, 0.0).astype(BF16)

    target = split(index((total, EXTRA), 0), TIGHT)[0]
    pick = jnp.where(index((total, EXTRA), 1) == target, 1.0, 0.0).astype(BF16)
    found = lax.dot_general(pick, code, (((1,), (1,)), ((), ())), preferred_element_type=F32)
    forth = matrix(found, index((total, WIDE), 0), index((total, WIDE), 1))
    target = split(index((EXTRA, total), 1), TIGHT)[0]
    pick = jnp.where(index((EXTRA, total), 0) == target, 1.0, 0.0).astype(BF16)
    found = jnp.dot(code, pick, preferred_element_type=F32)
    back_ref[...] = matrix(found, index((WIDE, total), 1), index((WIDE, total), 0))
    rows = rows_ref[...]
    for t in range(ALONG):
        out_ref[t] = jnp.dot(
            forth[t * TIGHT : (t + 1) * TIGHT], rows, preferred_element_type=F32
        ).astype(BF16)


def gate(rows_ref, gain_ref, own_ref, other_ref, kept_ref, sent_ref, squares):
    step = pl.program_id(0)
    cols = own_ref.shape[1]

    @pl.when(step == 0)
    def _():
        kept_ref[...] = jnp.zeros_like(kept_ref)
        squares[...] = jnp.zeros_like(squares)

    values = rows_ref[...].astype(F32)
    squares[...] += jnp.sum(values * values, axis=1, keepdims=True)
    scaled = (values * gain_ref[...].astype(F32)).astype(BF16)
    kept_ref[:, :cols] += jnp.dot(scaled, own_ref[...], preferred_element_type=F32)
    kept_ref[:, cols : 2 * cols] += jnp.dot(scaled, other_ref[...], preferred_element_type=F32)

    @pl.when(step == pl.num_programs(0) - 1)
    def _():
        total = squares[...]
        high = total.astype(BF16).astype(F32)
        lane = lax.broadcasted_iota(jnp.int32, total.shape, 1)
        pieces = jnp.where(lane == 0, high, jnp.where(lane == 1, total - high, 0.0))
        kept_ref[:, 2 * cols :] = total
        sent_ref[:, : 2 * cols] = kept_ref[:, : 2 * cols].astype(BF16)
        sent_ref[:, 2 * cols :] = pieces.astype(BF16)


def expert(width, info_ref, tail_ref, kept_ref, got_ref, own_ref, other_ref, out_ref, hidden):
    units = own_ref.shape[0]

    @pl.when(pl.program_id(0) == 0)
    def _():
        which = info_ref[1]
        tail = tail_ref[...].astype(F32)
        lane = lax.broadcasted_iota(jnp.int32, tail.shape, 1)
        mine = (lane == which) | (lane == which + EXPERTS)
        weight = jnp.sum(jnp.where(mine, tail, 0.0), axis=1, keepdims=True)
        far = jnp.sum(got_ref[:, 4 * units :].astype(F32), axis=1, keepdims=True)
        squares = kept_ref[:, 4 * units : 4 * units + 1] + far
        scale = lax.rsqrt(squares * (1.0 / width) + 1e-06)
        for at in range(2):
            lo = 2 * units * at
            a = (kept_ref[:, lo : lo + units] + got_ref[:, lo : lo + units].astype(F32)) * scale
            lo += units
            b = (kept_ref[:, lo : lo + units] + got_ref[:, lo : lo + units].astype(F32)) * scale
            value = a / (1.0 + jnp.exp(-a)) * b * weight
            hidden[:, at * units : (at + 1) * units] = value.astype(BF16)

    out_ref[...] = (
        jnp.dot(hidden[:, :units], own_ref[...], preferred_element_type=F32)
        + jnp.dot(hidden[:, units:], other_ref[...], preferred_element_type=F32)
    ).astype(BF16)


def gather_parts(back_ref, parts_ref, out_ref):
    out_ref[...] = jnp.dot(back_ref[...], parts_ref[...], preferred_element_type=F32).astype(BF16)


def finish(back_ref, parts_ref, rows_ref, out_ref, squares_ref):
    mixture = jnp.dot(back_ref[...], parts_ref[...], preferred_element_type=F32)[:ROWS]
    layer = (rows_ref[...].astype(F32) + mixture).astype(BF16)
    out_ref[...] = layer
    values = layer.astype(F32)
    squares_ref[...] = jnp.broadcast_to(
        jnp.sum(values * values, axis=1, keepdims=True), squares_ref.shape
    )


def close(width, theirs_ref, far_ref, gain_ref, out_ref):
    values = theirs_ref[...].astype(F32)
    total = jnp.sum(values * values, axis=1, keepdims=True) + far_ref[:, :1]
    scale = lax.rsqrt(total * (1.0 / width) + 1e-06)
    out_ref[...] = (values * scale * gain_ref[...].astype(F32)).astype(BF16)


def local(kernel, outs, *args, smem=0):
    specs = [
        pl.BlockSpec(memory_space=pltpu.SMEM if at < smem else pltpu.VMEM) for at in range(len(args))
    ]
    out_specs = [pl.BlockSpec(memory_space=pltpu.VMEM) for _ in outs]
    return pl.pallas_call(kernel, out_shape=outs, in_specs=specs, out_specs=out_specs, **PARAMS)(*args)


def shape(*dims, dtype=BF16):
    return jax.ShapeDtypeStruct(dims, dtype)


def body(section_rows, routes, route_weights, in_gain, gate_up, down, out_gain):
    rows = section_rows[0]
    half_width = rows.shape[1]
    ep = lax.axis_size("ep")
    width = half_width * lax.axis_size("tp")
    units = down.shape[2]
    cols = gate_up.shape[3]
    near, far = crossed_groups(ep, 0), crossed_groups(ep, 1)
    place = lax.axis_index("ep")
    info = jnp.stack([place % 2, place // SPAN]).astype(jnp.int32)
    other_core = [(i, i ^ 1) for i in range(ep)]
    swap = [(0, 1), (1, 0)]
    full = half_width + EXTRA
    total = ALONG * TIGHT

    gate_own, down_own = gate_up[0, 0], down[0, 0]
    gate_other = lax.ppermute(gate_own, "ep", other_core)
    down_other = lax.ppermute(down_own, "ep", other_core)
    gain_other = lax.ppermute(out_gain, "section", swap)

    leaving, home_back = local(
        announce, [shape(WIDE, full), shape(8, WIDE)], info, rows, routes[0], route_weights[0], smem=1
    )
    met = traded(leaving.reshape(ALONG, ROWS, full), near).reshape(WIDE, full)
    sorted_rows, far_back = local(
        sort_rows, [shape(ALONG, TIGHT, full), shape(WIDE, total)], info, met, smem=1
    )
    gathered = traded(sorted_rows, far).reshape(total, full)
    gathered, gain_other = lax.optimization_barrier((gathered, gain_other))

    steps = 4
    deep = half_width // steps
    kept, sent = pl.pallas_call(
        gate,
        grid=(steps,),
        out_shape=[shape(total, 2 * cols + EXTRA, dtype=F32), shape(total, 2 * cols + EXTRA)],
        in_specs=[
            pl.BlockSpec((total, deep), lambda k: (0, k)),
            pl.BlockSpec((1, deep), lambda k: (0, k)),
            pl.BlockSpec((deep, cols), lambda k: (k, 0)),
            pl.BlockSpec((deep, cols), lambda k: (k, 0)),
        ],
        out_specs=[pl.BlockSpec((total, 2 * cols + EXTRA), lambda k: (0, 0))] * 2,
        scratch_shapes=[pltpu.VMEM((total, EXTRA), F32)],
        **PARAMS,
    )(gathered, in_gain, gate_own, gate_other)
    got = lax.ppermute(sent, "tp", swap)
    parts = pl.pallas_call(
        functools.partial(expert, width),
        grid=(steps,),
        out_shape=shape(total, half_width),
        in_specs=[
            pl.BlockSpec(memory_space=pltpu.SMEM),
            pl.BlockSpec((total, EXTRA), lambda k: (0, half_width // EXTRA)),
            pl.BlockSpec((total, 2 * cols + EXTRA), lambda k: (0, 0)),
            pl.BlockSpec((total, 2 * cols + EXTRA), lambda k: (0, 0)),
            pl.BlockSpec((units, deep), lambda k: (0, k)),
            pl.BlockSpec((units, deep), lambda k: (0, k)),
        ],
        out_specs=pl.BlockSpec((total, deep), lambda k: (0, k)),
        scratch_shapes=[pltpu.VMEM((total, 2 * units), BF16)],
        **PARAMS,
    )(info, gathered, kept, got, down_own, down_other)
    returned = traded(parts.reshape(ALONG, TIGHT, half_width), far).reshape(total, half_width)
    (summed,) = local(gather_parts, [shape(WIDE, half_width)], far_back, returned)
    home = traded(summed.reshape(ALONG, ROWS, half_width), near).reshape(WIDE, half_width)
    layer_out, squares = local(
        finish, [shape(ROWS, half_width), shape(ROWS, EXTRA, dtype=F32)], home_back, home, rows
    )
    theirs = lax.ppermute(layer_out, "section", swap)
    far_squares = lax.ppermute(squares, ("section", "tp"), [(0, 3), (3, 0), (1, 2), (2, 1)])
    (handed,) = local(
        functools.partial(close, width), [shape(ROWS, half_width)], theirs, far_squares, gain_other
    )
    return (layer_out[None], handed[None])


def solution(mesh):
    return jax.shard_map(
        body,
        mesh=mesh,
        in_specs=(
            P("section", "ep", "tp"),
            P("section", "ep", None),
            P("section", "ep", None),
            P("section", "tp"),
            P("section", "ep", "tp", None),
            P("section", "ep", None, "tp"),
            P("section", "tp"),
        ),
        out_specs=(P("section", "ep", "tp"), P("section", "ep", "tp")),
        check_vma=False,
    )
```

time: 133 us -> 123 us (0.925)
  waiting for transfers between devices: 34.1 us -> 20.5 us
  Pallas kernels: 0 us -> 11.2 us
  blocking collectives: 50.2 us -> 57.7 us
  matrix products: 7.3 us -> 0 us
  starting transfers between devices: 33.3 us -> 28.3 us
  other arithmetic: 3.63 us -> 0.08 us
    all_to_all x2 -> x1, waiting for transfers between devices: 25 us -> 10 us  [traded(): lax.all_to_all(block, 'ep', 0, 0, axis_index_groups=groups, tiled=True)]
    pallas_call x0 -> x7, Pallas kernels: none -> 11.2 us  [the longest x5 4.22 us: local(): pl.pallas_call(kernel, out_shape=outs, in_specs=specs, out_specs=out_spec...]
    all_to_all x2 -> x3, blocking collectives: 50.2 us -> 57.7 us  [traded(): lax.all_to_all(block, 'ep', 0, 0, axis_index_groups=groups, tiled=True)]
    dot_general x4 -> x0, matrix products: 7.3 us -> none  [the longest x1 2.38 us: body(): jnp.dot(scaled, gate_own, preferred_element_type=f32)]
    all_to_all x2 -> x1, starting transfers between devices: 11.1 us -> 7.68 us  [traded(): lax.all_to_all(block, 'ep', 0, 0, axis_index_groups=groups, tiled=True)]
    unnamed x8 -> x18, local copies, waits for them, and re-layouts: 0.01 us -> 3.23 us
    reduce_sum x7 -> x0, other arithmetic: 2.1 us -> none  [the longest x1 0.79 us: body(): dense = jnp.sum(jnp.where(named, route_weights[0][:, :, None], 0.0), axis=1)]
    ppermute x5 -> x4, starting transfers between devices: 17.9 us -> 16.3 us  [the longest x1 4.93 us: body(): gain_other = lax.ppermute(out_gain, 'section', swap)]
  transfers between devices with their start and end apart: 9 -> 7, of which waited for: 5 -> 4; matrix products, arithmetic and copies ran while one was open for 5% -> 0% of each run, Pallas kernels for 0% -> 3%
where the time goes in v2:
time: 123 us; the launch traced here: 122 us
  blocking collectives  57.7 us (47%)
  starting transfers between devices  28.3 us (23%)
  waiting for transfers between devices  20.5 us (17%)
  Pallas kernels  11.2 us (9%)
  local copies, waits for them, and re-layouts  3.48 us (3%)
    all_to_all x3, blocking collectives, traded(): lax.all_to_all(block, 'ep', 0, 0, axis_index_groups=groups, tiled=True)  57.7 us
    all_to_all x1, waiting for transfers between devices, traded(): lax.all_to_all(block, 'ep', 0, 0, axis_index_groups=groups, tiled=True)  10 us
    all_to_all x1, starting transfers between devices, traded(): lax.all_to_all(block, 'ep', 0, 0, axis_index_groups=groups, tiled=True)  7.68 us
    ppermute x1, starting transfers between devices, body(): gain_other = lax.ppermute(out_gain, 'section', swap)  4.93 us
    ppermute x1, starting transfers between devices, body(): theirs = lax.ppermute(layer_out, 'section', swap)  4.92 us
    ppermute x1, waiting for transfers between devices, body(): got = lax.ppermute(sent, 'tp', swap)  4.67 us
    pallas_call x5, Pallas kernels, local(): pl.pallas_call(kernel, out_shape=outs, in_specs=specs, out_specs=out_spec...  4.22 us
    ppermute x1, waiting for transfers between devices, body(): lax.ppermute(squares, ('section', 'tp'), [(0, 3), (3, 0), (1, 2), (2, 1)])  3.62 us
  transfers between devices with their start and end apart: 7, of which 4 were waited for; matrix products, arithmetic and copies ran while one was open for 0% of the time, Pallas kernels for 3%

profile of v2, /device:TPU:8, one launch (start us, length us, event | category | flops | bytes accessed | tf_op | source)
XLA Modules:
  0.0 122.1 jit_solution(8999566016877587564)
XLA Ops:
  0.7 0.7 copy-done.3
  1.5 0.7 copy-done.6
  2.2 0.7 copy-done.7
  2.8 0.9 shard_map.86
  3.8 20.3 %all_to_all.20 = bf16[8,4,3712]{2,1,0:T(4,128)(2,1)S(1)} all-to-all(bf16[8,4,3712]{2,1,0:T(4,128)(2,1)S(1)} %reshape.25), channel_id=1, replica_groups={{0,4,8,12,16,20,24,28},{32,36,40,44,48,52,56,60},{64,68,72,76,80,84,88,..., dimensions={0} | all-to-all | bytes 475136 | tf_op jit(solution)/shard_map/all_to_all | solution.py:31
  24.2 1.4 %shard_map.87 = (bf16[8,24,3712]{2,1,0:T(8,128)(2,1)S(1)}, bf16[32,192]{1,0:T(8,128)(2,1)S(1)}) custom-call(s32[2]{0:T(128)S(1)} %pad_add_fusion.info_ref, bf16[32,3712]{1,0:T(8,128)(2,1)S(1)} %reshape.26.rows_ref), custom_call_target="tpu_custom_call" | custom-call | tf_op jit(solution)/shard_map/pallas_call | solution.py:192
  25.6 1.1 copy-done.1
  26.7 7.7 %all-to-all-start.1 = ((bf16[8,24,3712]{2,1,0:T(8,128)(2,1)}), bf16[8,24,3712]{2,1,0:T(8,128)(2,1)S(1)}, u32[]{:S(2)}, u32[]{:S(2)}) async-start(bf16[8,24,3712]{2,1,0:T(8,128)(2,1)} %copy-done.1), calls=%async_computation.1 | async-start | bytes 2850816 | tf_op jit(solution)/shard_map/all_to_all | solution.py:31
  34.4 1.9 %collective-permute-start.1 = (bf16[3584,256]{1,0:T(8,128)(2,1)S(1)}, bf16[3584,256]{1,0:T(8,128)(2,1)}, u32[]{:S(2)}, u32[]{:S(2)}) collective-permute-start(bf16[3584,256]{1,0:T(8,128)(2,1)S(1)} %bitcast.16), channel_id=1, source_target_pairs={{0,2},{2,0},{4,6},{6,4},{8,10},{10,8},{12,14},{14,12},{16,18},{18,... | collective-permute-start | bytes 5505032 | tf_op jit(solution)/shard_map/ppermute | solution.py:215
  36.3 2.4 %collective-permute-start.3 = (bf16[128,3584]{1,0:T(8,128)(2,1)}, bf16[128,3584]{1,0:T(8,128)(2,1)}, u32[]{:S(2)}, u32[]{:S(2)}) collective-permute-start(bf16[128,3584]{1,0:T(8,128)(2,1)} %bitcast.18), channel_id=1, source_target_pairs={{0,2},{2,0},{4,6},{6,4},{8,10},{10,8},{12,14},{14,12},{16,18},{18,... | collective-permute-start | bytes 2752520 | tf_op jit(solution)/shard_map/ppermute | solution.py:216
  38.7 4.9 %collective-permute-start = (bf16[1,3584]{1,0:T(2,128)(2,1)S(1)}, bf16[1,3584]{1,0:T(2,128)(2,1)S(1)}, u32[]{:S(2)}, u32[]{:S(2)}) collective-permute-start(bf16[1,3584]{1,0:T(2,128)(2,1)S(1)} %copy-done.8), channel_id=1, source_target_pairs={{0,256},{256,0},{1,257},{257,1},{2,258},{258,2},{3,259},{259,3},{4... | collective-permute-start | bytes 21512 | tf_op jit(solution)/shard_map/ppermute | solution.py:217
  43.7 2.2 %collective-permute-done.gain_ref = bf16[1,3584]{1,0:T(2,128)(2,1)S(1)} collective-permute-done((bf16[1,3584]{1,0:T(2,128)(2,1)S(1)}, bf16[1,3584]{1,0:T(2,128)(2,1)S(1)}, u32[]{:S(2)}, u32[]{:S(2)}) %collective-permute-start) | collective-permute-done | bytes 7200 | tf_op jit(solution)/shard_map/ppermute | solution.py:217
  45.9 10.0 %all-to-all-done.1 = bf16[8,24,3712]{2,1,0:T(8,128)(2,1)S(1)} async-done(((bf16[8,24,3712]{2,1,0:T(8,128)(2,1)}), bf16[8,24,3712]{2,1,0:T(8,128)(2,1)S(1)}, u32[]{:S(2)}, u32[]{:S(2)}) %all-to-all-start.1) | async-done | bytes 1425440 | tf_op jit(solution)/shard_map/all_to_all | solution.py:31
  55.9 3.6 %shard_map.88 = (f32[192,640]{1,0:T(8,128)S(1)}, bf16[192,640]{1,0:T(8,128)(2,1)S(1)}) custom-call(bf16[192,3712]{1,0:T(8,128)(2,1)S(1)} %bitcast.12, bf16[1,3584]{1,0:T(2,128)(2,1)S(1)} %copy-done.5, bf16[3584,256]{1,0:T(8,128)(2,1)S(1)} %bitcast.17, bf16[3584,256]{1,0:T(8,128)(2,1)} %collective-permute-done.1.other_ref), custom_call_target="tpu_custom_call" | custom-call | tf_op jit(solution)/shard_map/pallas_call | solution.py:231
  59.5 3.4 %collective-permute-start.2 = (bf16[192,640]{1,0:T(8,128)(2,1)S(1)}, bf16[192,640]{1,0:T(8,128)(2,1)S(1)}, u32[]{:S(2)}, u32[]{:S(2)}) collective-permute-start(bf16[192,640]{1,0:T(8,128)(2,1)S(1)} %get-tuple-element.18), channel_id=1, source_target_pairs={{0,1},{1,0},{2,3},{3,2},{4,5},{5,4},{6,7},{7,6},{8,9},{9,8},{10,11... | collective-permute-start | bytes 737288 | tf_op jit(solution)/shard_map/ppermute | solution.py:245
  62.9 4.7 %collective-permute-done.2.got_ref = bf16[192,640]{1,0:T(8,128)(2,1)S(1)} collective-permute-done((bf16[192,640]{1,0:T(8,128)(2,1)S(1)}, bf16[192,640]{1,0:T(8,128)(2,1)S(1)}, u32[]{:S(2)}, u32[]{:S(2)}) %collective-permute-start.2) | collective-permute-done | bytes 245792 | tf_op jit(solution)/shard_map/ppermute | solution.py:245
  67.6 3.4 %shard_map.89 = bf16[192,3584]{1,0:T(8,128)(2,1)S(1)} custom-call(s32[2]{0:T(128)S(1)} %pad_add_fusion.info_ref, bf16[192,3712]{1,0:T(8,128)(2,1)S(1)} %bitcast.13, f32[192,640]{1,0:T(8,128)S(1)} %get-tuple-element.17.kept_ref, bf16[192,640]{1,0:T(8,128)(2,1)S(1)} %collective-permute-done.2.got_ref, bf16[128,3584]{1,0:T(8,128)(2,1)S(1)} %bitcast.19, ...), custom_call_target="tpu_custom_call" | custom-call | tf_op jit(solution)/shard_map/pallas_call | solution.py:246
  71.0 24.9 %all_to_all.21 = bf16[8,24,3584]{2,1,0:T(8,128)(2,1)S(1)} all-to-all(bf16[8,24,3584]{2,1,0:T(8,128)(2,1)S(1)} %bitcast.14), channel_id=1, replica_groups={{2,6,10,14,18,22,26,30},{34,38,42,46,50,54,58,62},{66,70,74,78,82,86,90..., dimensions={0} | all-to-all | bytes 2752512 | tf_op jit(solution)/shard_map/all_to_all | solution.py:31
  96.3 12.5 %all_to_all.22 = bf16[8,4,3584]{2,1,0:T(4,128)(2,1)S(1)} all-to-all(bf16[8,4,3584]{2,1,0:T(4,128)(2,1)S(1)} %reshape.30), channel_id=1, replica_groups={{0,4,8,12,16,20,24,28},{32,36,40,44,48,52,56,60},{64,68,72,76,80,84,88,..., dimensions={0} | all-to-all | bytes 458752 | tf_op jit(solution)/shard_map/all_to_all | solution.py:31
  108.9 0.8 shard_map.91
  109.6 4.9 %collective-permute-start.4 = (bf16[4,3584]{1,0:T(4,128)(2,1)}, bf16[4,3584]{1,0:T(4,128)(2,1)S(1)}, u32[]{:S(2)}, u32[]{:S(2)}) collective-permute-start(bf16[4,3584]{1,0:T(4,128)(2,1)} %get-tuple-element.19), channel_id=1, source_target_pairs={{0,256},{256,0},{1,257},{257,1},{2,258},{258,2},{3,259},{259,3},{4... | collective-permute-start | bytes 86024 | tf_op jit(solution)/shard_map/ppermute | solution.py:268
  114.6 3.1 %collective-permute-start.5 = (f32[4,128]{1,0:T(4,128)S(1)}, f32[4,128]{1,0:T(4,128)S(1)}, u32[]{:S(2)}, u32[]{:S(2)}) collective-permute-start(f32[4,128]{1,0:T(4,128)S(1)} %get-tuple-element.20), channel_id=1, source_target_pairs={{0,257},{257,0},{1,256},{256,1},{2,259},{259,2},{3,258},{258,3},{4... | collective-permute-start | bytes 6152 | tf_op jit(solution)/shard_map/ppermute | solution.py:269
  117.6 3.6 %collective-permute-done.5.far_ref = f32[4,128]{1,0:T(4,128)S(1)} collective-permute-done((f32[4,128]{1,0:T(4,128)S(1)}, f32[4,128]{1,0:T(4,128)S(1)}, u32[]{:S(2)}, u32[]{:S(2)}) %collective-permute-start.5) | collective-permute-done | bytes 2080 | tf_op jit(solution)/shard_map/ppermute | solution.py:269
  121.3 0.8 shard_map.92
  (23 shorter events, 0.7 us)
Async XLA Ops:
  0.7 0.7 copy-start.3
  1.5 0.7 copy-start.6
  2.2 0.7 copy-start.7
  25.6 1.1 copy-start.1
  26.7 7.7 %copy-start = (bf16[1,1,3584,256]{3,2,1,0:T(8,128)(2,1)S(1)}, bf16[1,1,3584,256]{3,2,1,0:T(8,128)(2,1)}, u32[]{:S(2)}) copy-start(bf16[1,1,3584,256]{3,2,1,0:T(8,128)(2,1)} %param.11) | copy-start | bytes 5505028
  26.7 12.0 %copy-start.8 = (bf16[1,3584]{1,0:T(2,128)(2,1)S(1)}, bf16[1,3584]{1,0:T(2,128)(2,1)}, u32[]{:S(2)}) copy-start(bf16[1,3584]{1,0:T(2,128)(2,1)} %param.13) | copy-start | bytes 21508
  26.7 29.2 %copy-start.5 = (bf16[1,3584]{1,0:T(2,128)(2,1)S(1)}, bf16[1,3584]{1,0:T(2,128)(2,1)}, u32[]{:S(2)}) copy-start(bf16[1,3584]{1,0:T(2,128)(2,1)} %gain_ref.1) | copy-start | bytes 21508
  26.7 29.2 %all-to-all-start.1 = ((bf16[8,24,3712]{2,1,0:T(8,128)(2,1)}), bf16[8,24,3712]{2,1,0:T(8,128)(2,1)S(1)}, u32[]{:S(2)}, u32[]{:S(2)}) async-start(bf16[8,24,3712]{2,1,0:T(8,128)(2,1)} %copy-done.1), calls=%async_computation.1 | async-start | bytes 2850816 | tf_op jit(solution)/shard_map/all_to_all | solution.py:31
  34.4 21.5 %collective-permute-start.1 = (bf16[3584,256]{1,0:T(8,128)(2,1)S(1)}, bf16[3584,256]{1,0:T(8,128)(2,1)}, u32[]{:S(2)}, u32[]{:S(2)}) collective-permute-start(bf16[3584,256]{1,0:T(8,128)(2,1)S(1)} %bitcast.16), channel_id=1, source_target_pairs={{0,2},{2,0},{4,6},{6,4},{8,10},{10,8},{12,14},{14,12},{16,18},{18,... | collective-permute-start | bytes 5505032 | tf_op jit(solution)/shard_map/ppermute | solution.py:215
  36.3 26.6 %collective-permute-start.3 = (bf16[128,3584]{1,0:T(8,128)(2,1)}, bf16[128,3584]{1,0:T(8,128)(2,1)}, u32[]{:S(2)}, u32[]{:S(2)}) collective-permute-start(bf16[128,3584]{1,0:T(8,128)(2,1)} %bitcast.18), channel_id=1, source_target_pairs={{0,2},{2,0},{4,6},{6,4},{8,10},{10,8},{12,14},{14,12},{16,18},{18,... | collective-permute-start | bytes 2752520 | tf_op jit(solution)/shard_map/ppermute | solution.py:216
  38.7 7.1 %collective-permute-start = (bf16[1,3584]{1,0:T(2,128)(2,1)S(1)}, bf16[1,3584]{1,0:T(2,128)(2,1)S(1)}, u32[]{:S(2)}, u32[]{:S(2)}) collective-permute-start(bf16[1,3584]{1,0:T(2,128)(2,1)S(1)} %copy-done.8), channel_id=1, source_target_pairs={{0,256},{256,0},{1,257},{257,1},{2,258},{258,2},{3,259},{259,3},{4... | collective-permute-start | bytes 21512 | tf_op jit(solution)/shard_map/ppermute | solution.py:217
  55.9 11.7 %copy-start.2 = (bf16[1,1,128,3584]{3,2,1,0:T(8,128)(2,1)S(1)}, bf16[1,1,128,3584]{3,2,1,0:T(8,128)(2,1)}, u32[]{:S(2)}) copy-start(bf16[1,1,128,3584]{3,2,1,0:T(8,128)(2,1)} %param.12) | copy-start | bytes 2752516
  59.5 8.1 %collective-permute-start.2 = (bf16[192,640]{1,0:T(8,128)(2,1)S(1)}, bf16[192,640]{1,0:T(8,128)(2,1)S(1)}, u32[]{:S(2)}, u32[]{:S(2)}) collective-permute-start(bf16[192,640]{1,0:T(8,128)(2,1)S(1)} %get-tuple-element.18), channel_id=1, source_target_pairs={{0,1},{1,0},{2,3},{3,2},{4,5},{5,4},{6,7},{7,6},{8,9},{9,8},{10,11... | collective-permute-start | bytes 737288 | tf_op jit(solution)/shard_map/ppermute | solution.py:245
  95.8 13.0 %copy-start.4 = (bf16[1,4,3584]{2,1,0:T(4,128)(2,1)S(1)}, bf16[1,4,3584]{2,1,0:T(4,128)(2,1)}, u32[]{:S(2)}) copy-start(bf16[1,4,3584]{2,1,0:T(4,128)(2,1)} %param.7) | copy-start | bytes 86020
  109.6 11.6 %collective-permute-start.4 = (bf16[4,3584]{1,0:T(4,128)(2,1)}, bf16[4,3584]{1,0:T(4,128)(2,1)S(1)}, u32[]{:S(2)}, u32[]{:S(2)}) collective-permute-start(bf16[4,3584]{1,0:T(4,128)(2,1)} %get-tuple-element.19), channel_id=1, source_target_pairs={{0,256},{256,0},{1,257},{257,1},{2,258},{258,2},{3,259},{259,3},{4... | collective-permute-start | bytes 86024 | tf_op jit(solution)/shard_map/ppermute | solution.py:268
  114.6 6.7 %collective-permute-start.5 = (f32[4,128]{1,0:T(4,128)S(1)}, f32[4,128]{1,0:T(4,128)S(1)}, u32[]{:S(2)}, u32[]{:S(2)}) collective-permute-start(f32[4,128]{1,0:T(4,128)S(1)} %get-tuple-element.20), channel_id=1, source_target_pairs={{0,257},{257,0},{1,256},{256,1},{2,259},{259,2},{3,258},{258,3},{4... | collective-permute-start | bytes 6152 | tf_op jit(solution)/shard_map/ppermute | solution.py:269

commit v3 on v2

v3 whole, which is shorter than its diff:
```python
import functools

import jax
import jax.numpy as jnp
import numpy as np
from jax import lax
from jax.experimental import pallas as pl
from jax.experimental.pallas import tpu as pltpu
from jax.sharding import PartitionSpec as P

BF16, F32 = jnp.bfloat16, jnp.float32
SPAN = 16
ALONG = 8
ROWS = 4
MOST = 3
EXPERTS = 8
EXTRA = 128
WIDE = ALONG * ROWS
TIGHT = ALONG * MOST
MIB = 1024 * 1024


def crossed_groups(ep, first):
    along_y = [[y * SPAN + i for y in range(ep // SPAN)] for i in range(SPAN)]
    along_z = [
        [y * SPAN + z * 2 + c for z in range(SPAN // 2)] for y in range(ep // SPAN) for c in range(2)
    ]
    return [g for g in along_z if g[0] % 2 == first] + [g for g in along_y if g[0] % 2 != first]


def traded(block, groups):
    return lax.all_to_all(block, "ep", 0, 0, axis_index_groups=groups, tiled=True)


def index(shape, axis):
    return lax.broadcasted_iota(jnp.int32, shape, axis).astype(F32)


def split(at, count):
    whole = jnp.floor((at + 0.5) * (1.0 / count))
    return whole, at - whole * count


def announce(info_ref, rows_ref, dense_ref, out_ref, back_ref):
    crossing = info_ref[0] == 0
    half_width = rows_ref.shape[1]
    lane = index((ROWS, EXTRA), 1)
    dense = dense_ref[...]
    high = dense.astype(BF16).astype(F32)
    extra = jnp.where(lane < EXPERTS, high, dense - high)
    named = jnp.where((dense > 0.0) & (lane < EXPERTS), 1.0, 0.0)
    codes, before = [], jnp.zeros((1, EXTRA), F32)
    for r in range(ROWS):
        codes.append(jnp.where(named[r : r + 1] > 0.5, before, -1.0))
        before = before + named[r : r + 1]
    rows = rows_ref[...].astype(F32)
    target, slot = split(index((WIDE, 1), 0), ROWS)
    pick = jnp.where(index((WIDE, EXTRA), 1) == target, 1.0, 0.0)
    body = jnp.zeros((WIDE, half_width), F32)
    tail = jnp.zeros((WIDE, EXTRA), F32)
    for r in range(ROWS):
        code = jnp.sum(pick * codes[r], axis=1, keepdims=True)
        here = jnp.where(jnp.where(crossing, r * 1.0, code) == slot, 1.0, 0.0)
        body += here * rows[r : r + 1]
        tail += here * extra[r : r + 1]
    out_ref[:, :half_width] = body.astype(BF16)
    out_ref[:, half_width:] = tail.astype(BF16)
    table = jnp.concatenate(codes + [jnp.full((8 - ROWS, EXTRA), -1.0, F32)], axis=0)
    target, slot = split(index((EXTRA, WIDE), 1), ROWS)
    spread = jnp.where(index((EXTRA, WIDE), 0) == target, 1.0, 0.0).astype(BF16)
    found = jnp.dot(table.astype(BF16), spread, preferred_element_type=F32)
    found = jnp.where(crossing, index((8, WIDE), 0), found)
    back_ref[...] = jnp.where(found == slot[:8], 1.0, 0.0).astype(BF16)


def sort_rows(info_ref, rows_ref, out_ref, back_ref, staged, sems):
    crossing = info_ref[0] == 0
    half_width = rows_ref.shape[1] - EXTRA
    total = ALONG * TIGHT
    tail = rows_ref[:, half_width:].astype(F32)
    named = jnp.where((tail > 0.0) & (index((WIDE, EXTRA), 1) < EXPERTS - 0.5), 1.0, 0.0)
    one, two = index((WIDE, WIDE), 0), index((WIDE, WIDE), 1)
    ahead = jnp.where((split(one, ROWS)[0] == split(two, ROWS)[0]) & (two < one), 1.0, 0.0)
    rank = jnp.dot(ahead.astype(BF16), named.astype(BF16), preferred_element_type=F32)
    code = jnp.where(named > 0.5, rank, -1.0).astype(BF16)

    def matrix(found, at, to):
        source, slot = split(split(at, TIGHT)[1], MOST)
        block, row = split(to, ROWS)
        found = jnp.where(crossing, found, row)
        return jnp.where((block == source) & (found == slot), 1.0, 0.0).astype(BF16)

    target = split(index((total, EXTRA), 0), TIGHT)[0]
    pick = jnp.where(index((total, EXTRA), 1) == target, 1.0, 0.0).astype(BF16)
    found = lax.dot_general(pick, code, (((1,), (1,)), ((), ())), preferred_element_type=F32)
    forth = matrix(found, index((total, WIDE), 0), index((total, WIDE), 1))
    target = split(index((EXTRA, total), 1), TIGHT)[0]
    pick = jnp.where(index((EXTRA, total), 0) == target, 1.0, 0.0).astype(BF16)
    found = jnp.dot(code, pick, preferred_element_type=F32)
    back_ref[...] = matrix(found, index((WIDE, total), 1), index((WIDE, total), 0))
    rows = rows_ref[...]
    copies = []
    for t in range(ALONG):
        staged[t] = jnp.dot(
            forth[t * TIGHT : (t + 1) * TIGHT], rows, preferred_element_type=F32
        ).astype(BF16)
        copies.append(pltpu.make_async_copy(staged.at[t], out_ref.at[t], sems.at[t]))
        copies[t].start()
    for copy in copies:
        copy.wait()


def gate(rows_ref, gain_ref, own_ref, other_ref, kept_ref, sent_ref, scaled, squares):
    half_width, cols = own_ref.shape
    deep = half_width // 4
    for k in range(4):
        at = slice(k * deep, (k + 1) * deep)
        values = rows_ref[:, at].astype(F32)
        part = jnp.sum(values * values, axis=1, keepdims=True)
        squares[...] = jnp.broadcast_to(part, squares.shape) + (squares[...] if k else 0.0)
        scaled[:, at] = (values * gain_ref[:, at].astype(F32)).astype(BF16)
    for at, weights in ((0, own_ref), (cols, other_ref)):
        sums = jnp.dot(scaled[...], weights[...], preferred_element_type=F32)
        kept_ref[:, at : at + cols] = sums
        sent_ref[:, at : at + cols] = sums.astype(BF16)
    total = squares[...]
    high = total.astype(BF16).astype(F32)
    lane = lax.broadcasted_iota(jnp.int32, total.shape, 1)
    pieces = jnp.where(lane == 0, high, jnp.where(lane == 1, total - high, 0.0))
    kept_ref[:, 2 * cols :] = total
    sent_ref[:, 2 * cols :] = pieces.astype(BF16)


def expert(width, info_ref, rows_ref, kept_ref, got_ref, down_ref, out_ref):
    units, half_width = down_ref.shape[0] // 2, down_ref.shape[1]
    which = info_ref[1]
    tail = rows_ref[:, half_width:].astype(F32)
    lane = lax.broadcasted_iota(jnp.int32, tail.shape, 1)
    mine = (lane == which) | (lane == which + EXPERTS)
    weight = jnp.sum(jnp.where(mine, tail, 0.0), axis=1, keepdims=True)
    far = jnp.sum(got_ref[:, 4 * units :].astype(F32), axis=1, keepdims=True)
    squares = kept_ref[:, 4 * units : 4 * units + 1] + far
    scale = lax.rsqrt(squares * (1.0 / width) + 1e-06)
    hidden = []
    for at in range(2):
        lo = 2 * units * at
        a = (kept_ref[:, lo : lo + units] + got_ref[:, lo : lo + units].astype(F32)) * scale
        lo += units
        b = (kept_ref[:, lo : lo + units] + got_ref[:, lo : lo + units].astype(F32)) * scale
        hidden.append((a / (1.0 + jnp.exp(-a)) * b * weight).astype(BF16))
    both = jnp.concatenate(hidden, axis=1)
    deep = half_width // 4
    for k in range(4):
        at = slice(k * deep, (k + 1) * deep)
        out_ref[:, at] = jnp.dot(both, down_ref[:, at], preferred_element_type=F32).astype(BF16)


def gather_parts(back_ref, parts_ref, out_ref):
    out_ref[...] = jnp.dot(back_ref[...], parts_ref[...], preferred_element_type=F32).astype(BF16)


def finish(back_ref, parts_ref, rows_ref, out_ref, squares_ref):
    mixture = jnp.dot(back_ref[...], parts_ref[...], preferred_element_type=F32)[:ROWS]
    layer = (rows_ref[...].astype(F32) + mixture).astype(BF16)
    out_ref[...] = layer
    values = layer.astype(F32)
    squares_ref[...] = jnp.broadcast_to(
        jnp.sum(values * values, axis=1, keepdims=True), squares_ref.shape
    )


def close(width, theirs_ref, far_ref, gain_ref, out_ref):
    values = theirs_ref[...].astype(F32)
    total = jnp.sum(values * values, axis=1, keepdims=True) + far_ref[:, :1]
    scale = lax.rsqrt(total * (1.0 / width) + 1e-06)
    out_ref[...] = (values * scale * gain_ref[...].astype(F32)).astype(BF16)


def local(kernel, outs, *args, spaces=None, out_spaces=None, scratch=(), vmem=24 * MIB):
    spaces = spaces or [pltpu.VMEM] * len(args)
    out_spaces = out_spaces or [pltpu.VMEM] * len(outs)
    return pl.pallas_call(
        kernel,
        out_shape=outs,
        in_specs=[pl.BlockSpec(memory_space=space) for space in spaces],
        out_specs=[pl.BlockSpec(memory_space=space) for space in out_spaces],
        scratch_shapes=list(scratch),
        compiler_params=pltpu.CompilerParams(vmem_limit_bytes=vmem),
    )(*args)


def shape(*dims, dtype=BF16):
    return jax.ShapeDtypeStruct(dims, dtype)


def body(section_rows, routes, route_weights, in_gain, gate_up, down, out_gain):
    rows = section_rows[0]
    half_width = rows.shape[1]
    ep = lax.axis_size("ep")
    width = half_width * lax.axis_size("tp")
    units = down.shape[2]
    cols = gate_up.shape[3]
    near, far = crossed_groups(ep, 0), crossed_groups(ep, 1)
    place = lax.axis_index("ep")
    info = jnp.stack([place % 2, place // SPAN]).astype(jnp.int32)
    other_core = [(i, i ^ 1) for i in range(ep)]
    swap = [(0, 1), (1, 0)]
    full = half_width + EXTRA
    total = ALONG * TIGHT

    gate_own, down_own = gate_up[0, 0], down[0, 0]
    gate_other = lax.ppermute(gate_own, "ep", other_core)
    down_other = lax.ppermute(down_own, "ep", other_core)
    gain_other = lax.ppermute(out_gain, "section", swap)

    down_all = jnp.concatenate([down_own, down_other], axis=0)

    slots = np.arange(EXTRA)
    slots = np.where(slots < 2 * EXPERTS, slots % EXPERTS, -1).astype(np.int32)
    named = routes[0][:, :, None] == slots[None, None, :]
    leaving, home_back = local(
        announce,
        [shape(WIDE, full), shape(8, WIDE)],
        info,
        rows,
        jnp.sum(jnp.where(named, route_weights[0][:, :, None], 0.0), axis=1),
        spaces=[pltpu.SMEM] + [pltpu.VMEM] * 2,
    )
    met = traded(leaving.reshape(ALONG, ROWS, full), near).reshape(WIDE, full)
    sorted_rows, far_back = local(
        sort_rows,
        [shape(ALONG, TIGHT, full), shape(WIDE, total)],
        info,
        met,
        spaces=[pltpu.SMEM, pltpu.VMEM],
        out_spaces=[pltpu.HBM, pltpu.VMEM],
        scratch=[pltpu.VMEM((ALONG, TIGHT, full), BF16), pltpu.SemaphoreType.DMA((ALONG,))],
        vmem=53 * MIB,
    )
    gathered = traded(sorted_rows, far).reshape(total, full)
    gathered, gain_other = lax.optimization_barrier((gathered, gain_other))
    kept, sent = local(
        gate,
        [shape(total, 2 * cols + EXTRA, dtype=F32), shape(total, 2 * cols + EXTRA)],
        gathered,
        in_gain,
        gate_own,
        gate_other,
        scratch=[pltpu.VMEM((total, half_width), BF16), pltpu.VMEM((total, EXTRA), F32)],
    )
    got = lax.ppermute(sent, "tp", swap)
    (parts,) = local(
        functools.partial(expert, width),
        [shape(total, half_width)],
        info,
        gathered,
        kept,
        got,
        down_all,
        spaces=[pltpu.SMEM] + [pltpu.VMEM] * 4,
    )
    returned = traded(parts.reshape(ALONG, TIGHT, half_width), far).reshape(total, half_width)
    (summed,) = local(gather_parts, [shape(WIDE, half_width)], far_back, returned)
    home = traded(summed.reshape(ALONG, ROWS, half_width), near).reshape(WIDE, half_width)
    layer_out, squares = local(
        finish, [shape(ROWS, half_width), shape(ROWS, EXTRA, dtype=F32)], home_back, home, rows
    )
    theirs = lax.ppermute(layer_out, "section", swap)
    far_squares = lax.ppermute(squares, ("section", "tp"), [(0, 3), (3, 0), (1, 2), (2, 1)])
    (handed,) = local(
        functools.partial(close, width), [shape(ROWS, half_width)], theirs, far_squares, gain_other
    )
    return (layer_out[None], handed[None])


def solution(mesh):
    return jax.shard_map(
        body,
        mesh=mesh,
        in_specs=(
            P("section", "ep", "tp"),
            P("section", "ep", None),
            P("section", "ep", None),
            P("section", "tp"),
            P("section", "ep", "tp", None),
            P("section", "ep", None, "tp"),
            P("section", "tp"),
        ),
        out_specs=(P("section", "ep", "tp"), P("section", "ep", "tp")),
        check_vma=False,
    )
```

time: 123 us -> 119 us (0.967)
  local copies, waits for them, and re-layouts: 3.48 us -> 1.02 us
  Pallas kernels: 11.2 us -> 8.88 us
  other arithmetic: 0.08 us -> 2.18 us
  waiting for transfers between devices: 20.5 us -> 19.2 us
    unnamed x18 -> x12, local copies, waits for them, and re-layouts: 3.23 us -> 0.76 us
    pallas_call x7, Pallas kernels: 11.2 us -> 8.88 us  [local(): pl.pallas_call(kernel, out_shape=outs, in_specs=[pl.BlockSpec(memory_spac...]
    ppermute x1, waiting for transfers between devices: 4.67 us -> 3.36 us  [body(): got = lax.ppermute(sent, 'tp', swap)]
    concatenate x0 -> x1, other arithmetic: none -> 1.3 us  [body(): down_all = jnp.concatenate([down_own, down_other], axis=0)]
  transfers between devices with their start and end apart: 7 -> 7, of which waited for: 4 -> 4; matrix products, arithmetic and copies ran while one was open for 0% -> 1% of each run, Pallas kernels for 3% -> 2%
where the time goes in v3:
time: 119 us; the launch traced here: 118 us
  blocking collectives  57.7 us (48%)
  starting transfers between devices  28.2 us (24%)
  waiting for transfers between devices  19.2 us (16%)
  Pallas kernels  8.88 us (7%)
  other arithmetic  2.18 us (2%)
    all_to_all x3, blocking collectives, traded(): lax.all_to_all(block, 'ep', 0, 0, axis_index_groups=groups, tiled=True)  57.7 us
    all_to_all x1, waiting for transfers between devices, traded(): lax.all_to_all(block, 'ep', 0, 0, axis_index_groups=groups, tiled=True)  10 us
    pallas_call x7, Pallas kernels, local(): pl.pallas_call(kernel, out_shape=outs, in_specs=[pl.BlockSpec(memory_spac...  8.88 us
    all_to_all x1, starting transfers between devices, traded(): lax.all_to_all(block, 'ep', 0, 0, axis_index_groups=groups, tiled=True)  7.56 us
    ppermute x1, starting transfers between devices, body(): gain_other = lax.ppermute(out_gain, 'section', swap)  4.93 us
    ppermute x1, starting transfers between devices, body(): theirs = lax.ppermute(layer_out, 'section', swap)  4.92 us
    ppermute x1, waiting for transfers between devices, body(): lax.ppermute(squares, ('section', 'tp'), [(0, 3), (3, 0), (1, 2), (2, 1)])  3.63 us
    ppermute x1, starting transfers between devices, body(): got = lax.ppermute(sent, 'tp', swap)  3.4 us
  transfers between devices with their start and end apart: 7, of which 4 were waited for; matrix products, arithmetic and copies ran while one was open for 1% of the time, Pallas kernels for 2%

profile of v3, /device:TPU:8, one launch (start us, length us, event | category | flops | bytes accessed | tf_op | source)
XLA Modules:
  0.0 118.0 jit_solution(12277286461771114055)
XLA Ops:
  0.7 0.8 select_reduce_fusion.dense_ref
  1.5 0.7 copy-done.1
  2.3 0.8 shard_map.95
  3.1 20.3 %all_to_all.20 = bf16[8,4,3712]{2,1,0:T(4,128)(2,1)S(1)} all-to-all(bf16[8,4,3712]{2,1,0:T(4,128)(2,1)S(1)} %reshape.27), channel_id=1, replica_groups={{0,4,8,12,16,20,24,28},{32,36,40,44,48,52,56,60},{64,68,72,76,80,84,88,..., dimensions={0} | all-to-all | bytes 475136 | tf_op jit(solution)/shard_map/all_to_all | solution.py:32
  23.5 2.2 %shard_map.96 = (bf16[8,24,3712]{2,1,0:T(8,128)(2,1)}, bf16[32,192]{1,0:T(8,128)(2,1)S(1)}) custom-call(s32[2]{0:T(128)S(1)} %pad_add_fusion.info_ref, bf16[32,3712]{1,0:T(8,128)(2,1)S(1)} %reshape.28.rows_ref), custom_call_target="tpu_custom_call" | custom-call | tf_op jit(solution)/shard_map/pallas_call | solution.py:182
  25.7 7.6 %all-to-all-start.1 = ((bf16[8,24,3712]{2,1,0:T(8,128)(2,1)}), bf16[8,24,3712]{2,1,0:T(8,128)(2,1)S(1)}, u32[]{:S(2)}, u32[]{:S(2)}) async-start(bf16[8,24,3712]{2,1,0:T(8,128)(2,1)} %get-tuple-element.15), calls=%async_computation.1 | async-start | bytes 2850816 | tf_op jit(solution)/shard_map/all_to_all | solution.py:32
  33.3 1.9 %collective-permute-start.1 = (bf16[3584,256]{1,0:T(8,128)(2,1)S(1)}, bf16[3584,256]{1,0:T(8,128)(2,1)}, u32[]{:S(2)}, u32[]{:S(2)}) collective-permute-start(bf16[3584,256]{1,0:T(8,128)(2,1)S(1)} %bitcast.16), channel_id=1, source_target_pairs={{0,2},{2,0},{4,6},{6,4},{8,10},{10,8},{12,14},{14,12},{16,18},{18,... | collective-permute-start | bytes 5505032 | tf_op jit(solution)/shard_map/ppermute | solution.py:212
  35.2 2.4 %collective-permute-start.3 = (bf16[128,3584]{1,0:T(8,128)(2,1)}, bf16[128,3584]{1,0:T(8,128)(2,1)}, u32[]{:S(2)}, u32[]{:S(2)}) collective-permute-start(bf16[128,3584]{1,0:T(8,128)(2,1)} %bitcast.20), channel_id=1, source_target_pairs={{0,2},{2,0},{4,6},{6,4},{8,10},{10,8},{12,14},{14,12},{16,18},{18,... | collective-permute-start | bytes 2752520 | tf_op jit(solution)/shard_map/ppermute | solution.py:213
  37.6 4.9 %collective-permute-start = (bf16[1,3584]{1,0:T(2,128)(2,1)S(1)}, bf16[1,3584]{1,0:T(2,128)(2,1)S(1)}, u32[]{:S(2)}, u32[]{:S(2)}) collective-permute-start(bf16[1,3584]{1,0:T(2,128)(2,1)S(1)} %copy-done.5), channel_id=1, source_target_pairs={{0,256},{256,0},{1,257},{257,1},{2,258},{258,2},{3,259},{259,3},{4... | collective-permute-start | bytes 21512 | tf_op jit(solution)/shard_map/ppermute | solution.py:214
  42.6 2.2 %collective-permute-done.gain_ref = bf16[1,3584]{1,0:T(2,128)(2,1)S(1)} collective-permute-done((bf16[1,3584]{1,0:T(2,128)(2,1)S(1)}, bf16[1,3584]{1,0:T(2,128)(2,1)S(1)}, u32[]{:S(2)}, u32[]{:S(2)}) %collective-permute-start) | collective-permute-done | bytes 7200 | tf_op jit(solution)/shard_map/ppermute | solution.py:214
  44.8 10.0 %all-to-all-done.1 = bf16[8,24,3712]{2,1,0:T(8,128)(2,1)S(1)} async-done(((bf16[8,24,3712]{2,1,0:T(8,128)(2,1)}), bf16[8,24,3712]{2,1,0:T(8,128)(2,1)S(1)}, u32[]{:S(2)}, u32[]{:S(2)}) %all-to-all-start.1) | async-done | bytes 1425440 | tf_op jit(solution)/shard_map/all_to_all | solution.py:32
  54.8 2.6 %shard_map.97 = (f32[192,640]{1,0:T(8,128)S(1)}, bf16[192,640]{1,0:T(8,128)(2,1)S(1)}) custom-call(bf16[192,3712]{1,0:T(8,128)(2,1)S(1)} %bitcast.12, bf16[1,3584]{1,0:T(2,128)(2,1)S(1)} %copy-done.3, bf16[3584,256]{1,0:T(8,128)(2,1)S(1)} %bitcast.17, bf16[3584,256]{1,0:T(8,128)(2,1)} %collective-permute-done.1.other_ref), custom_call_target="tpu_custom_call" | custom-call | tf_op jit(solution)/shard_map/pallas_call | solution.py:182
  57.4 3.4 %collective-permute-start.2 = (bf16[192,640]{1,0:T(8,128)(2,1)S(1)}, bf16[192,640]{1,0:T(8,128)(2,1)S(1)}, u32[]{:S(2)}, u32[]{:S(2)}) collective-permute-start(bf16[192,640]{1,0:T(8,128)(2,1)S(1)} %get-tuple-element.18), channel_id=1, source_target_pairs={{0,1},{1,0},{2,3},{3,2},{4,5},{5,4},{6,7},{7,6},{8,9},{9,8},{10,11... | collective-permute-start | bytes 737288 | tf_op jit(solution)/shard_map/ppermute | solution.py:251
  60.9 1.3 %pad_maximum_fusion.down_ref = bf16[256,3584]{1,0:T(8,128)(2,1)S(1)} fusion(bf16[128,3584]{1,0:T(8,128)(2,1)} %collective-permute-done.3, bf16[128,3584]{1,0:T(8,128)(2,1)S(1)} %bitcast.21), kind=kLoop, calls=%fused_computation | loop fusion | flops 3670016 | bytes 3670016 | tf_op jit(solution)/shard_map/concatenate | solution.py:216
  62.2 3.4 %collective-permute-done.2.got_ref = bf16[192,640]{1,0:T(8,128)(2,1)S(1)} collective-permute-done((bf16[192,640]{1,0:T(8,128)(2,1)S(1)}, bf16[192,640]{1,0:T(8,128)(2,1)S(1)}, u32[]{:S(2)}, u32[]{:S(2)}) %collective-permute-start.2) | collective-permute-done | bytes 245792 | tf_op jit(solution)/shard_map/ppermute | solution.py:251
  65.5 1.3 %shard_map.98 = bf16[192,3584]{1,0:T(8,128)(2,1)S(1)} custom-call(s32[2]{0:T(128)S(1)} %pad_add_fusion.info_ref, bf16[192,3712]{1,0:T(8,128)(2,1)S(1)} %bitcast.13, f32[192,640]{1,0:T(8,128)S(1)} %get-tuple-element.17.kept_ref, bf16[192,640]{1,0:T(8,128)(2,1)S(1)} %collective-permute-done.2.got_ref, bf16[256,3584]{1,0:T(8,128)(2,1)S(1)} %pad_maximum_fusion.down_ref), custom_call_target="tpu_custom_call" | custom-call | tf_op jit(solution)/shard_map/pallas_call | solution.py:182
  66.9 24.9 %all_to_all.21 = bf16[8,24,3584]{2,1,0:T(8,128)(2,1)S(1)} all-to-all(bf16[8,24,3584]{2,1,0:T(8,128)(2,1)S(1)} %bitcast.14), channel_id=1, replica_groups={{2,6,10,14,18,22,26,30},{34,38,42,46,50,54,58,62},{66,70,74,78,82,86,90..., dimensions={0} | all-to-all | bytes 2752512 | tf_op jit(solution)/shard_map/all_to_all | solution.py:32
  91.7 0.3 shard_map.99
  92.2 12.5 %all_to_all.22 = bf16[8,4,3584]{2,1,0:T(4,128)(2,1)S(1)} all-to-all(bf16[8,4,3584]{2,1,0:T(4,128)(2,1)S(1)} %reshape.32), channel_id=1, replica_groups={{0,4,8,12,16,20,24,28},{32,36,40,44,48,52,56,60},{64,68,72,76,80,84,88,..., dimensions={0} | all-to-all | bytes 458752 | tf_op jit(solution)/shard_map/all_to_all | solution.py:32
  104.8 0.8 shard_map.100
  105.5 4.9 %collective-permute-start.4 = (bf16[4,3584]{1,0:T(4,128)(2,1)}, bf16[4,3584]{1,0:T(4,128)(2,1)S(1)}, u32[]{:S(2)}, u32[]{:S(2)}) collective-permute-start(bf16[4,3584]{1,0:T(4,128)(2,1)} %get-tuple-element.19), channel_id=1, source_target_pairs={{0,256},{256,0},{1,257},{257,1},{2,258},{258,2},{3,259},{259,3},{4... | collective-permute-start | bytes 86024 | tf_op jit(solution)/shard_map/ppermute | solution.py:268
  110.5 3.0 %collective-permute-start.5 = (f32[4,128]{1,0:T(4,128)S(1)}, f32[4,128]{1,0:T(4,128)S(1)}, u32[]{:S(2)}, u32[]{:S(2)}) collective-permute-start(f32[4,128]{1,0:T(4,128)S(1)} %get-tuple-element.20), channel_id=1, source_target_pairs={{0,257},{257,0},{1,256},{256,1},{2,259},{259,2},{3,258},{258,3},{4... | collective-permute-start | bytes 6152 | tf_op jit(solution)/shard_map/ppermute | solution.py:269
  113.5 3.6 %collective-permute-done.5.far_ref = f32[4,128]{1,0:T(4,128)S(1)} collective-permute-done((f32[4,128]{1,0:T(4,128)S(1)}, f32[4,128]{1,0:T(4,128)S(1)}, u32[]{:S(2)}, u32[]{:S(2)}) %collective-permute-start.5) | collective-permute-done | bytes 2080 | tf_op jit(solution)/shard_map/ppermute | solution.py:269
  117.2 0.8 shard_map.101
  (19 shorter events, 0.4 us)
Async XLA Ops:
  1.5 0.8 copy-start.1
  23.5 9.8 %copy-start = (bf16[1,1,3584,256]{3,2,1,0:T(8,128)(2,1)S(1)}, bf16[1,1,3584,256]{3,2,1,0:T(8,128)(2,1)}, u32[]{:S(2)}) copy-start(bf16[1,1,3584,256]{3,2,1,0:T(8,128)(2,1)} %param.12) | copy-start | bytes 5505028
  23.5 14.2 %copy-start.5 = (bf16[1,3584]{1,0:T(2,128)(2,1)S(1)}, bf16[1,3584]{1,0:T(2,128)(2,1)}, u32[]{:S(2)}) copy-start(bf16[1,3584]{1,0:T(2,128)(2,1)} %param.14) | copy-start | bytes 21508
  23.5 31.3 %copy-start.3 = (bf16[1,3584]{1,0:T(2,128)(2,1)S(1)}, bf16[1,3584]{1,0:T(2,128)(2,1)}, u32[]{:S(2)}) copy-start(bf16[1,3584]{1,0:T(2,128)(2,1)} %gain_ref.1) | copy-start | bytes 21508
  25.7 29.0 %all-to-all-start.1 = ((bf16[8,24,3712]{2,1,0:T(8,128)(2,1)}), bf16[8,24,3712]{2,1,0:T(8,128)(2,1)S(1)}, u32[]{:S(2)}, u32[]{:S(2)}) async-start(bf16[8,24,3712]{2,1,0:T(8,128)(2,1)} %get-tuple-element.15), calls=%async_computation.1 | async-start | bytes 2850816 | tf_op jit(solution)/shard_map/all_to_all | solution.py:32
  33.3 21.5 %collective-permute-start.1 = (bf16[3584,256]{1,0:T(8,128)(2,1)S(1)}, bf16[3584,256]{1,0:T(8,128)(2,1)}, u32[]{:S(2)}, u32[]{:S(2)}) collective-permute-start(bf16[3584,256]{1,0:T(8,128)(2,1)S(1)} %bitcast.16), channel_id=1, source_target_pairs={{0,2},{2,0},{4,6},{6,4},{8,10},{10,8},{12,14},{14,12},{16,18},{18,... | collective-permute-start | bytes 5505032 | tf_op jit(solution)/shard_map/ppermute | solution.py:212
  35.2 25.6 %collective-permute-start.3 = (bf16[128,3584]{1,0:T(8,128)(2,1)}, bf16[128,3584]{1,0:T(8,128)(2,1)}, u32[]{:S(2)}, u32[]{:S(2)}) collective-permute-start(bf16[128,3584]{1,0:T(8,128)(2,1)} %bitcast.20), channel_id=1, source_target_pairs={{0,2},{2,0},{4,6},{6,4},{8,10},{10,8},{12,14},{14,12},{16,18},{18,... | collective-permute-start | bytes 2752520 | tf_op jit(solution)/shard_map/ppermute | solution.py:213
  37.6 7.1 %collective-permute-start = (bf16[1,3584]{1,0:T(2,128)(2,1)S(1)}, bf16[1,3584]{1,0:T(2,128)(2,1)S(1)}, u32[]{:S(2)}, u32[]{:S(2)}) collective-permute-start(bf16[1,3584]{1,0:T(2,128)(2,1)S(1)} %copy-done.5), channel_id=1, source_target_pairs={{0,256},{256,0},{1,257},{257,1},{2,258},{258,2},{3,259},{259,3},{4... | collective-permute-start | bytes 21512 | tf_op jit(solution)/shard_map/ppermute | solution.py:214
  54.8 6.1 %copy-start.4 = (bf16[1,1,128,3584]{3,2,1,0:T(8,128)(2,1)S(1)}, bf16[1,1,128,3584]{3,2,1,0:T(8,128)(2,1)}, u32[]{:S(2)}) copy-start(bf16[1,1,128,3584]{3,2,1,0:T(8,128)(2,1)} %param.13) | copy-start | bytes 2752516
  57.4 8.1 %collective-permute-start.2 = (bf16[192,640]{1,0:T(8,128)(2,1)S(1)}, bf16[192,640]{1,0:T(8,128)(2,1)S(1)}, u32[]{:S(2)}, u32[]{:S(2)}) collective-permute-start(bf16[192,640]{1,0:T(8,128)(2,1)S(1)} %get-tuple-element.18), channel_id=1, source_target_pairs={{0,1},{1,0},{2,3},{3,2},{4,5},{5,4},{6,7},{7,6},{8,9},{9,8},{10,11... | collective-permute-start | bytes 737288 | tf_op jit(solution)/shard_map/ppermute | solution.py:251
  91.7 13.0 %copy-start.2 = (bf16[1,4,3584]{2,1,0:T(4,128)(2,1)S(1)}, bf16[1,4,3584]{2,1,0:T(4,128)(2,1)}, u32[]{:S(2)}) copy-start(bf16[1,4,3584]{2,1,0:T(4,128)(2,1)} %param.8) | copy-start | bytes 86020
  105.5 11.6 %collective-permute-start.4 = (bf16[4,3584]{1,0:T(4,128)(2,1)}, bf16[4,3584]{1,0:T(4,128)(2,1)S(1)}, u32[]{:S(2)}, u32[]{:S(2)}) collective-permute-start(bf16[4,3584]{1,0:T(4,128)(2,1)} %get-tuple-element.19), channel_id=1, source_target_pairs={{0,256},{256,0},{1,257},{257,1},{2,258},{258,2},{3,259},{259,3},{4... | collective-permute-start | bytes 86024 | tf_op jit(solution)/shard_map/ppermute | solution.py:268
  110.5 6.7 %collective-permute-start.5 = (f32[4,128]{1,0:T(4,128)S(1)}, f32[4,128]{1,0:T(4,128)S(1)}, u32[]{:S(2)}, u32[]{:S(2)}) collective-permute-start(f32[4,128]{1,0:T(4,128)S(1)} %get-tuple-element.20), channel_id=1, source_target_pairs={{0,257},{257,0},{1,256},{256,1},{2,259},{259,2},{3,258},{258,3},{4... | collective-permute-start | bytes 6152 | tf_op jit(solution)/shard_map/ppermute | solution.py:269

commit v4 on v3

--- a/solution.py
+++ b/solution.py
@@ -2,7 +2,6 @@
 
 import jax
 import jax.numpy as jnp
-import numpy as np
 from jax import lax
 from jax.experimental import pallas as pl
 from jax.experimental.pallas import tpu as pltpu
@@ -18,6 +17,7 @@
 WIDE = ALONG * ROWS
 TIGHT = ALONG * MOST
 MIB = 1024 * 1024
+CHUNK = 1024
 
 
 def crossed_groups(ep, first):
@@ -41,40 +41,26 @@
     return whole, at - whole * count
 
 
-def announce(info_ref, rows_ref, dense_ref, out_ref, back_ref):
-    crossing = info_ref[0] == 0
+def announce(rows_ref, routes_ref, weights_ref, out_ref):
     half_width = rows_ref.shape[1]
-    lane = index((ROWS, EXTRA), 1)
-    dense = dense_ref[...]
+    row = lax.broadcasted_iota(jnp.int32, (ROWS, EXTRA), 0)
+    lane = lax.broadcasted_iota(jnp.int32, (ROWS, EXTRA), 1)
+    dense = jnp.zeros((ROWS, EXTRA), F32)
+    for r in range(ROWS):
+        for k in range(routes_ref.shape[1]):
+            name = routes_ref[r, k]
+            here = (row == r) & ((lane == name) | (lane == name + EXPERTS))
+            dense += jnp.where(here, weights_ref[r, k], 0.0)
     high = dense.astype(BF16).astype(F32)
-    extra = jnp.where(lane < EXPERTS, high, dense - high)
-    named = jnp.where((dense > 0.0) & (lane < EXPERTS), 1.0, 0.0)
-    codes, before = [], jnp.zeros((1, EXTRA), F32)
-    for r in range(ROWS):
-        codes.append(jnp.where(named[r : r + 1] > 0.5, before, -1.0))
-        before = before + named[r : r + 1]
-    rows = rows_ref[...].astype(F32)
-    target, slot = split(index((WIDE, 1), 0), ROWS)
-    pick = jnp.where(index((WIDE, EXTRA), 1) == target, 1.0, 0.0)
-    body = jnp.zeros((WIDE, half_width), F32)
-    tail = jnp.zeros((WIDE, EXTRA), F32)
-    for r in range(ROWS):
-        code = jnp.sum(pick * codes[r], axis=1, keepdims=True)
-        here = jnp.where(jnp.where(crossing, r * 1.0, code) == slot, 1.0, 0.0)
-        body += here * rows[r : r + 1]
-        tail += here * extra[r : r + 1]
-    out_ref[:, :half_width] = body.astype(BF16)
-    out_ref[:, half_width:] = tail.astype(BF16)
-    table = jnp.concatenate(codes + [jnp.full((8 - ROWS, EXTRA), -1.0, F32)], axis=0)
-    target, slot = split(index((EXTRA, WIDE), 1), ROWS)
-    spread = jnp.where(index((EXTRA, WIDE), 0) == target, 1.0, 0.0).astype(BF16)
-    found = jnp.dot(table.astype(BF16), spread, preferred_element_type=F32)
-    found = jnp.where(crossing, index((8, WIDE), 0), found)
-    back_ref[...] = jnp.where(found == slot[:8], 1.0, 0.0).astype(BF16)
+    extra = jnp.where(lane < EXPERTS, high, dense - high).astype(BF16)
+    rows = rows_ref[...]
+    for t in range(ALONG):
+        out_ref[t, :, :half_width] = rows
+        out_ref[t, :, half_width:] = extra
 
 
 def sort_rows(info_ref, rows_ref, out_ref, back_ref, staged, sems):
-    crossing = info_ref[0] == 0
+    crossing, which = info_ref[0] == 0, info_ref[1].astype(F32)
     half_width = rows_ref.shape[1] - EXTRA
     total = ALONG * TIGHT
     tail = rows_ref[:, half_width:].astype(F32)
@@ -86,32 +72,35 @@
 
     def matrix(found, at, to):
         source, slot = split(split(at, TIGHT)[1], MOST)
-        block, row = split(to, ROWS)
-        found = jnp.where(crossing, found, row)
+        block = split(to, ROWS)[0]
         return jnp.where((block == source) & (found == slot), 1.0, 0.0).astype(BF16)
 
-    target = split(index((total, EXTRA), 0), TIGHT)[0]
-    pick = jnp.where(index((total, EXTRA), 1) == target, 1.0, 0.0).astype(BF16)
-    found = lax.dot_general(pick, code, (((1,), (1,)), ((), ())), preferred_element_type=F32)
-    forth = matrix(found, index((total, WIDE), 0), index((total, WIDE), 1))
-    target = split(index((EXTRA, total), 1), TIGHT)[0]
-    pick = jnp.where(index((EXTRA, total), 0) == target, 1.0, 0.0).astype(BF16)
-    found = jnp.dot(code, pick, preferred_element_type=F32)
-    back_ref[...] = matrix(found, index((WIDE, total), 1), index((WIDE, total), 0))
-    rows = rows_ref[...]
+    def pick(at, to):
+        target = jnp.where(crossing, split(at, TIGHT)[0], which)
+        return jnp.where(to == target, 1.0, 0.0).astype(BF16)
+
+    chosen = pick(index((total, 1), 0), index((total, EXTRA), 1))
+    found = lax.dot_general(chosen, code, (((1,), (1,)), ((), ())), preferred_element_type=F32)
+    forth = matrix(found, index((total, 1), 0), index((1, WIDE), 1))
     copies = []
-    for t in range(ALONG):
-        staged[t] = jnp.dot(
-            forth[t * TIGHT : (t + 1) * TIGHT], rows, preferred_element_type=F32
-        ).astype(BF16)
-        copies.append(pltpu.make_async_copy(staged.at[t], out_ref.at[t], sems.at[t]))
-        copies[t].start()
+    for k, lo in enumerate(range(0, half_width + EXTRA, CHUNK)):
+        at = pl.ds(lo, min(CHUNK, half_width + EXTRA - lo))
+        staged[:, at] = jnp.dot(forth, rows_ref[:, at], preferred_element_type=F32).astype(BF16)
+        copies.append(pltpu.make_async_copy(staged.at[:, at], out_ref.at[:, at], sems.at[k]))
+        copies[k].start()
+    chosen = pick(index((1, total), 1), index((EXTRA, total), 0))
+    found = jnp.dot(code, chosen, preferred_element_type=F32)
+    back_ref[...] = matrix(found, index((1, total), 1), index((WIDE, 1), 0))
     for copy in copies:
         copy.wait()
 
 
-def gate(rows_ref, gain_ref, own_ref, other_ref, kept_ref, sent_ref, scaled, squares):
+def gate(
+    rows_ref, gain_ref, own_ref, other_hbm, kept_ref, sent_ref, scaled, squares, other_ref, sem
+):
     half_width, cols = own_ref.shape
+    copy = pltpu.make_async_copy(other_hbm, other_ref, sem)
+    copy.start()
     deep = half_width // 4
     for k in range(4):
         at = slice(k * deep, (k + 1) * deep)
@@ -120,6 +109,8 @@
         squares[...] = jnp.broadcast_to(part, squares.shape) + (squares[...] if k else 0.0)
         scaled[:, at] = (values * gain_ref[:, at].astype(F32)).astype(BF16)
     for at, weights in ((0, own_ref), (cols, other_ref)):
+        if at:
+            copy.wait()
         sums = jnp.dot(scaled[...], weights[...], preferred_element_type=F32)
         kept_ref[:, at : at + cols] = sums
         sent_ref[:, at : at + cols] = sums.astype(BF16)
@@ -159,8 +150,10 @@
     out_ref[...] = jnp.dot(back_ref[...], parts_ref[...], preferred_element_type=F32).astype(BF16)
 
 
-def finish(back_ref, parts_ref, rows_ref, out_ref, squares_ref):
-    mixture = jnp.dot(back_ref[...], parts_ref[...], preferred_element_type=F32)[:ROWS]
+def finish(parts_ref, rows_ref, out_ref, squares_ref):
+    mixture = parts_ref[0].astype(F32)
+    for t in range(1, ALONG):
+        mixture += parts_ref[t].astype(F32)
     layer = (rows_ref[...].astype(F32) + mixture).astype(BF16)
     out_ref[...] = layer
     values = layer.astype(F32)
@@ -215,29 +208,27 @@
 
     down_all = jnp.concatenate([down_own, down_other], axis=0)
 
-    slots = np.arange(EXTRA)
-    slots = np.where(slots < 2 * EXPERTS, slots % EXPERTS, -1).astype(np.int32)
-    named = routes[0][:, :, None] == slots[None, None, :]
-    leaving, home_back = local(
+    (leaving,) = local(
         announce,
-        [shape(WIDE, full), shape(8, WIDE)],
-        info,
+        [shape(ALONG, ROWS, full)],
         rows,
-        jnp.sum(jnp.where(named, route_weights[0][:, :, None], 0.0), axis=1),
-        spaces=[pltpu.SMEM] + [pltpu.VMEM] * 2,
-    )
-    met = traded(leaving.reshape(ALONG, ROWS, full), near).reshape(WIDE, full)
+        routes[0],
+        route_weights[0],
+        spaces=[pltpu.VMEM, pltpu.SMEM, pltpu.SMEM],
+        vmem=60 * MIB,
+    )
+    met = traded(leaving, near).reshape(WIDE, full)
     sorted_rows, far_back = local(
         sort_rows,
-        [shape(ALONG, TIGHT, full), shape(WIDE, total)],
+        [shape(total, full), shape(WIDE, total)],
         info,
         met,
         spaces=[pltpu.SMEM, pltpu.VMEM],
         out_spaces=[pltpu.HBM, pltpu.VMEM],
-        scratch=[pltpu.VMEM((ALONG, TIGHT, full), BF16), pltpu.SemaphoreType.DMA((ALONG,))],
+        scratch=[pltpu.VMEM((total, full), BF16), pltpu.SemaphoreType.DMA((-(-full // CHUNK),))],
         vmem=53 * MIB,
     )
-    gathered = traded(sorted_rows, far).reshape(total, full)
+    gathered = traded(sorted_rows.reshape(ALONG, TIGHT, full), far).reshape(total, full)
     gathered, gain_other = lax.optimization_barrier((gathered, gain_other))
     kept, sent = local(
         gate,
@@ -246,7 +237,13 @@
         in_gain,
         gate_own,
         gate_other,
-        scratch=[pltpu.VMEM((total, half_width), BF16), pltpu.VMEM((total, EXTRA), F32)],
+        spaces=[pltpu.VMEM] * 3 + [pl.ANY],
+        scratch=[
+            pltpu.VMEM((total, half_width), BF16),
+            pltpu.VMEM((total, EXTRA), F32),
+            pltpu.VMEM((half_width, cols), BF16),
+            pltpu.SemaphoreType.DMA,
+        ],
     )
     got = lax.ppermute(sent, "tp", swap)
     (parts,) = local(
@@ -261,9 +258,9 @@
     )
     returned = traded(parts.reshape(ALONG, TIGHT, half_width), far).reshape(total, half_width)
     (summed,) = local(gather_parts, [shape(WIDE, half_width)], far_back, returned)
-    home = traded(summed.reshape(ALONG, ROWS, half_width), near).reshape(WIDE, half_width)
+    home = traded(summed.reshape(ALONG, ROWS, half_width), near)
     layer_out, squares = local(
-        finish, [shape(ROWS, half_width), shape(ROWS, EXTRA, dtype=F32)], home_back, home, rows
+        finish, [shape(ROWS, half_width), shape(ROWS, EXTRA, dtype=F32)], home, rows
     )
     theirs = lax.ppermute(layer_out, "section", swap)
     far_squares = lax.ppermute(squares, ("section", "tp"), [(0, 3), (3, 0), (1, 2), (2, 1)])

time: 119 us -> 118 us (level)
  blocking collectives: 57.7 us -> 37.4 us
  starting transfers between devices: 28.2 us -> 38.5 us
  waiting for transfers between devices: 19.2 us -> 29.3 us
    all_to_all x3 -> x2, blocking collectives: 57.7 us -> 37.4 us  [traded(): lax.all_to_all(block, 'ep', 0, 0, axis_index_groups=groups, tiled=True)]
    all_to_all x1 -> x2, starting transfers between devices: 7.56 us -> 17.9 us  [traded(): lax.all_to_all(block, 'ep', 0, 0, axis_index_groups=groups, tiled=True)]
    all_to_all x1 -> x2, waiting for transfers between devices: 10 us -> 20.1 us  [traded(): lax.all_to_all(block, 'ep', 0, 0, axis_index_groups=groups, tiled=True)]
  transfers between devices with their start and end apart: 7 -> 8, of which waited for: 4 -> 5; matrix products, arithmetic and copies ran while one was open for 1% -> 1% of each run, Pallas kernels for 2% -> 3%
where the time goes in v4:
time: 118 us
  starting transfers between devices  38.5 us (33%)
  blocking collectives  37.4 us (32%)
  waiting for transfers between devices  29.3 us (25%)
  Pallas kernels  10 us (8%)
  other arithmetic  1.38 us (1%)
    all_to_all x2, blocking collectives, traded(): lax.all_to_all(block, 'ep', 0, 0, axis_index_groups=groups, tiled=True)  37.4 us
    all_to_all x2, waiting for transfers between devices, traded(): lax.all_to_all(block, 'ep', 0, 0, axis_index_groups=groups, tiled=True)  20.1 us
    all_to_all x2, starting transfers between devices, traded(): lax.all_to_all(block, 'ep', 0, 0, axis_index_groups=groups, tiled=True)  17.9 us
    pallas_call x7, Pallas kernels, local(): pl.pallas_call(kernel, out_shape=outs, in_specs=[pl.BlockSpec(memory_spac...  10 us
    ppermute x1, starting transfers between devices, body(): gain_other = lax.ppermute(out_gain, 'section', swap)  4.93 us
    ppermute x1, starting transfers between devices, body(): theirs = lax.ppermute(layer_out, 'section', swap)  4.9 us
    ppermute x1, waiting for transfers between devices, body(): lax.ppermute(squares, ('section', 'tp'), [(0, 3), (3, 0), (1, 2), (2, 1)])  3.62 us
    ppermute x1, starting transfers between devices, body(): got = lax.ppermute(sent, 'tp', swap)  3.4 us
  transfers between devices with their start and end apart: 8, of which 5 were waited for; matrix products, arithmetic and copies ran while one was open for 1% of the time, Pallas kernels for 3%

profile of v4, /device:TPU:8, one launch (start us, length us, event | category | flops | bytes accessed | tf_op | source)
XLA Modules:
  0.0 117.5 jit_solution(5360425731221700517)
XLA Ops:
  0.6 1.6 %shard_map.86 = bf16[8,4,3712]{2,1,0:T(4,128)(2,1)} custom-call(bf16[4,3584]{1,0:T(4,128)(2,1)} %bitcast.19, s32[4,4]{1,0:T(4,128)} %bitcast.25, f32[4,4]{1,0:T(4,128)} %bitcast.26), custom_call_target="tpu_custom_call" | custom-call | tf_op jit(solution)/shard_map/pallas_call | solution.py:175
  2.2 10.3 %all-to-all-start = ((bf16[8,4,3712]{2,1,0:T(4,128)(2,1)}), bf16[8,4,3712]{2,1,0:T(4,128)(2,1)S(1)}, u32[]{:S(2)}, u32[]{:S(2)}) async-start(bf16[8,4,3712]{2,1,0:T(4,128)(2,1)} %shard_map.86), calls=%async_computation | async-start | bytes 475136 | tf_op jit(solution)/shard_map/all_to_all | solution.py:32
  12.7 10.1 %all-to-all-done = bf16[8,4,3712]{2,1,0:T(4,128)(2,1)S(1)} async-done(((bf16[8,4,3712]{2,1,0:T(4,128)(2,1)}), bf16[8,4,3712]{2,1,0:T(4,128)(2,1)S(1)}, u32[]{:S(2)}, u32[]{:S(2)}) %all-to-all-start) | async-done | bytes 237600 | tf_op jit(solution)/shard_map/all_to_all | solution.py:32
  22.8 2.2 %shard_map.87 = (bf16[192,3712]{1,0:T(8,128)(2,1)}, bf16[32,192]{1,0:T(8,128)(2,1)S(1)}) custom-call(s32[2]{0:T(128)S(1)} %pad_add_fusion.info_ref, bf16[32,3712]{1,0:T(8,128)(2,1)S(1)} %reshape.22.rows_ref), custom_call_target="tpu_custom_call" | custom-call | tf_op jit(solution)/shard_map/pallas_call | solution.py:175
  25.0 7.6 %all-to-all-start.1 = ((bf16[8,24,3712]{2,1,0:T(8,128)(2,1)}), bf16[8,24,3712]{2,1,0:T(8,128)(2,1)S(1)}, u32[]{:S(2)}, u32[]{:S(2)}) async-start(bf16[8,24,3712]{2,1,0:T(8,128)(2,1)} %bitcast.21), calls=%async_computation.1 | async-start | bytes 2850816 | tf_op jit(solution)/shard_map/all_to_all | solution.py:32
  32.6 1.9 %collective-permute-start.1 = (bf16[3584,256]{1,0:T(8,128)(2,1)S(1)}, bf16[3584,256]{1,0:T(8,128)(2,1)}, u32[]{:S(2)}, u32[]{:S(2)}) collective-permute-start(bf16[3584,256]{1,0:T(8,128)(2,1)S(1)} %bitcast.17), channel_id=1, source_target_pairs={{0,2},{2,0},{4,6},{6,4},{8,10},{10,8},{12,14},{14,12},{16,18},{18,... | collective-permute-start | bytes 5505032 | tf_op jit(solution)/shard_map/ppermute | solution.py:205
  34.5 2.4 %collective-permute-start.3 = (bf16[128,3584]{1,0:T(8,128)(2,1)}, bf16[128,3584]{1,0:T(8,128)(2,1)}, u32[]{:S(2)}, u32[]{:S(2)}) collective-permute-start(bf16[128,3584]{1,0:T(8,128)(2,1)} %bitcast.22), channel_id=1, source_target_pairs={{0,2},{2,0},{4,6},{6,4},{8,10},{10,8},{12,14},{14,12},{16,18},{18,... | collective-permute-start | bytes 2752520 | tf_op jit(solution)/shard_map/ppermute | solution.py:206
  36.9 4.9 %collective-permute-start = (bf16[1,3584]{1,0:T(2,128)(2,1)S(1)}, bf16[1,3584]{1,0:T(2,128)(2,1)S(1)}, u32[]{:S(2)}, u32[]{:S(2)}) collective-permute-start(bf16[1,3584]{1,0:T(2,128)(2,1)S(1)} %copy-done.4), channel_id=1, source_target_pairs={{0,256},{256,0},{1,257},{257,1},{2,258},{258,2},{3,259},{259,3},{4... | collective-permute-start | bytes 21512 | tf_op jit(solution)/shard_map/ppermute | solution.py:207
  41.8 2.2 %collective-permute-done.gain_ref = bf16[1,3584]{1,0:T(2,128)(2,1)S(1)} collective-permute-done((bf16[1,3584]{1,0:T(2,128)(2,1)S(1)}, bf16[1,3584]{1,0:T(2,128)(2,1)S(1)}, u32[]{:S(2)}, u32[]{:S(2)}) %collective-permute-start) | collective-permute-done | bytes 7200 | tf_op jit(solution)/shard_map/ppermute | solution.py:207
  44.0 10.0 %all-to-all-done.1 = bf16[8,24,3712]{2,1,0:T(8,128)(2,1)S(1)} async-done(((bf16[8,24,3712]{2,1,0:T(8,128)(2,1)}), bf16[8,24,3712]{2,1,0:T(8,128)(2,1)S(1)}, u32[]{:S(2)}, u32[]{:S(2)}) %all-to-all-start.1) | async-done | bytes 1425440 | tf_op jit(solution)/shard_map/all_to_all | solution.py:32
  54.1 3.1 %shard_map.88 = (f32[192,640]{1,0:T(8,128)S(1)}, bf16[192,640]{1,0:T(8,128)(2,1)S(1)}) custom-call(bf16[192,3712]{1,0:T(8,128)(2,1)S(1)} %bitcast.13, bf16[1,3584]{1,0:T(2,128)(2,1)S(1)} %copy-done.2, bf16[3584,256]{1,0:T(8,128)(2,1)S(1)} %bitcast.18, bf16[3584,256]{1,0:T(8,128)(2,1)} %collective-permute-done.1.other_hbm), custom_call_target="tpu_custom_call" | custom-call | tf_op jit(solution)/shard_map/pallas_call | solution.py:175
  57.2 3.4 %collective-permute-start.2 = (bf16[192,640]{1,0:T(8,128)(2,1)S(1)}, bf16[192,640]{1,0:T(8,128)(2,1)S(1)}, u32[]{:S(2)}, u32[]{:S(2)}) collective-permute-start(bf16[192,640]{1,0:T(8,128)(2,1)S(1)} %get-tuple-element.14), channel_id=1, source_target_pairs={{0,1},{1,0},{2,3},{3,2},{4,5},{5,4},{6,7},{7,6},{8,9},{9,8},{10,11... | collective-permute-start | bytes 737288 | tf_op jit(solution)/shard_map/ppermute | solution.py:248
  60.6 1.3 %pad_maximum_fusion.down_ref = bf16[256,3584]{1,0:T(8,128)(2,1)S(1)} fusion(bf16[128,3584]{1,0:T(8,128)(2,1)} %collective-permute-done.3, bf16[128,3584]{1,0:T(8,128)(2,1)S(1)} %bitcast.23), kind=kLoop, calls=%fused_computation | loop fusion | flops 3670016 | bytes 3670016 | tf_op jit(solution)/shard_map/concatenate | solution.py:209
  61.9 3.4 %collective-permute-done.2.got_ref = bf16[192,640]{1,0:T(8,128)(2,1)S(1)} collective-permute-done((bf16[192,640]{1,0:T(8,128)(2,1)S(1)}, bf16[192,640]{1,0:T(8,128)(2,1)S(1)}, u32[]{:S(2)}, u32[]{:S(2)}) %collective-permute-start.2) | collective-permute-done | bytes 245792 | tf_op jit(solution)/shard_map/ppermute | solution.py:248
  65.3 1.3 %shard_map.89 = bf16[192,3584]{1,0:T(8,128)(2,1)S(1)} custom-call(s32[2]{0:T(128)S(1)} %pad_add_fusion.info_ref, bf16[192,3712]{1,0:T(8,128)(2,1)S(1)} %bitcast.14, f32[192,640]{1,0:T(8,128)S(1)} %get-tuple-element.13.kept_ref, bf16[192,640]{1,0:T(8,128)(2,1)S(1)} %collective-permute-done.2.got_ref, bf16[256,3584]{1,0:T(8,128)(2,1)S(1)} %pad_maximum_fusion.down_ref), custom_call_target="tpu_custom_call" | custom-call | tf_op jit(solution)/shard_map/pallas_call | solution.py:175
  66.6 24.9 %all_to_all.20 = bf16[8,24,3584]{2,1,0:T(8,128)(2,1)S(1)} all-to-all(bf16[8,24,3584]{2,1,0:T(8,128)(2,1)S(1)} %bitcast.15), channel_id=1, replica_groups={{2,6,10,14,18,22,26,30},{34,38,42,46,50,54,58,62},{66,70,74,78,82,86,90..., dimensions={0} | all-to-all | bytes 2752512 | tf_op jit(solution)/shard_map/all_to_all | solution.py:32
  91.5 0.3 shard_map.90
  91.9 0.1 reshape.27
  91.9 12.5 %all_to_all.21.parts_ref = bf16[8,4,3584]{2,1,0:T(4,128)(2,1)S(1)} all-to-all(bf16[8,4,3584]{2,1,0:T(4,128)(2,1)S(1)} %reshape.27), channel_id=1, replica_groups={{0,4,8,12,16,20,24,28},{32,36,40,44,48,52,56,60},{64,68,72,76,80,84,88,..., dimensions={0} | all-to-all | bytes 458752 | tf_op jit(solution)/shard_map/all_to_all | solution.py:32
  104.5 0.7 shard_map.91
  105.1 4.9 %collective-permute-start.4 = (bf16[4,3584]{1,0:T(4,128)(2,1)}, bf16[4,3584]{1,0:T(4,128)(2,1)S(1)}, u32[]{:S(2)}, u32[]{:S(2)}) collective-permute-start(bf16[4,3584]{1,0:T(4,128)(2,1)} %get-tuple-element.15), channel_id=1, source_target_pairs={{0,256},{256,0},{1,257},{257,1},{2,258},{258,2},{3,259},{259,3},{4... | collective-permute-start | bytes 86024 | tf_op jit(solution)/shard_map/ppermute | solution.py:265
  110.0 3.1 %collective-permute-start.5 = (f32[4,128]{1,0:T(4,128)S(1)}, f32[4,128]{1,0:T(4,128)S(1)}, u32[]{:S(2)}, u32[]{:S(2)}) collective-permute-start(f32[4,128]{1,0:T(4,128)S(1)} %get-tuple-element.16), channel_id=1, source_target_pairs={{0,257},{257,0},{1,256},{256,1},{2,259},{259,2},{3,258},{258,3},{4... | collective-permute-start | bytes 6152 | tf_op jit(solution)/shard_map/ppermute | solution.py:266
  113.1 3.6 %collective-permute-done.5.far_ref = f32[4,128]{1,0:T(4,128)S(1)} collective-permute-done((f32[4,128]{1,0:T(4,128)S(1)}, f32[4,128]{1,0:T(4,128)S(1)}, u32[]{:S(2)}, u32[]{:S(2)}) %collective-permute-start.5) | collective-permute-done | bytes 2080 | tf_op jit(solution)/shard_map/ppermute | solution.py:266
  116.7 0.8 shard_map.92
  (15 shorter events, 0.2 us)
Async XLA Ops:
  2.2 20.5 %all-to-all-start = ((bf16[8,4,3712]{2,1,0:T(4,128)(2,1)}), bf16[8,4,3712]{2,1,0:T(4,128)(2,1)S(1)}, u32[]{:S(2)}, u32[]{:S(2)}) async-start(bf16[8,4,3712]{2,1,0:T(4,128)(2,1)} %shard_map.86), calls=%async_computation | async-start | bytes 475136 | tf_op jit(solution)/shard_map/all_to_all | solution.py:32
  12.5 20.0 %copy-start = (bf16[1,1,3584,256]{3,2,1,0:T(8,128)(2,1)S(1)}, bf16[1,1,3584,256]{3,2,1,0:T(8,128)(2,1)}, u32[]{:S(2)}) copy-start(bf16[1,1,3584,256]{3,2,1,0:T(8,128)(2,1)} %param.11) | copy-start | bytes 5505028
  12.5 24.4 %copy-start.4 = (bf16[1,3584]{1,0:T(2,128)(2,1)S(1)}, bf16[1,3584]{1,0:T(2,128)(2,1)}, u32[]{:S(2)}) copy-start(bf16[1,3584]{1,0:T(2,128)(2,1)} %param.13) | copy-start | bytes 21508
  12.6 41.5 %copy-start.2 = (bf16[1,3584]{1,0:T(2,128)(2,1)S(1)}, bf16[1,3584]{1,0:T(2,128)(2,1)}, u32[]{:S(2)}) copy-start(bf16[1,3584]{1,0:T(2,128)(2,1)} %gain_ref.1) | copy-start | bytes 21508
  25.0 29.1 %all-to-all-start.1 = ((bf16[8,24,3712]{2,1,0:T(8,128)(2,1)}), bf16[8,24,3712]{2,1,0:T(8,128)(2,1)S(1)}, u32[]{:S(2)}, u32[]{:S(2)}) async-start(bf16[8,24,3712]{2,1,0:T(8,128)(2,1)} %bitcast.21), calls=%async_computation.1 | async-start | bytes 2850816 | tf_op jit(solution)/shard_map/all_to_all | solution.py:32
  32.6 21.5 %collective-permute-start.1 = (bf16[3584,256]{1,0:T(8,128)(2,1)S(1)}, bf16[3584,256]{1,0:T(8,128)(2,1)}, u32[]{:S(2)}, u32[]{:S(2)}) collective-permute-start(bf16[3584,256]{1,0:T(8,128)(2,1)S(1)} %bitcast.17), channel_id=1, source_target_pairs={{0,2},{2,0},{4,6},{6,4},{8,10},{10,8},{12,14},{14,12},{16,18},{18,... | collective-permute-start | bytes 5505032 | tf_op jit(solution)/shard_map/ppermute | solution.py:205
  34.5 26.1 %collective-permute-start.3 = (bf16[128,3584]{1,0:T(8,128)(2,1)}, bf16[128,3584]{1,0:T(8,128)(2,1)}, u32[]{:S(2)}, u32[]{:S(2)}) collective-permute-start(bf16[128,3584]{1,0:T(8,128)(2,1)} %bitcast.22), channel_id=1, source_target_pairs={{0,2},{2,0},{4,6},{6,4},{8,10},{10,8},{12,14},{14,12},{16,18},{18,... | collective-permute-start | bytes 2752520 | tf_op jit(solution)/shard_map/ppermute | solution.py:206
  36.9 7.1 %collective-permute-start = (bf16[1,3584]{1,0:T(2,128)(2,1)S(1)}, bf16[1,3584]{1,0:T(2,128)(2,1)S(1)}, u32[]{:S(2)}, u32[]{:S(2)}) collective-permute-start(bf16[1,3584]{1,0:T(2,128)(2,1)S(1)} %copy-done.4), channel_id=1, source_target_pairs={{0,256},{256,0},{1,257},{257,1},{2,258},{258,2},{3,259},{259,3},{4... | collective-permute-start | bytes 21512 | tf_op jit(solution)/shard_map/ppermute | solution.py:207
  54.0 6.6 %copy-start.3 = (bf16[1,1,128,3584]{3,2,1,0:T(8,128)(2,1)S(1)}, bf16[1,1,128,3584]{3,2,1,0:T(8,128)(2,1)}, u32[]{:S(2)}) copy-start(bf16[1,1,128,3584]{3,2,1,0:T(8,128)(2,1)} %param.12) | copy-start | bytes 2752516
  57.2 8.1 %collective-permute-start.2 = (bf16[192,640]{1,0:T(8,128)(2,1)S(1)}, bf16[192,640]{1,0:T(8,128)(2,1)S(1)}, u32[]{:S(2)}, u32[]{:S(2)}) collective-permute-start(bf16[192,640]{1,0:T(8,128)(2,1)S(1)} %get-tuple-element.14), channel_id=1, source_target_pairs={{0,1},{1,0},{2,3},{3,2},{4,5},{5,4},{6,7},{7,6},{8,9},{9,8},{10,11... | collective-permute-start | bytes 737288 | tf_op jit(solution)/shard_map/ppermute | solution.py:248
  91.5 13.0 %copy-start.1 = (bf16[1,4,3584]{2,1,0:T(4,128)(2,1)S(1)}, bf16[1,4,3584]{2,1,0:T(4,128)(2,1)}, u32[]{:S(2)}) copy-start(bf16[1,4,3584]{2,1,0:T(4,128)(2,1)} %param.7) | copy-start | bytes 86020
  105.1 11.6 %collective-permute-start.4 = (bf16[4,3584]{1,0:T(4,128)(2,1)}, bf16[4,3584]{1,0:T(4,128)(2,1)S(1)}, u32[]{:S(2)}, u32[]{:S(2)}) collective-permute-start(bf16[4,3584]{1,0:T(4,128)(2,1)} %get-tuple-element.15), channel_id=1, source_target_pairs={{0,256},{256,0},{1,257},{257,1},{2,258},{258,2},{3,259},{259,3},{4... | collective-permute-start | bytes 86024 | tf_op jit(solution)/shard_map/ppermute | solution.py:265
  110.0 6.7 %collective-permute-start.5 = (f32[4,128]{1,0:T(4,128)S(1)}, f32[4,128]{1,0:T(4,128)S(1)}, u32[]{:S(2)}, u32[]{:S(2)}) collective-permute-start(f32[4,128]{1,0:T(4,128)S(1)} %get-tuple-element.16), channel_id=1, source_target_pairs={{0,257},{257,0},{1,256},{256,1},{2,259},{259,2},{3,258},{258,3},{4... | collective-permute-start | bytes 6152 | tf_op jit(solution)/shard_map/ppermute | solution.py:266

commit v5 on v4

--- a/solution.py
+++ b/solution.py
@@ -95,25 +95,19 @@
         copy.wait()
 
 
-def gate(
-    rows_ref, gain_ref, own_ref, other_hbm, kept_ref, sent_ref, scaled, squares, other_ref, sem
-):
+def gate(rows_ref, gain_ref, own_ref, other_ref, kept_ref, sent_ref, squares):
     half_width, cols = own_ref.shape
-    copy = pltpu.make_async_copy(other_hbm, other_ref, sem)
-    copy.start()
-    deep = half_width // 4
-    for k in range(4):
+    deep = half_width // 7
+    for k in range(7):
         at = slice(k * deep, (k + 1) * deep)
         values = rows_ref[:, at].astype(F32)
         part = jnp.sum(values * values, axis=1, keepdims=True)
         squares[...] = jnp.broadcast_to(part, squares.shape) + (squares[...] if k else 0.0)
-        scaled[:, at] = (values * gain_ref[:, at].astype(F32)).astype(BF16)
-    for at, weights in ((0, own_ref), (cols, other_ref)):
-        if at:
-            copy.wait()
-        sums = jnp.dot(scaled[...], weights[...], preferred_element_type=F32)
-        kept_ref[:, at : at + cols] = sums
-        sent_ref[:, at : at + cols] = sums.astype(BF16)
+        scaled = (values * gain_ref[:, at].astype(F32)).astype(BF16)
+        for lo, weights in ((0, own_ref), (cols, other_ref)):
+            sums = jnp.dot(scaled, weights[at, :], preferred_element_type=F32)
+            kept_ref[:, lo : lo + cols] = sums + (kept_ref[:, lo : lo + cols] if k else 0.0)
+    sent_ref[:, : 2 * cols] = kept_ref[:, : 2 * cols].astype(BF16)
     total = squares[...]
     high = total.astype(BF16).astype(F32)
     lane = lax.broadcasted_iota(jnp.int32, total.shape, 1)
@@ -150,21 +144,28 @@
     out_ref[...] = jnp.dot(back_ref[...], parts_ref[...], preferred_element_type=F32).astype(BF16)
 
 
-def finish(parts_ref, rows_ref, out_ref, squares_ref):
+def finish(parts_ref, rows_ref, out_ref, sent_ref):
+    half_width = rows_ref.shape[1]
     mixture = parts_ref[0].astype(F32)
     for t in range(1, ALONG):
         mixture += parts_ref[t].astype(F32)
     layer = (rows_ref[...].astype(F32) + mixture).astype(BF16)
     out_ref[...] = layer
     values = layer.astype(F32)
-    squares_ref[...] = jnp.broadcast_to(
-        jnp.sum(values * values, axis=1, keepdims=True), squares_ref.shape
-    )
-
-
-def close(width, theirs_ref, far_ref, gain_ref, out_ref):
-    values = theirs_ref[...].astype(F32)
-    total = jnp.sum(values * values, axis=1, keepdims=True) + far_ref[:, :1]
+    total = jnp.sum(values * values, axis=1, keepdims=True)
+    high = total.astype(BF16).astype(F32)
+    lane = lax.broadcasted_iota(jnp.int32, (ROWS, EXTRA), 1)
+    pieces = jnp.where(lane == 0, high, jnp.where(lane == 1, total - high, 0.0)).astype(BF16)
+    for to in range(sent_ref.shape[0]):
+        sent_ref[to, :, :half_width] = layer
+        sent_ref[to, :, half_width:] = pieces
+
+
+def close(width, info_ref, got_ref, gain_ref, out_ref):
+    half_width = gain_ref.shape[1]
+    values = got_ref[info_ref[2], :, :half_width].astype(F32)
+    far = got_ref[info_ref[3], :, half_width:].astype(F32)
+    total = jnp.sum(values * values, axis=1, keepdims=True) + jnp.sum(far, axis=1, keepdims=True)
     scale = lax.rsqrt(total * (1.0 / width) + 1e-06)
     out_ref[...] = (values * scale * gain_ref[...].astype(F32)).astype(BF16)
 
@@ -195,7 +196,10 @@
     cols = gate_up.shape[3]
     near, far = crossed_groups(ep, 0), crossed_groups(ep, 1)
     place = lax.axis_index("ep")
-    info = jnp.stack([place % 2, place // SPAN]).astype(jnp.int32)
+    crossed, side = 1 - lax.axis_index("section"), lax.axis_index("tp")
+    info = jnp.stack(
+        [place % 2, place // SPAN, crossed * 2 + side, crossed * 2 + 1 - side]
+    ).astype(jnp.int32)
     other_core = [(i, i ^ 1) for i in range(ep)]
     swap = [(0, 1), (1, 0)]
     full = half_width + EXTRA
@@ -237,13 +241,7 @@
         in_gain,
         gate_own,
         gate_other,
-        spaces=[pltpu.VMEM] * 3 + [pl.ANY],
-        scratch=[
-            pltpu.VMEM((total, half_width), BF16),
-            pltpu.VMEM((total, EXTRA), F32),
-            pltpu.VMEM((half_width, cols), BF16),
-            pltpu.SemaphoreType.DMA,
-        ],
+        scratch=[pltpu.VMEM((total, EXTRA), F32)],
     )
     got = lax.ppermute(sent, "tp", swap)
     (parts,) = local(
@@ -259,13 +257,17 @@
     returned = traded(parts.reshape(ALONG, TIGHT, half_width), far).reshape(total, half_width)
     (summed,) = local(gather_parts, [shape(WIDE, half_width)], far_back, returned)
     home = traded(summed.reshape(ALONG, ROWS, half_width), near)
-    layer_out, squares = local(
-        finish, [shape(ROWS, half_width), shape(ROWS, EXTRA, dtype=F32)], home, rows
-    )
-    theirs = lax.ppermute(layer_out, "section", swap)
-    far_squares = lax.ppermute(squares, ("section", "tp"), [(0, 3), (3, 0), (1, 2), (2, 1)])
+    layer_out, leaving = local(
+        finish, [shape(ROWS, half_width), shape(4, ROWS, full)], home, rows
+    )
+    got = lax.all_to_all(leaving, ("section", "tp"), 0, 0, tiled=True)
     (handed,) = local(
-        functools.partial(close, width), [shape(ROWS, half_width)], theirs, far_squares, gain_other
+        functools.partial(close, width),
+        [shape(ROWS, half_width)],
+        info,
+        got,
+        gain_other,
+        spaces=[pltpu.SMEM] + [pltpu.VMEM] * 2,
     )
     return (layer_out[None], handed[None])
 

time: 118 us -> 117 us (level)
  the two profiles are of different devices: /device:TPU:8 before, /device:TPU:2 now
where the time goes in v5:
time: 117 us; the launch traced here: 116 us
  blocking collectives  46.4 us (40%)
  waiting for transfers between devices  29 us (25%)
  starting transfers between devices  28.2 us (24%)
  Pallas kernels  9.95 us (9%)
  other arithmetic  1.38 us (1%)
    all_to_all x2, blocking collectives, traded(): lax.all_to_all(block, 'ep', 0, 0, axis_index_groups=groups, tiled=True)  37.3 us
    all_to_all x2, waiting for transfers between devices, traded(): lax.all_to_all(block, 'ep', 0, 0, axis_index_groups=groups, tiled=True)  21.6 us
    all_to_all x2, starting transfers between devices, traded(): lax.all_to_all(block, 'ep', 0, 0, axis_index_groups=groups, tiled=True)  17.4 us
    pallas_call x7, Pallas kernels, local(): pl.pallas_call(kernel, out_shape=outs, in_specs=[pl.BlockSpec(memory_spac...  9.95 us
    all_to_all x1, blocking collectives, body(): got = lax.all_to_all(leaving, ('section', 'tp'), 0, 0, tiled=True)  9.07 us
    ppermute x1, waiting for transfers between devices, body(): got = lax.ppermute(sent, 'tp', swap)  4.32 us
    ppermute x1, starting transfers between devices, body(): gain_other = lax.ppermute(out_gain, 'section', swap)  4.04 us
    ppermute x1, waiting for transfers between devices, body(): gain_other = lax.ppermute(out_gain, 'section', swap)  3.07 us
  transfers between devices with their start and end apart: 6, of which 4 were waited for; matrix products, arithmetic and copies ran while one was open for 1% of the time, Pallas kernels for 2%

profile of v5, /device:TPU:2, one launch (start us, length us, event | category | flops | bytes accessed | tf_op | source)
XLA Modules:
  0.0 115.9 jit_solution(744161615208957642)
XLA Ops:
  0.6 1.6 %shard_map.86 = bf16[8,4,3712]{2,1,0:T(4,128)(2,1)} custom-call(bf16[4,3584]{1,0:T(4,128)(2,1)} %bitcast.21, s32[4,4]{1,0:T(4,128)} %bitcast.27, f32[4,4]{1,0:T(4,128)} %bitcast.28), custom_call_target="tpu_custom_call" | custom-call | tf_op jit(solution)/shard_map/pallas_call | solution.py:176
  2.2 10.3 %all-to-all-start = ((bf16[8,4,3712]{2,1,0:T(4,128)(2,1)}), bf16[8,4,3712]{2,1,0:T(4,128)(2,1)S(1)}, u32[]{:S(2)}, u32[]{:S(2)}) async-start(bf16[8,4,3712]{2,1,0:T(4,128)(2,1)} %shard_map.86), calls=%async_computation | async-start | bytes 475136 | tf_op jit(solution)/shard_map/all_to_all | solution.py:32
  12.6 0.1 pad_add_fusion.info_ref
  12.7 10.1 %all-to-all-done = bf16[8,4,3712]{2,1,0:T(4,128)(2,1)S(1)} async-done(((bf16[8,4,3712]{2,1,0:T(4,128)(2,1)}), bf16[8,4,3712]{2,1,0:T(4,128)(2,1)S(1)}, u32[]{:S(2)}, u32[]{:S(2)}) %all-to-all-start) | async-done | bytes 237600 | tf_op jit(solution)/shard_map/all_to_all | solution.py:32
  22.8 0.1 reshape.22.rows_ref
  22.8 2.2 %shard_map.87 = (bf16[192,3712]{1,0:T(8,128)(2,1)}, bf16[32,192]{1,0:T(8,128)(2,1)S(1)}) custom-call(s32[4]{0:T(128)S(1)} %pad_add_fusion.info_ref, bf16[32,3712]{1,0:T(8,128)(2,1)S(1)} %reshape.22.rows_ref), custom_call_target="tpu_custom_call" | custom-call | tf_op jit(solution)/shard_map/pallas_call | solution.py:176
  25.0 7.1 %all-to-all-start.1 = ((bf16[8,24,3712]{2,1,0:T(8,128)(2,1)}), bf16[8,24,3712]{2,1,0:T(8,128)(2,1)S(1)}, u32[]{:S(2)}, u32[]{:S(2)}) async-start(bf16[8,24,3712]{2,1,0:T(8,128)(2,1)} %bitcast.23), calls=%async_computation.1 | async-start | bytes 2850816 | tf_op jit(solution)/shard_map/all_to_all | solution.py:32
  32.1 1.9 %collective-permute-start.1 = (bf16[3584,256]{1,0:T(8,128)(2,1)S(1)}, bf16[3584,256]{1,0:T(8,128)(2,1)}, u32[]{:S(2)}, u32[]{:S(2)}) collective-permute-start(bf16[3584,256]{1,0:T(8,128)(2,1)S(1)} %bitcast.19), channel_id=1, source_target_pairs={{0,2},{2,0},{4,6},{6,4},{8,10},{10,8},{12,14},{14,12},{16,18},{18,... | collective-permute-start | bytes 5505032 | tf_op jit(solution)/shard_map/ppermute | solution.py:209
  34.1 2.4 %collective-permute-start.3 = (bf16[128,3584]{1,0:T(8,128)(2,1)}, bf16[128,3584]{1,0:T(8,128)(2,1)}, u32[]{:S(2)}, u32[]{:S(2)}) collective-permute-start(bf16[128,3584]{1,0:T(8,128)(2,1)} %bitcast.24), channel_id=1, source_target_pairs={{0,2},{2,0},{4,6},{6,4},{8,10},{10,8},{12,14},{14,12},{16,18},{18,... | collective-permute-start | bytes 2752520 | tf_op jit(solution)/shard_map/ppermute | solution.py:210
  36.5 4.0 %collective-permute-start = (bf16[1,3584]{1,0:T(2,128)(2,1)S(1)}, bf16[1,3584]{1,0:T(2,128)(2,1)S(1)}, u32[]{:S(2)}, u32[]{:S(2)}) collective-permute-start(bf16[1,3584]{1,0:T(2,128)(2,1)S(1)} %copy-done.4), channel_id=1, source_target_pairs={{0,256},{256,0},{1,257},{257,1},{2,258},{258,2},{3,259},{259,3},{4... | collective-permute-start | bytes 21512 | tf_op jit(solution)/shard_map/ppermute | solution.py:211
  40.5 3.1 %collective-permute-done.gain_ref = bf16[1,3584]{1,0:T(2,128)(2,1)S(1)} collective-permute-done((bf16[1,3584]{1,0:T(2,128)(2,1)S(1)}, bf16[1,3584]{1,0:T(2,128)(2,1)S(1)}, u32[]{:S(2)}, u32[]{:S(2)}) %collective-permute-start) | collective-permute-done | bytes 7200 | tf_op jit(solution)/shard_map/ppermute | solution.py:211
  43.6 11.5 %all-to-all-done.1 = bf16[8,24,3712]{2,1,0:T(8,128)(2,1)S(1)} async-done(((bf16[8,24,3712]{2,1,0:T(8,128)(2,1)}), bf16[8,24,3712]{2,1,0:T(8,128)(2,1)S(1)}, u32[]{:S(2)}, u32[]{:S(2)}) %all-to-all-start.1) | async-done | bytes 1425440 | tf_op jit(solution)/shard_map/all_to_all | solution.py:32
  55.1 2.6 %shard_map.88 = (f32[192,640]{1,0:T(8,128)S(1)}, bf16[192,640]{1,0:T(8,128)(2,1)S(1)}) custom-call(bf16[192,3712]{1,0:T(8,128)(2,1)S(1)} %bitcast.15, bf16[1,3584]{1,0:T(2,128)(2,1)S(1)} %copy-done.2, bf16[3584,256]{1,0:T(8,128)(2,1)S(1)} %bitcast.20, bf16[3584,256]{1,0:T(8,128)(2,1)} %collective-permute-done.1.other_ref), custom_call_target="tpu_custom_call" | custom-call | tf_op jit(solution)/shard_map/pallas_call | solution.py:176
  57.7 2.4 %collective-permute-start.2 = (bf16[192,640]{1,0:T(8,128)(2,1)S(1)}, bf16[192,640]{1,0:T(8,128)(2,1)S(1)}, u32[]{:S(2)}, u32[]{:S(2)}) collective-permute-start(bf16[192,640]{1,0:T(8,128)(2,1)S(1)} %get-tuple-element.14), channel_id=1, source_target_pairs={{0,1},{1,0},{2,3},{3,2},{4,5},{5,4},{6,7},{7,6},{8,9},{9,8},{10,11... | collective-permute-start | bytes 737288 | tf_op jit(solution)/shard_map/ppermute | solution.py:246
  60.2 1.3 %pad_maximum_fusion.down_ref = bf16[256,3584]{1,0:T(8,128)(2,1)S(1)} fusion(bf16[128,3584]{1,0:T(8,128)(2,1)} %collective-permute-done.3, bf16[128,3584]{1,0:T(8,128)(2,1)S(1)} %bitcast.25), kind=kLoop, calls=%fused_computation | loop fusion | flops 3670016 | bytes 3670016 | tf_op jit(solution)/shard_map/concatenate | solution.py:213
  61.5 4.3 %collective-permute-done.2.got_ref = bf16[192,640]{1,0:T(8,128)(2,1)S(1)} collective-permute-done((bf16[192,640]{1,0:T(8,128)(2,1)S(1)}, bf16[192,640]{1,0:T(8,128)(2,1)S(1)}, u32[]{:S(2)}, u32[]{:S(2)}) %collective-permute-start.2) | collective-permute-done | bytes 245792 | tf_op jit(solution)/shard_map/ppermute | solution.py:246
  65.8 1.3 %shard_map.89 = bf16[192,3584]{1,0:T(8,128)(2,1)S(1)} custom-call(s32[4]{0:T(128)S(1)} %pad_add_fusion.info_ref, bf16[192,3712]{1,0:T(8,128)(2,1)S(1)} %bitcast.16, f32[192,640]{1,0:T(8,128)S(1)} %get-tuple-element.13.kept_ref, bf16[192,640]{1,0:T(8,128)(2,1)S(1)} %collective-permute-done.2.got_ref, bf16[256,3584]{1,0:T(8,128)(2,1)S(1)} %pad_maximum_fusion.down_ref), custom_call_target="tpu_custom_call" | custom-call | tf_op jit(solution)/shard_map/pallas_call | solution.py:176
  67.1 24.8 %all_to_all.25 = bf16[8,24,3584]{2,1,0:T(8,128)(2,1)S(1)} all-to-all(bf16[8,24,3584]{2,1,0:T(8,128)(2,1)S(1)} %bitcast.17), channel_id=1, replica_groups={{2,6,10,14,18,22,26,30},{34,38,42,46,50,54,58,62},{66,70,74,78,82,86,90..., dimensions={0} | all-to-all | bytes 2752512 | tf_op jit(solution)/shard_map/all_to_all | solution.py:32
  91.9 0.3 shard_map.90
  92.3 0.1 reshape.27
  92.4 12.5 %all_to_all.26.parts_ref = bf16[8,4,3584]{2,1,0:T(4,128)(2,1)S(1)} all-to-all(bf16[8,4,3584]{2,1,0:T(4,128)(2,1)S(1)} %reshape.27), channel_id=1, replica_groups={{0,4,8,12,16,20,24,28},{32,36,40,44,48,52,56,60},{64,68,72,76,80,84,88,..., dimensions={0} | all-to-all | bytes 458752 | tf_op jit(solution)/shard_map/all_to_all | solution.py:32
  104.9 0.7 shard_map.91
  105.6 9.1 %all_to_all.27.got_ref = bf16[4,4,3712]{2,1,0:T(4,128)(2,1)S(1)} all-to-all(bf16[4,4,3712]{2,1,0:T(4,128)(2,1)S(1)} %get-tuple-element.16), channel_id=1, replica_groups=mesh['section'=2,'ep'=128,'tp'=2] {'section','tp'}, dimensions={0} | all-to-all | bytes 237568 | tf_op jit(solution)/shard_map/all_to_all | solution.py:263
  114.6 1.3 %shard_map.92 = bf16[4,3584]{1,0:T(4,128)(2,1)} custom-call(s32[4]{0:T(128)S(1)} %pad_add_fusion.info_ref, bf16[4,4,3712]{2,1,0:T(4,128)(2,1)S(1)} %all_to_all.27.got_ref, bf16[1,3584]{1,0:T(2,128)(2,1)S(1)} %collective-permute-done.gain_ref), custom_call_target="tpu_custom_call" | custom-call | tf_op jit(solution)/shard_map/pallas_call | solution.py:176
  (12 shorter events, 0.0 us)
Async XLA Ops:
  2.2 20.5 %all-to-all-start = ((bf16[8,4,3712]{2,1,0:T(4,128)(2,1)}), bf16[8,4,3712]{2,1,0:T(4,128)(2,1)S(1)}, u32[]{:S(2)}, u32[]{:S(2)}) async-start(bf16[8,4,3712]{2,1,0:T(4,128)(2,1)} %shard_map.86), calls=%async_computation | async-start | bytes 475136 | tf_op jit(solution)/shard_map/all_to_all | solution.py:32
  12.5 19.6 %copy-start = (bf16[1,1,3584,256]{3,2,1,0:T(8,128)(2,1)S(1)}, bf16[1,1,3584,256]{3,2,1,0:T(8,128)(2,1)}, u32[]{:S(2)}) copy-start(bf16[1,1,3584,256]{3,2,1,0:T(8,128)(2,1)} %param.11) | copy-start | bytes 5505028
  12.5 23.9 %copy-start.4 = (bf16[1,3584]{1,0:T(2,128)(2,1)S(1)}, bf16[1,3584]{1,0:T(2,128)(2,1)}, u32[]{:S(2)}) copy-start(bf16[1,3584]{1,0:T(2,128)(2,1)} %param.13) | copy-start | bytes 21508
  12.6 42.6 %copy-start.2 = (bf16[1,3584]{1,0:T(2,128)(2,1)S(1)}, bf16[1,3584]{1,0:T(2,128)(2,1)}, u32[]{:S(2)}) copy-start(bf16[1,3584]{1,0:T(2,128)(2,1)} %gain_ref.1) | copy-start | bytes 21508
  25.0 30.1 %all-to-all-start.1 = ((bf16[8,24,3712]{2,1,0:T(8,128)(2,1)}), bf16[8,24,3712]{2,1,0:T(8,128)(2,1)S(1)}, u32[]{:S(2)}, u32[]{:S(2)}) async-start(bf16[8,24,3712]{2,1,0:T(8,128)(2,1)} %bitcast.23), calls=%async_computation.1 | async-start | bytes 2850816 | tf_op jit(solution)/shard_map/all_to_all | solution.py:32
  32.1 23.0 %collective-permute-start.1 = (bf16[3584,256]{1,0:T(8,128)(2,1)S(1)}, bf16[3584,256]{1,0:T(8,128)(2,1)}, u32[]{:S(2)}, u32[]{:S(2)}) collective-permute-start(bf16[3584,256]{1,0:T(8,128)(2,1)S(1)} %bitcast.19), channel_id=1, source_target_pairs={{0,2},{2,0},{4,6},{6,4},{8,10},{10,8},{12,14},{14,12},{16,18},{18,... | collective-permute-start | bytes 5505032 | tf_op jit(solution)/shard_map/ppermute | solution.py:209
  34.1 26.1 %collective-permute-start.3 = (bf16[128,3584]{1,0:T(8,128)(2,1)}, bf16[128,3584]{1,0:T(8,128)(2,1)}, u32[]{:S(2)}, u32[]{:S(2)}) collective-permute-start(bf16[128,3584]{1,0:T(8,128)(2,1)} %bitcast.24), channel_id=1, source_target_pairs={{0,2},{2,0},{4,6},{6,4},{8,10},{10,8},{12,14},{14,12},{16,18},{18,... | collective-permute-start | bytes 2752520 | tf_op jit(solution)/shard_map/ppermute | solution.py:210
  36.5 7.1 %collective-permute-start = (bf16[1,3584]{1,0:T(2,128)(2,1)S(1)}, bf16[1,3584]{1,0:T(2,128)(2,1)S(1)}, u32[]{:S(2)}, u32[]{:S(2)}) collective-permute-start(bf16[1,3584]{1,0:T(2,128)(2,1)S(1)} %copy-done.4), channel_id=1, source_target_pairs={{0,256},{256,0},{1,257},{257,1},{2,258},{258,2},{3,259},{259,3},{4... | collective-permute-start | bytes 21512 | tf_op jit(solution)/shard_map/ppermute | solution.py:211
  55.1 5.0 %copy-start.3 = (bf16[1,1,128,3584]{3,2,1,0:T(8,128)(2,1)S(1)}, bf16[1,1,128,3584]{3,2,1,0:T(8,128)(2,1)}, u32[]{:S(2)}) copy-start(bf16[1,1,128,3584]{3,2,1,0:T(8,128)(2,1)} %param.12) | copy-start | bytes 2752516
  57.7 8.1 %collective-permute-start.2 = (bf16[192,640]{1,0:T(8,128)(2,1)S(1)}, bf16[192,640]{1,0:T(8,128)(2,1)S(1)}, u32[]{:S(2)}, u32[]{:S(2)}) collective-permute-start(bf16[192,640]{1,0:T(8,128)(2,1)S(1)} %get-tuple-element.14), channel_id=1, source_target_pairs={{0,1},{1,0},{2,3},{3,2},{4,5},{5,4},{6,7},{7,6},{8,9},{9,8},{10,11... | collective-permute-start | bytes 737288 | tf_op jit(solution)/shard_map/ppermute | solution.py:246
  91.9 13.0 %copy-start.1 = (bf16[1,4,3584]{2,1,0:T(4,128)(2,1)S(1)}, bf16[1,4,3584]{2,1,0:T(4,128)(2,1)}, u32[]{:S(2)}) copy-start(bf16[1,4,3584]{2,1,0:T(4,128)(2,1)} %param.7) | copy-start | bytes 86020

commit v6 on v5

--- a/solution.py
+++ b/solution.py
@@ -41,8 +41,13 @@
     return whole, at - whole * count
 
 
-def announce(rows_ref, routes_ref, weights_ref, out_ref):
-    half_width = rows_ref.shape[1]
+def announce(rows_hbm, routes_ref, weights_ref, out_hbm, extra_ref, sems):
+    half_width = rows_hbm.shape[1]
+    copies = []
+    for t in range(ALONG):
+        target = out_hbm.at[t, :, pl.ds(0, half_width)]
+        copies.append(pltpu.make_async_copy(rows_hbm, target, sems.at[t]))
+        copies[t].start()
     row = lax.broadcasted_iota(jnp.int32, (ROWS, EXTRA), 0)
     lane = lax.broadcasted_iota(jnp.int32, (ROWS, EXTRA), 1)
     dense = jnp.zeros((ROWS, EXTRA), F32)
@@ -52,11 +57,13 @@
             here = (row == r) & ((lane == name) | (lane == name + EXPERTS))
             dense += jnp.where(here, weights_ref[r, k], 0.0)
     high = dense.astype(BF16).astype(F32)
-    extra = jnp.where(lane < EXPERTS, high, dense - high).astype(BF16)
-    rows = rows_ref[...]
+    extra_ref[...] = jnp.where(lane < EXPERTS, high, dense - high).astype(BF16)
     for t in range(ALONG):
-        out_ref[t, :, :half_width] = rows
-        out_ref[t, :, half_width:] = extra
+        target = out_hbm.at[t, :, pl.ds(half_width, EXTRA)]
+        copies.append(pltpu.make_async_copy(extra_ref, target, sems.at[ALONG + t]))
+        copies[ALONG + t].start()
+    for copy in copies:
+        copy.wait()
 
 
 def sort_rows(info_ref, rows_ref, out_ref, back_ref, staged, sems):
@@ -95,43 +102,55 @@
         copy.wait()
 
 
-def gate(rows_ref, gain_ref, own_ref, other_ref, kept_ref, sent_ref, squares):
-    half_width, cols = own_ref.shape
+def gate(
+    rows_ref, gain_ref, own_ref, other_hbm, kept_ref, sent_ref, squares_ref, scaled_ref, other_ref, sem
+):
+    copy = pltpu.make_async_copy(other_hbm, other_ref, sem)
+    copy.start()
+    half_width, cols = own_ref.shape[0], kept_ref.shape[1]
+    rows = rows_ref.shape[0]
     deep = half_width // 7
     for k in range(7):
         at = slice(k * deep, (k + 1) * deep)
         values = rows_ref[:, at].astype(F32)
         part = jnp.sum(values * values, axis=1, keepdims=True)
-        squares[...] = jnp.broadcast_to(part, squares.shape) + (squares[...] if k else 0.0)
+        squares_ref[...] = jnp.broadcast_to(part, squares_ref.shape) + (
+            squares_ref[...] if k else 0.0
+        )
         scaled = (values * gain_ref[:, at].astype(F32)).astype(BF16)
-        for lo, weights in ((0, own_ref), (cols, other_ref)):
-            sums = jnp.dot(scaled, weights[at, :], preferred_element_type=F32)
-            kept_ref[:, lo : lo + cols] = sums + (kept_ref[:, lo : lo + cols] if k else 0.0)
-    sent_ref[:, : 2 * cols] = kept_ref[:, : 2 * cols].astype(BF16)
-    total = squares[...]
+        scaled_ref[:, at] = scaled
+        sums = jnp.dot(scaled, own_ref[at, :], preferred_element_type=F32)
+        kept_ref[:, : cols // 2] = sums + (kept_ref[:, : cols // 2] if k else 0.0)
+    copy.wait()
+    kept_ref[:, cols // 2 :] = jnp.dot(scaled_ref[...], other_ref[...], preferred_element_type=F32)
+    sent_ref[:rows] = kept_ref[...].astype(BF16)
+    across = lax.broadcasted_iota(jnp.int32, (rows, cols), 1)
+    down = lax.broadcasted_iota(jnp.int32, (rows, cols), 0)
+    total = jnp.sum(jnp.where(across == down, squares_ref[:, :1], 0.0), axis=0, keepdims=True)
     high = total.astype(BF16).astype(F32)
-    lane = lax.broadcasted_iota(jnp.int32, total.shape, 1)
-    pieces = jnp.where(lane == 0, high, jnp.where(lane == 1, total - high, 0.0))
-    kept_ref[:, 2 * cols :] = total
-    sent_ref[:, 2 * cols :] = pieces.astype(BF16)
-
-
-def expert(width, info_ref, rows_ref, kept_ref, got_ref, down_ref, out_ref):
+    row = lax.broadcasted_iota(jnp.int32, (16, cols), 0)
+    sent_ref[rows:] = jnp.where(row == 0, high, jnp.where(row == 1, total - high, 0.0)).astype(BF16)
+
+
+def expert(width, info_ref, rows_ref, kept_ref, squares_ref, got_ref, down_ref, out_ref):
     units, half_width = down_ref.shape[0] // 2, down_ref.shape[1]
     which = info_ref[1]
     tail = rows_ref[:, half_width:].astype(F32)
     lane = lax.broadcasted_iota(jnp.int32, tail.shape, 1)
     mine = (lane == which) | (lane == which + EXPERTS)
     weight = jnp.sum(jnp.where(mine, tail, 0.0), axis=1, keepdims=True)
-    far = jnp.sum(got_ref[:, 4 * units :].astype(F32), axis=1, keepdims=True)
-    squares = kept_ref[:, 4 * units : 4 * units + 1] + far
+    rows = kept_ref.shape[0]
+    far = jnp.sum(got_ref[rows:].astype(F32), axis=0, keepdims=True)
+    across = lax.broadcasted_iota(jnp.int32, (rows, far.shape[1]), 1)
+    same = across == lax.broadcasted_iota(jnp.int32, (rows, far.shape[1]), 0)
+    squares = squares_ref[:, :1] + jnp.sum(jnp.where(same, far, 0.0), axis=1, keepdims=True)
     scale = lax.rsqrt(squares * (1.0 / width) + 1e-06)
     hidden = []
     for at in range(2):
         lo = 2 * units * at
-        a = (kept_ref[:, lo : lo + units] + got_ref[:, lo : lo + units].astype(F32)) * scale
+        a = (kept_ref[:, lo : lo + units] + got_ref[:rows, lo : lo + units].astype(F32)) * scale
         lo += units
-        b = (kept_ref[:, lo : lo + units] + got_ref[:, lo : lo + units].astype(F32)) * scale
+        b = (kept_ref[:, lo : lo + units] + got_ref[:rows, lo : lo + units].astype(F32)) * scale
         hidden.append((a / (1.0 + jnp.exp(-a)) * b * weight).astype(BF16))
     both = jnp.concatenate(hidden, axis=1)
     deep = half_width // 4
@@ -218,7 +237,9 @@
         rows,
         routes[0],
         route_weights[0],
-        spaces=[pltpu.VMEM, pltpu.SMEM, pltpu.SMEM],
+        spaces=[pltpu.HBM, pltpu.SMEM, pltpu.SMEM],
+        out_spaces=[pltpu.HBM],
+        scratch=[pltpu.VMEM((ROWS, EXTRA), BF16), pltpu.SemaphoreType.DMA((2 * ALONG,))],
         vmem=60 * MIB,
     )
     met = traded(leaving, near).reshape(WIDE, full)
@@ -234,14 +255,23 @@
     )
     gathered = traded(sorted_rows.reshape(ALONG, TIGHT, full), far).reshape(total, full)
     gathered, gain_other = lax.optimization_barrier((gathered, gain_other))
-    kept, sent = local(
+    kept, sent, squares = local(
         gate,
-        [shape(total, 2 * cols + EXTRA, dtype=F32), shape(total, 2 * cols + EXTRA)],
+        [
+            shape(total, 2 * cols, dtype=F32),
+            shape(total + 16, 2 * cols),
+            shape(total, EXTRA, dtype=F32),
+        ],
         gathered,
         in_gain,
         gate_own,
         gate_other,
-        scratch=[pltpu.VMEM((total, EXTRA), F32)],
+        spaces=[pltpu.VMEM] * 3 + [pl.ANY],
+        scratch=[
+            pltpu.VMEM((total, half_width), BF16),
+            pltpu.VMEM((half_width, cols), BF16),
+            pltpu.SemaphoreType.DMA,
+        ],
     )
     got = lax.ppermute(sent, "tp", swap)
     (parts,) = local(
@@ -250,9 +280,10 @@
         info,
         gathered,
         kept,
+        squares,
         got,
         down_all,
-        spaces=[pltpu.SMEM] + [pltpu.VMEM] * 4,
+        spaces=[pltpu.SMEM] + [pltpu.VMEM] * 5,
     )
     returned = traded(parts.reshape(ALONG, TIGHT, half_width), far).reshape(total, half_width)
     (summed,) = local(gather_parts, [shape(WIDE, half_width)], far_back, returned)

time: 117 us -> 123 us (1.051)
  Pallas kernels: 9.95 us -> 17.2 us
    pallas_call x7, Pallas kernels: 9.95 us -> 17.2 us  [local(): pl.pallas_call(kernel, out_shape=outs, in_specs=[pl.BlockSpec(memory_spac...]
where the time goes in v6:
time: 123 us
  blocking collectives  46.4 us (38%)
  waiting for transfers between devices  28.7 us (23%)
  starting transfers between devices  28.2 us (23%)
  Pallas kernels  17.2 us (14%)
  other arithmetic  1.38 us (1%)
    all_to_all x2, blocking collectives, traded(): lax.all_to_all(block, 'ep', 0, 0, axis_index_groups=groups, tiled=True)  37.3 us
    all_to_all x2, waiting for transfers between devices, traded(): lax.all_to_all(block, 'ep', 0, 0, axis_index_groups=groups, tiled=True)  21.6 us
    all_to_all x2, starting transfers between devices, traded(): lax.all_to_all(block, 'ep', 0, 0, axis_index_groups=groups, tiled=True)  17.4 us
    pallas_call x7, Pallas kernels, local(): pl.pallas_call(kernel, out_shape=outs, in_specs=[pl.BlockSpec(memory_spac...  17.2 us
    all_to_all x1, blocking collectives, body(): got = lax.all_to_all(leaving, ('section', 'tp'), 0, 0, tiled=True)  9.06 us
    ppermute x1, starting transfers between devices, body(): gain_other = lax.ppermute(out_gain, 'section', swap)  4.03 us
    ppermute x1, waiting for transfers between devices, body(): got = lax.ppermute(sent, 'tp', swap)  3.97 us
    ppermute x1, waiting for transfers between devices, body(): gain_other = lax.ppermute(out_gain, 'section', swap)  3.08 us
  transfers between devices with their start and end apart: 6, of which 4 were waited for; matrix products, arithmetic and copies ran while one was open for 1% of the time, Pallas kernels for 2%

profile of v6, /device:TPU:2, one launch (start us, length us, event | category | flops | bytes accessed | tf_op | source)
XLA Modules:
  0.0 122.8 jit_solution(7520832399500719235)
XLA Ops:
  0.6 8.9 %shard_map.86 = bf16[8,4,3712]{2,1,0:T(4,128)(2,1)} custom-call(bf16[4,3584]{1,0:T(4,128)(2,1)} %bitcast.21, s32[4,4]{1,0:T(4,128)} %bitcast.27, f32[4,4]{1,0:T(4,128)} %bitcast.28), custom_call_target="tpu_custom_call" | custom-call | tf_op jit(solution)/shard_map/pallas_call | solution.py:195
  9.6 10.3 %all-to-all-start = ((bf16[8,4,3712]{2,1,0:T(4,128)(2,1)}), bf16[8,4,3712]{2,1,0:T(4,128)(2,1)S(1)}, u32[]{:S(2)}, u32[]{:S(2)}) async-start(bf16[8,4,3712]{2,1,0:T(4,128)(2,1)} %shard_map.86), calls=%async_computation | async-start | bytes 475136 | tf_op jit(solution)/shard_map/all_to_all | solution.py:32
  19.9 0.1 pad_add_fusion.info_ref
  20.0 10.1 %all-to-all-done = bf16[8,4,3712]{2,1,0:T(4,128)(2,1)S(1)} async-done(((bf16[8,4,3712]{2,1,0:T(4,128)(2,1)}), bf16[8,4,3712]{2,1,0:T(4,128)(2,1)S(1)}, u32[]{:S(2)}, u32[]{:S(2)}) %all-to-all-start) | async-done | bytes 237600 | tf_op jit(solution)/shard_map/all_to_all | solution.py:32
  30.1 0.1 reshape.22.rows_ref
  30.2 2.2 %shard_map.87 = (bf16[192,3712]{1,0:T(8,128)(2,1)}, bf16[32,192]{1,0:T(8,128)(2,1)S(1)}) custom-call(s32[4]{0:T(128)S(1)} %pad_add_fusion.info_ref, bf16[32,3712]{1,0:T(8,128)(2,1)S(1)} %reshape.22.rows_ref), custom_call_target="tpu_custom_call" | custom-call | tf_op jit(solution)/shard_map/pallas_call | solution.py:195
  32.4 7.1 %all-to-all-start.1 = ((bf16[8,24,3712]{2,1,0:T(8,128)(2,1)}), bf16[8,24,3712]{2,1,0:T(8,128)(2,1)S(1)}, u32[]{:S(2)}, u32[]{:S(2)}) async-start(bf16[8,24,3712]{2,1,0:T(8,128)(2,1)} %bitcast.23), calls=%async_computation.1 | async-start | bytes 2850816 | tf_op jit(solution)/shard_map/all_to_all | solution.py:32
  39.5 1.9 %collective-permute-start.1 = (bf16[3584,256]{1,0:T(8,128)(2,1)S(1)}, bf16[3584,256]{1,0:T(8,128)(2,1)}, u32[]{:S(2)}, u32[]{:S(2)}) collective-permute-start(bf16[3584,256]{1,0:T(8,128)(2,1)S(1)} %bitcast.19), channel_id=1, source_target_pairs={{0,2},{2,0},{4,6},{6,4},{8,10},{10,8},{12,14},{14,12},{16,18},{18,... | collective-permute-start | bytes 5505032 | tf_op jit(solution)/shard_map/ppermute | solution.py:228
  41.4 2.4 %collective-permute-start.3 = (bf16[128,3584]{1,0:T(8,128)(2,1)}, bf16[128,3584]{1,0:T(8,128)(2,1)}, u32[]{:S(2)}, u32[]{:S(2)}) collective-permute-start(bf16[128,3584]{1,0:T(8,128)(2,1)} %bitcast.24), channel_id=1, source_target_pairs={{0,2},{2,0},{4,6},{6,4},{8,10},{10,8},{12,14},{14,12},{16,18},{18,... | collective-permute-start | bytes 2752520 | tf_op jit(solution)/shard_map/ppermute | solution.py:229
  43.8 4.0 %collective-permute-start = (bf16[1,3584]{1,0:T(2,128)(2,1)S(1)}, bf16[1,3584]{1,0:T(2,128)(2,1)S(1)}, u32[]{:S(2)}, u32[]{:S(2)}) collective-permute-start(bf16[1,3584]{1,0:T(2,128)(2,1)S(1)} %copy-done.4), channel_id=1, source_target_pairs={{0,256},{256,0},{1,257},{257,1},{2,258},{258,2},{3,259},{259,3},{4... | collective-permute-start | bytes 21512 | tf_op jit(solution)/shard_map/ppermute | solution.py:230
  47.9 3.1 %collective-permute-done.gain_ref = bf16[1,3584]{1,0:T(2,128)(2,1)S(1)} collective-permute-done((bf16[1,3584]{1,0:T(2,128)(2,1)S(1)}, bf16[1,3584]{1,0:T(2,128)(2,1)S(1)}, u32[]{:S(2)}, u32[]{:S(2)}) %collective-permute-start) | collective-permute-done | bytes 7200 | tf_op jit(solution)/shard_map/ppermute | solution.py:230
  51.0 11.5 %all-to-all-done.1 = bf16[8,24,3712]{2,1,0:T(8,128)(2,1)S(1)} async-done(((bf16[8,24,3712]{2,1,0:T(8,128)(2,1)}), bf16[8,24,3712]{2,1,0:T(8,128)(2,1)S(1)}, u32[]{:S(2)}, u32[]{:S(2)}) %all-to-all-start.1) | async-done | bytes 1425440 | tf_op jit(solution)/shard_map/all_to_all | solution.py:32
  62.5 2.5 %shard_map.88 = (f32[192,512]{1,0:T(8,128)S(1)}, bf16[208,512]{1,0:T(8,128)(2,1)S(1)}, f32[192,128]{1,0:T(8,128)S(1)}) custom-call(bf16[192,3712]{1,0:T(8,128)(2,1)S(1)} %bitcast.15, bf16[1,3584]{1,0:T(2,128)(2,1)S(1)} %copy-done.2, bf16[3584,256]{1,0:T(8,128)(2,1)S(1)} %bitcast.20, bf16[3584,256]{1,0:T(8,128)(2,1)} %collective-permute-done.1.other_hbm), custom_call_target="tpu_custom_call" | custom-call | tf_op jit(solution)/shard_map/pallas_call | solution.py:195
  65.0 2.4 %collective-permute-start.2 = (bf16[208,512]{1,0:T(8,128)(2,1)S(1)}, bf16[208,512]{1,0:T(8,128)(2,1)S(1)}, u32[]{:S(2)}, u32[]{:S(2)}) collective-permute-start(bf16[208,512]{1,0:T(8,128)(2,1)S(1)} %get-tuple-element.16), channel_id=1, source_target_pairs={{0,1},{1,0},{2,3},{3,2},{4,5},{5,4},{6,7},{7,6},{8,9},{9,8},{10,11... | collective-permute-start | bytes 638984 | tf_op jit(solution)/shard_map/ppermute | solution.py:276
  67.4 1.3 %pad_maximum_fusion.down_ref = bf16[256,3584]{1,0:T(8,128)(2,1)S(1)} fusion(bf16[128,3584]{1,0:T(8,128)(2,1)} %collective-permute-done.3, bf16[128,3584]{1,0:T(8,128)(2,1)S(1)} %bitcast.25), kind=kLoop, calls=%fused_computation | loop fusion | flops 3670016 | bytes 3670016 | tf_op jit(solution)/shard_map/concatenate | solution.py:232
  68.7 4.0 %collective-permute-done.2.got_ref = bf16[208,512]{1,0:T(8,128)(2,1)S(1)} collective-permute-done((bf16[208,512]{1,0:T(8,128)(2,1)S(1)}, bf16[208,512]{1,0:T(8,128)(2,1)S(1)}, u32[]{:S(2)}, u32[]{:S(2)}) %collective-permute-start.2) | collective-permute-done | bytes 213024 | tf_op jit(solution)/shard_map/ppermute | solution.py:276
  72.7 1.3 %shard_map.89 = bf16[192,3584]{1,0:T(8,128)(2,1)S(1)} custom-call(s32[4]{0:T(128)S(1)} %pad_add_fusion.info_ref, bf16[192,3712]{1,0:T(8,128)(2,1)S(1)} %bitcast.16, f32[192,512]{1,0:T(8,128)S(1)} %get-tuple-element.14.kept_ref, f32[192,128]{1,0:T(8,128)S(1)} %get-tuple-element.15.squares_ref, bf16[208,512]{1,0:T(8,128)(2,1)S(1)} %collective-permute-done.2.got_ref, ...), custom_call_target="tpu_custom_call" | custom-call | tf_op jit(solution)/shard_map/pallas_call | solution.py:195
  74.0 24.8 %all_to_all.25 = bf16[8,24,3584]{2,1,0:T(8,128)(2,1)S(1)} all-to-all(bf16[8,24,3584]{2,1,0:T(8,128)(2,1)S(1)} %bitcast.17), channel_id=1, replica_groups={{2,6,10,14,18,22,26,30},{34,38,42,46,50,54,58,62},{66,70,74,78,82,86,90..., dimensions={0} | all-to-all | bytes 2752512 | tf_op jit(solution)/shard_map/all_to_all | solution.py:32
  98.8 0.3 shard_map.90
  99.2 0.1 reshape.27
  99.3 12.5 %all_to_all.26.parts_ref = bf16[8,4,3584]{2,1,0:T(4,128)(2,1)S(1)} all-to-all(bf16[8,4,3584]{2,1,0:T(4,128)(2,1)S(1)} %reshape.27), channel_id=1, replica_groups={{0,4,8,12,16,20,24,28},{32,36,40,44,48,52,56,60},{64,68,72,76,80,84,88,..., dimensions={0} | all-to-all | bytes 458752 | tf_op jit(solution)/shard_map/all_to_all | solution.py:32
  111.8 0.7 shard_map.91
  112.5 9.1 %all_to_all.27.got_ref = bf16[4,4,3712]{2,1,0:T(4,128)(2,1)S(1)} all-to-all(bf16[4,4,3712]{2,1,0:T(4,128)(2,1)S(1)} %get-tuple-element.18), channel_id=1, replica_groups=mesh['section'=2,'ep'=128,'tp'=2] {'section','tp'}, dimensions={0} | all-to-all | bytes 237568 | tf_op jit(solution)/shard_map/all_to_all | solution.py:294
  121.5 1.3 %shard_map.92 = bf16[4,3584]{1,0:T(4,128)(2,1)} custom-call(s32[4]{0:T(128)S(1)} %pad_add_fusion.info_ref, bf16[4,4,3712]{2,1,0:T(4,128)(2,1)S(1)} %all_to_all.27.got_ref, bf16[1,3584]{1,0:T(2,128)(2,1)S(1)} %collective-permute-done.gain_ref), custom_call_target="tpu_custom_call" | custom-call | tf_op jit(solution)/shard_map/pallas_call | solution.py:195
  (12 shorter events, 0.0 us)
Async XLA Ops:
  9.6 20.5 %all-to-all-start = ((bf16[8,4,3712]{2,1,0:T(4,128)(2,1)}), bf16[8,4,3712]{2,1,0:T(4,128)(2,1)S(1)}, u32[]{:S(2)}, u32[]{:S(2)}) async-start(bf16[8,4,3712]{2,1,0:T(4,128)(2,1)} %shard_map.86), calls=%async_computation | async-start | bytes 475136 | tf_op jit(solution)/shard_map/all_to_all | solution.py:32
  19.9 19.6 %copy-start = (bf16[1,1,3584,256]{3,2,1,0:T(8,128)(2,1)S(1)}, bf16[1,1,3584,256]{3,2,1,0:T(8,128)(2,1)}, u32[]{:S(2)}) copy-start(bf16[1,1,3584,256]{3,2,1,0:T(8,128)(2,1)} %param.11) | copy-start | bytes 5505028
  19.9 23.9 %copy-start.4 = (bf16[1,3584]{1,0:T(2,128)(2,1)S(1)}, bf16[1,3584]{1,0:T(2,128)(2,1)}, u32[]{:S(2)}) copy-start(bf16[1,3584]{1,0:T(2,128)(2,1)} %param.13) | copy-start | bytes 21508
  19.9 42.6 %copy-start.2 = (bf16[1,3584]{1,0:T(2,128)(2,1)S(1)}, bf16[1,3584]{1,0:T(2,128)(2,1)}, u32[]{:S(2)}) copy-start(bf16[1,3584]{1,0:T(2,128)(2,1)} %gain_ref.1) | copy-start | bytes 21508
  32.4 30.1 %all-to-all-start.1 = ((bf16[8,24,3712]{2,1,0:T(8,128)(2,1)}), bf16[8,24,3712]{2,1,0:T(8,128)(2,1)S(1)}, u32[]{:S(2)}, u32[]{:S(2)}) async-start(bf16[8,24,3712]{2,1,0:T(8,128)(2,1)} %bitcast.23), calls=%async_computation.1 | async-start | bytes 2850816 | tf_op jit(solution)/shard_map/all_to_all | solution.py:32
  39.5 23.0 %collective-permute-start.1 = (bf16[3584,256]{1,0:T(8,128)(2,1)S(1)}, bf16[3584,256]{1,0:T(8,128)(2,1)}, u32[]{:S(2)}, u32[]{:S(2)}) collective-permute-start(bf16[3584,256]{1,0:T(8,128)(2,1)S(1)} %bitcast.19), channel_id=1, source_target_pairs={{0,2},{2,0},{4,6},{6,4},{8,10},{10,8},{12,14},{14,12},{16,18},{18,... | collective-permute-start | bytes 5505032 | tf_op jit(solution)/shard_map/ppermute | solution.py:228
  41.4 26.0 %collective-permute-start.3 = (bf16[128,3584]{1,0:T(8,128)(2,1)}, bf16[128,3584]{1,0:T(8,128)(2,1)}, u32[]{:S(2)}, u32[]{:S(2)}) collective-permute-start(bf16[128,3584]{1,0:T(8,128)(2,1)} %bitcast.24), channel_id=1, source_target_pairs={{0,2},{2,0},{4,6},{6,4},{8,10},{10,8},{12,14},{14,12},{16,18},{18,... | collective-permute-start | bytes 2752520 | tf_op jit(solution)/shard_map/ppermute | solution.py:229
  43.8 7.1 %collective-permute-start = (bf16[1,3584]{1,0:T(2,128)(2,1)S(1)}, bf16[1,3584]{1,0:T(2,128)(2,1)S(1)}, u32[]{:S(2)}, u32[]{:S(2)}) collective-permute-start(bf16[1,3584]{1,0:T(2,128)(2,1)S(1)} %copy-done.4), channel_id=1, source_target_pairs={{0,256},{256,0},{1,257},{257,1},{2,258},{258,2},{3,259},{259,3},{4... | collective-permute-start | bytes 21512 | tf_op jit(solution)/shard_map/ppermute | solution.py:230
  62.5 4.9 %copy-start.3 = (bf16[1,1,128,3584]{3,2,1,0:T(8,128)(2,1)S(1)}, bf16[1,1,128,3584]{3,2,1,0:T(8,128)(2,1)}, u32[]{:S(2)}) copy-start(bf16[1,1,128,3584]{3,2,1,0:T(8,128)(2,1)} %param.12) | copy-start | bytes 2752516
  65.0 7.7 %collective-permute-start.2 = (bf16[208,512]{1,0:T(8,128)(2,1)S(1)}, bf16[208,512]{1,0:T(8,128)(2,1)S(1)}, u32[]{:S(2)}, u32[]{:S(2)}) collective-permute-start(bf16[208,512]{1,0:T(8,128)(2,1)S(1)} %get-tuple-element.16), channel_id=1, source_target_pairs={{0,1},{1,0},{2,3},{3,2},{4,5},{5,4},{6,7},{7,6},{8,9},{9,8},{10,11... | collective-permute-start | bytes 638984 | tf_op jit(solution)/shard_map/ppermute | solution.py:276
  98.8 13.0 %copy-start.1 = (bf16[1,4,3584]{2,1,0:T(4,128)(2,1)S(1)}, bf16[1,4,3584]{2,1,0:T(4,128)(2,1)}, u32[]{:S(2)}) copy-start(bf16[1,4,3584]{2,1,0:T(4,128)(2,1)} %param.7) | copy-start | bytes 86020

commit v7 on v6

--- a/solution.py
+++ b/solution.py
@@ -41,13 +41,8 @@
     return whole, at - whole * count
 
 
-def announce(rows_hbm, routes_ref, weights_ref, out_hbm, extra_ref, sems):
-    half_width = rows_hbm.shape[1]
-    copies = []
-    for t in range(ALONG):
-        target = out_hbm.at[t, :, pl.ds(0, half_width)]
-        copies.append(pltpu.make_async_copy(rows_hbm, target, sems.at[t]))
-        copies[t].start()
+def announce(rows_ref, routes_ref, weights_ref, out_ref):
+    half_width = rows_ref.shape[1]
     row = lax.broadcasted_iota(jnp.int32, (ROWS, EXTRA), 0)
     lane = lax.broadcasted_iota(jnp.int32, (ROWS, EXTRA), 1)
     dense = jnp.zeros((ROWS, EXTRA), F32)
@@ -57,17 +52,16 @@
             here = (row == r) & ((lane == name) | (lane == name + EXPERTS))
             dense += jnp.where(here, weights_ref[r, k], 0.0)
     high = dense.astype(BF16).astype(F32)
-    extra_ref[...] = jnp.where(lane < EXPERTS, high, dense - high).astype(BF16)
+    extra = jnp.where(lane < EXPERTS, high, dense - high).astype(BF16)
+    rows = rows_ref[...]
     for t in range(ALONG):
-        target = out_hbm.at[t, :, pl.ds(half_width, EXTRA)]
-        copies.append(pltpu.make_async_copy(extra_ref, target, sems.at[ALONG + t]))
-        copies[ALONG + t].start()
-    for copy in copies:
-        copy.wait()
-
-
-def sort_rows(info_ref, rows_ref, out_ref, back_ref, staged, sems):
-    crossing, which = info_ref[0] == 0, info_ref[1].astype(F32)
+        out_ref[t, :, :half_width] = rows
+        out_ref[t, :, half_width:] = extra
+
+
+def sort_rows(rows_ref, out_ref, back_ref, staged, sems):
+    place = lax.axis_index("ep")
+    crossing, which = place % 2 == 0, (place // SPAN).astype(F32)
     half_width = rows_ref.shape[1] - EXTRA
     total = ALONG * TIGHT
     tail = rows_ref[:, half_width:].astype(F32)
@@ -132,9 +126,9 @@
     sent_ref[rows:] = jnp.where(row == 0, high, jnp.where(row == 1, total - high, 0.0)).astype(BF16)
 
 
-def expert(width, info_ref, rows_ref, kept_ref, squares_ref, got_ref, down_ref, out_ref):
+def expert(width, rows_ref, kept_ref, squares_ref, got_ref, down_ref, out_ref):
     units, half_width = down_ref.shape[0] // 2, down_ref.shape[1]
-    which = info_ref[1]
+    which = lax.axis_index("ep") // SPAN
     tail = rows_ref[:, half_width:].astype(F32)
     lane = lax.broadcasted_iota(jnp.int32, tail.shape, 1)
     mine = (lane == which) | (lane == which + EXPERTS)
@@ -180,10 +174,11 @@
         sent_ref[to, :, half_width:] = pieces
 
 
-def close(width, info_ref, got_ref, gain_ref, out_ref):
+def close(width, got_ref, gain_ref, out_ref):
     half_width = gain_ref.shape[1]
-    values = got_ref[info_ref[2], :, :half_width].astype(F32)
-    far = got_ref[info_ref[3], :, half_width:].astype(F32)
+    crossed, side = 1 - lax.axis_index("section"), lax.axis_index("tp")
+    values = got_ref[crossed * 2 + side, :, :half_width].astype(F32)
+    far = got_ref[crossed * 2 + 1 - side, :, half_width:].astype(F32)
     total = jnp.sum(values * values, axis=1, keepdims=True) + jnp.sum(far, axis=1, keepdims=True)
     scale = lax.rsqrt(total * (1.0 / width) + 1e-06)
     out_ref[...] = (values * scale * gain_ref[...].astype(F32)).astype(BF16)
@@ -214,11 +209,6 @@
     units = down.shape[2]
     cols = gate_up.shape[3]
     near, far = crossed_groups(ep, 0), crossed_groups(ep, 1)
-    place = lax.axis_index("ep")
-    crossed, side = 1 - lax.axis_index("section"), lax.axis_index("tp")
-    info = jnp.stack(
-        [place % 2, place // SPAN, crossed * 2 + side, crossed * 2 + 1 - side]
-    ).astype(jnp.int32)
     other_core = [(i, i ^ 1) for i in range(ep)]
     swap = [(0, 1), (1, 0)]
     full = half_width + EXTRA
@@ -237,18 +227,14 @@
         rows,
         routes[0],
         route_weights[0],
-        spaces=[pltpu.HBM, pltpu.SMEM, pltpu.SMEM],
-        out_spaces=[pltpu.HBM],
-        scratch=[pltpu.VMEM((ROWS, EXTRA), BF16), pltpu.SemaphoreType.DMA((2 * ALONG,))],
+        spaces=[pltpu.VMEM, pltpu.SMEM, pltpu.SMEM],
         vmem=60 * MIB,
     )
     met = traded(leaving, near).reshape(WIDE, full)
     sorted_rows, far_back = local(
         sort_rows,
         [shape(total, full), shape(WIDE, total)],
-        info,
         met,
-        spaces=[pltpu.SMEM, pltpu.VMEM],
         out_spaces=[pltpu.HBM, pltpu.VMEM],
         scratch=[pltpu.VMEM((total, full), BF16), pltpu.SemaphoreType.DMA((-(-full // CHUNK),))],
         vmem=53 * MIB,
@@ -277,13 +263,11 @@
     (parts,) = local(
         functools.partial(expert, width),
         [shape(total, half_width)],
-        info,
         gathered,
         kept,
         squares,
         got,
         down_all,
-        spaces=[pltpu.SMEM] + [pltpu.VMEM] * 5,
     )
     returned = traded(parts.reshape(ALONG, TIGHT, half_width), far).reshape(total, half_width)
     (summed,) = local(gather_parts, [shape(WIDE, half_width)], far_back, returned)
@@ -295,10 +279,8 @@
     (handed,) = local(
         functools.partial(close, width),
         [shape(ROWS, half_width)],
-        info,
         got,
         gain_other,
-        spaces=[pltpu.SMEM] + [pltpu.VMEM] * 2,
     )
     return (layer_out[None], handed[None])
 

time: 123 us -> 115 us (0.935)
  blocking collectives: 46.4 us -> 66.9 us
  starting transfers between devices: 28.2 us -> 17.9 us
  waiting for transfers between devices: 28.7 us -> 18.6 us
  Pallas kernels: 17.2 us -> 8.26 us
    all_to_all x2 -> x3, blocking collectives: 37.3 us -> 57.9 us  [traded(): lax.all_to_all(block, 'ep', 0, 0, axis_index_groups=groups, tiled=True)]
    all_to_all x2 -> x1, starting transfers between devices: 17.4 us -> 7.11 us  [traded(): lax.all_to_all(block, 'ep', 0, 0, axis_index_groups=groups, tiled=True)]
    all_to_all x2 -> x1, waiting for transfers between devices: 21.6 us -> 11.5 us  [traded(): lax.all_to_all(block, 'ep', 0, 0, axis_index_groups=groups, tiled=True)]
    pallas_call x7, Pallas kernels: 17.2 us -> 8.26 us  [local(): pl.pallas_call(kernel, out_shape=outs, in_specs=[pl.BlockSpec(memory_spac...]
  transfers between devices with their start and end apart: 6 -> 5, of which waited for: 4 -> 3; matrix products, arithmetic and copies ran while one was open for 1% -> 1% of each run, Pallas kernels for 2% -> 2%
where the time goes in v7:
time: 115 us; the launch traced here: 114 us
  blocking collectives  66.9 us (58%)
  waiting for transfers between devices  18.6 us (16%)
  starting transfers between devices  17.9 us (16%)
  Pallas kernels  8.26 us (7%)
  other arithmetic  1.3 us (1%)
    all_to_all x3, blocking collectives, traded(): lax.all_to_all(block, 'ep', 0, 0, axis_index_groups=groups, tiled=True)  57.9 us
    all_to_all x1, waiting for transfers between devices, traded(): lax.all_to_all(block, 'ep', 0, 0, axis_index_groups=groups, tiled=True)  11.5 us
    all_to_all x1, blocking collectives, body(): got = lax.all_to_all(leaving, ('section', 'tp'), 0, 0, tiled=True)  9.07 us
    pallas_call x7, Pallas kernels, local(): pl.pallas_call(kernel, out_shape=outs, in_specs=[pl.BlockSpec(memory_spac...  8.26 us
    all_to_all x1, starting transfers between devices, traded(): lax.all_to_all(block, 'ep', 0, 0, axis_index_groups=groups, tiled=True)  7.11 us
    ppermute x1, starting transfers between devices, body(): gain_other = lax.ppermute(out_gain, 'section', swap)  4.04 us
    ppermute x1, waiting for transfers between devices, body(): got = lax.ppermute(sent, 'tp', swap)  3.96 us
    ppermute x1, waiting for transfers between devices, body(): gain_other = lax.ppermute(out_gain, 'section', swap)  3.07 us
  transfers between devices with their start and end apart: 5, of which 3 were waited for; matrix products, arithmetic and copies ran while one was open for 1% of the time, Pallas kernels for 2%

profile of v7, /device:TPU:2, one launch (start us, length us, event | category | flops | bytes accessed | tf_op | source)
XLA Modules:
  0.0 113.9 jit_solution(18332770855768019249)
XLA Ops:
  0.6 1.6 %shard_map.86 = bf16[8,4,3712]{2,1,0:T(4,128)(2,1)} custom-call(bf16[4,3584]{1,0:T(4,128)(2,1)} %bitcast.17, s32[4,4]{1,0:T(4,128)} %bitcast.23, f32[4,4]{1,0:T(4,128)} %bitcast.24), custom_call_target="tpu_custom_call" | custom-call | tf_op jit(solution)/shard_map/pallas_call | solution.py:190
  2.2 20.5 %all_to_all.25 = bf16[8,4,3712]{2,1,0:T(4,128)(2,1)S(1)} all-to-all(bf16[8,4,3712]{2,1,0:T(4,128)(2,1)} %shard_map.86), channel_id=1, replica_groups={{0,4,8,12,16,20,24,28},{32,36,40,44,48,52,56,60},{64,68,72,76,80,84,88,..., dimensions={0} | all-to-all | bytes 475136 | tf_op jit(solution)/shard_map/all_to_all | solution.py:32
  22.8 0.1 reshape.22.rows_ref
  22.8 1.7 %shard_map.87 = (bf16[192,3712]{1,0:T(8,128)(2,1)}, bf16[32,192]{1,0:T(8,128)(2,1)S(1)}) custom-call(bf16[32,3712]{1,0:T(8,128)(2,1)S(1)} %reshape.22.rows_ref), custom_call_target="tpu_custom_call" | custom-call | tf_op jit(solution)/shard_map/pallas_call | solution.py:190
  24.5 7.1 %all-to-all-start.1 = ((bf16[8,24,3712]{2,1,0:T(8,128)(2,1)}), bf16[8,24,3712]{2,1,0:T(8,128)(2,1)S(1)}, u32[]{:S(2)}, u32[]{:S(2)}) async-start(bf16[8,24,3712]{2,1,0:T(8,128)(2,1)} %bitcast.19), calls=%async_computation.1 | async-start | bytes 2850816 | tf_op jit(solution)/shard_map/all_to_all | solution.py:32
  31.6 1.9 %collective-permute-start.1 = (bf16[3584,256]{1,0:T(8,128)(2,1)S(1)}, bf16[3584,256]{1,0:T(8,128)(2,1)}, u32[]{:S(2)}, u32[]{:S(2)}) collective-permute-start(bf16[3584,256]{1,0:T(8,128)(2,1)S(1)} %bitcast.15), channel_id=1, source_target_pairs={{0,2},{2,0},{4,6},{6,4},{8,10},{10,8},{12,14},{14,12},{16,18},{18,... | collective-permute-start | bytes 5505032 | tf_op jit(solution)/shard_map/ppermute | solution.py:218
  33.5 2.4 %collective-permute-start.3 = (bf16[128,3584]{1,0:T(8,128)(2,1)}, bf16[128,3584]{1,0:T(8,128)(2,1)}, u32[]{:S(2)}, u32[]{:S(2)}) collective-permute-start(bf16[128,3584]{1,0:T(8,128)(2,1)} %bitcast.20), channel_id=1, source_target_pairs={{0,2},{2,0},{4,6},{6,4},{8,10},{10,8},{12,14},{14,12},{16,18},{18,... | collective-permute-start | bytes 2752520 | tf_op jit(solution)/shard_map/ppermute | solution.py:219
  36.0 4.0 %collective-permute-start = (bf16[1,3584]{1,0:T(2,128)(2,1)S(1)}, bf16[1,3584]{1,0:T(2,128)(2,1)S(1)}, u32[]{:S(2)}, u32[]{:S(2)}) collective-permute-start(bf16[1,3584]{1,0:T(2,128)(2,1)S(1)} %copy-done.4), channel_id=1, source_target_pairs={{0,256},{256,0},{1,257},{257,1},{2,258},{258,2},{3,259},{259,3},{4... | collective-permute-start | bytes 21512 | tf_op jit(solution)/shard_map/ppermute | solution.py:220
  40.0 3.1 %collective-permute-done.gain_ref = bf16[1,3584]{1,0:T(2,128)(2,1)S(1)} collective-permute-done((bf16[1,3584]{1,0:T(2,128)(2,1)S(1)}, bf16[1,3584]{1,0:T(2,128)(2,1)S(1)}, u32[]{:S(2)}, u32[]{:S(2)}) %collective-permute-start) | collective-permute-done | bytes 7200 | tf_op jit(solution)/shard_map/ppermute | solution.py:220
  43.1 11.5 %all-to-all-done.1 = bf16[8,24,3712]{2,1,0:T(8,128)(2,1)S(1)} async-done(((bf16[8,24,3712]{2,1,0:T(8,128)(2,1)}), bf16[8,24,3712]{2,1,0:T(8,128)(2,1)S(1)}, u32[]{:S(2)}, u32[]{:S(2)}) %all-to-all-start.1) | async-done | bytes 1425440 | tf_op jit(solution)/shard_map/all_to_all | solution.py:32
  54.6 0.0 collective-permute-done.1.other_hbm
  54.6 2.5 %shard_map.88 = (f32[192,512]{1,0:T(8,128)S(1)}, bf16[208,512]{1,0:T(8,128)(2,1)S(1)}, f32[192,128]{1,0:T(8,128)S(1)}) custom-call(bf16[192,3712]{1,0:T(8,128)(2,1)S(1)} %bitcast.11, bf16[1,3584]{1,0:T(2,128)(2,1)S(1)} %copy-done.2, bf16[3584,256]{1,0:T(8,128)(2,1)S(1)} %bitcast.16, bf16[3584,256]{1,0:T(8,128)(2,1)} %collective-permute-done.1.other_hbm), custom_call_target="tpu_custom_call" | custom-call | tf_op jit(solution)/shard_map/pallas_call | solution.py:190
  57.1 2.4 %collective-permute-start.2 = (bf16[208,512]{1,0:T(8,128)(2,1)S(1)}, bf16[208,512]{1,0:T(8,128)(2,1)S(1)}, u32[]{:S(2)}, u32[]{:S(2)}) collective-permute-start(bf16[208,512]{1,0:T(8,128)(2,1)S(1)} %get-tuple-element.16), channel_id=1, source_target_pairs={{0,1},{1,0},{2,3},{3,2},{4,5},{5,4},{6,7},{7,6},{8,9},{9,8},{10,11... | collective-permute-start | bytes 638984 | tf_op jit(solution)/shard_map/ppermute | solution.py:262
  59.5 0.0 collective-permute-done.3
  59.6 1.3 %pad_maximum_fusion.down_ref = bf16[256,3584]{1,0:T(8,128)(2,1)S(1)} fusion(bf16[128,3584]{1,0:T(8,128)(2,1)} %collective-permute-done.3, bf16[128,3584]{1,0:T(8,128)(2,1)S(1)} %bitcast.21), kind=kLoop, calls=%fused_computation | loop fusion | flops 3670016 | bytes 3670016 | tf_op jit(solution)/shard_map/concatenate | solution.py:222
  60.9 4.0 %collective-permute-done.2.got_ref = bf16[208,512]{1,0:T(8,128)(2,1)S(1)} collective-permute-done((bf16[208,512]{1,0:T(8,128)(2,1)S(1)}, bf16[208,512]{1,0:T(8,128)(2,1)S(1)}, u32[]{:S(2)}, u32[]{:S(2)}) %collective-permute-start.2) | collective-permute-done | bytes 213024 | tf_op jit(solution)/shard_map/ppermute | solution.py:262
  64.8 0.8 shard_map.89
  65.6 24.8 %all_to_all.26 = bf16[8,24,3584]{2,1,0:T(8,128)(2,1)S(1)} all-to-all(bf16[8,24,3584]{2,1,0:T(8,128)(2,1)S(1)} %bitcast.13), channel_id=1, replica_groups={{2,6,10,14,18,22,26,30},{34,38,42,46,50,54,58,62},{66,70,74,78,82,86,90..., dimensions={0} | all-to-all | bytes 2752512 | tf_op jit(solution)/shard_map/all_to_all | solution.py:32
  90.4 0.3 shard_map.90
  90.8 0.1 reshape.27
  90.9 12.5 %all_to_all.27.parts_ref = bf16[8,4,3584]{2,1,0:T(4,128)(2,1)S(1)} all-to-all(bf16[8,4,3584]{2,1,0:T(4,128)(2,1)S(1)} %reshape.27), channel_id=1, replica_groups={{0,4,8,12,16,20,24,28},{32,36,40,44,48,52,56,60},{64,68,72,76,80,84,88,..., dimensions={0} | all-to-all | bytes 458752 | tf_op jit(solution)/shard_map/all_to_all | solution.py:32
  103.4 0.7 shard_map.91
  104.1 9.1 %all_to_all.28.got_ref = bf16[4,4,3712]{2,1,0:T(4,128)(2,1)S(1)} all-to-all(bf16[4,4,3712]{2,1,0:T(4,128)(2,1)S(1)} %get-tuple-element.18), channel_id=1, replica_groups=mesh['section'=2,'ep'=128,'tp'=2] {'section','tp'}, dimensions={0} | all-to-all | bytes 237568 | tf_op jit(solution)/shard_map/all_to_all | solution.py:278
  113.1 0.7 shard_map.92
  (10 shorter events, 0.0 us)
Async XLA Ops:
  22.8 8.9 %copy-start = (bf16[1,1,3584,256]{3,2,1,0:T(8,128)(2,1)S(1)}, bf16[1,1,3584,256]{3,2,1,0:T(8,128)(2,1)}, u32[]{:S(2)}) copy-start(bf16[1,1,3584,256]{3,2,1,0:T(8,128)(2,1)} %param.11) | copy-start | bytes 5505028
  22.8 13.2 %copy-start.4 = (bf16[1,3584]{1,0:T(2,128)(2,1)S(1)}, bf16[1,3584]{1,0:T(2,128)(2,1)}, u32[]{:S(2)}) copy-start(bf16[1,3584]{1,0:T(2,128)(2,1)} %param.13) | copy-start | bytes 21508
  22.8 31.8 %copy-start.2 = (bf16[1,3584]{1,0:T(2,128)(2,1)S(1)}, bf16[1,3584]{1,0:T(2,128)(2,1)}, u32[]{:S(2)}) copy-start(bf16[1,3584]{1,0:T(2,128)(2,1)} %gain_ref.1) | copy-start | bytes 21508
  24.5 30.1 %all-to-all-start.1 = ((bf16[8,24,3712]{2,1,0:T(8,128)(2,1)}), bf16[8,24,3712]{2,1,0:T(8,128)(2,1)S(1)}, u32[]{:S(2)}, u32[]{:S(2)}) async-start(bf16[8,24,3712]{2,1,0:T(8,128)(2,1)} %bitcast.19), calls=%async_computation.1 | async-start | bytes 2850816 | tf_op jit(solution)/shard_map/all_to_all | solution.py:32
  31.6 23.0 %collective-permute-start.1 = (bf16[3584,256]{1,0:T(8,128)(2,1)S(1)}, bf16[3584,256]{1,0:T(8,128)(2,1)}, u32[]{:S(2)}, u32[]{:S(2)}) collective-permute-start(bf16[3584,256]{1,0:T(8,128)(2,1)S(1)} %bitcast.15), channel_id=1, source_target_pairs={{0,2},{2,0},{4,6},{6,4},{8,10},{10,8},{12,14},{14,12},{16,18},{18,... | collective-permute-start | bytes 5505032 | tf_op jit(solution)/shard_map/ppermute | solution.py:218
  33.5 26.0 %collective-permute-start.3 = (bf16[128,3584]{1,0:T(8,128)(2,1)}, bf16[128,3584]{1,0:T(8,128)(2,1)}, u32[]{:S(2)}, u32[]{:S(2)}) collective-permute-start(bf16[128,3584]{1,0:T(8,128)(2,1)} %bitcast.20), channel_id=1, source_target_pairs={{0,2},{2,0},{4,6},{6,4},{8,10},{10,8},{12,14},{14,12},{16,18},{18,... | collective-permute-start | bytes 2752520 | tf_op jit(solution)/shard_map/ppermute | solution.py:219
  36.0 7.1 %collective-permute-start = (bf16[1,3584]{1,0:T(2,128)(2,1)S(1)}, bf16[1,3584]{1,0:T(2,128)(2,1)S(1)}, u32[]{:S(2)}, u32[]{:S(2)}) collective-permute-start(bf16[1,3584]{1,0:T(2,128)(2,1)S(1)} %copy-done.4), channel_id=1, source_target_pairs={{0,256},{256,0},{1,257},{257,1},{2,258},{258,2},{3,259},{259,3},{4... | collective-permute-start | bytes 21512 | tf_op jit(solution)/shard_map/ppermute | solution.py:220
  54.6 4.9 %copy-start.3 = (bf16[1,1,128,3584]{3,2,1,0:T(8,128)(2,1)S(1)}, bf16[1,1,128,3584]{3,2,1,0:T(8,128)(2,1)}, u32[]{:S(2)}) copy-start(bf16[1,1,128,3584]{3,2,1,0:T(8,128)(2,1)} %param.12) | copy-start | bytes 2752516
  57.1 7.7 %collective-permute-start.2 = (bf16[208,512]{1,0:T(8,128)(2,1)S(1)}, bf16[208,512]{1,0:T(8,128)(2,1)S(1)}, u32[]{:S(2)}, u32[]{:S(2)}) collective-permute-start(bf16[208,512]{1,0:T(8,128)(2,1)S(1)} %get-tuple-element.16), channel_id=1, source_target_pairs={{0,1},{1,0},{2,3},{3,2},{4,5},{5,4},{6,7},{7,6},{8,9},{9,8},{10,11... | collective-permute-start | bytes 638984 | tf_op jit(solution)/shard_map/ppermute | solution.py:262
  90.4 13.0 %copy-start.1 = (bf16[1,4,3584]{2,1,0:T(4,128)(2,1)S(1)}, bf16[1,4,3584]{2,1,0:T(4,128)(2,1)}, u32[]{:S(2)}) copy-start(bf16[1,4,3584]{2,1,0:T(4,128)(2,1)} %param.7) | copy-start | bytes 86020

commit v8 on v7

--- a/solution.py
+++ b/solution.py
@@ -43,14 +43,12 @@
 
 def announce(rows_ref, routes_ref, weights_ref, out_ref):
     half_width = rows_ref.shape[1]
-    row = lax.broadcasted_iota(jnp.int32, (ROWS, EXTRA), 0)
     lane = lax.broadcasted_iota(jnp.int32, (ROWS, EXTRA), 1)
     dense = jnp.zeros((ROWS, EXTRA), F32)
-    for r in range(ROWS):
-        for k in range(routes_ref.shape[1]):
-            name = routes_ref[r, k]
-            here = (row == r) & ((lane == name) | (lane == name + EXPERTS))
-            dense += jnp.where(here, weights_ref[r, k], 0.0)
+    routes, weights = routes_ref[...], weights_ref[...]
+    for k in range(routes.shape[1]):
+        name = routes[:, k : k + 1]
+        dense += jnp.where((lane == name) | (lane == name + EXPERTS), weights[:, k : k + 1], 0.0)
     high = dense.astype(BF16).astype(F32)
     extra = jnp.where(lane < EXPERTS, high, dense - high).astype(BF16)
     rows = rows_ref[...]
@@ -61,7 +59,7 @@
 
 def sort_rows(rows_ref, out_ref, back_ref, staged, sems):
     place = lax.axis_index("ep")
-    crossing, which = place % 2 == 0, (place // SPAN).astype(F32)
+    crossing, which = place % 2 == 1, (place // SPAN).astype(F32)
     half_width = rows_ref.shape[1] - EXTRA
     total = ALONG * TIGHT
     tail = rows_ref[:, half_width:].astype(F32)
@@ -208,7 +206,7 @@
     width = half_width * lax.axis_size("tp")
     units = down.shape[2]
     cols = gate_up.shape[3]
-    near, far = crossed_groups(ep, 0), crossed_groups(ep, 1)
+    near, far = crossed_groups(ep, 1), crossed_groups(ep, 0)
     other_core = [(i, i ^ 1) for i in range(ep)]
     swap = [(0, 1), (1, 0)]
     full = half_width + EXTRA
@@ -227,7 +225,6 @@
         rows,
         routes[0],
         route_weights[0],
-        spaces=[pltpu.VMEM, pltpu.SMEM, pltpu.SMEM],
         vmem=60 * MIB,
     )
     met = traded(leaving, near).reshape(WIDE, full)

time: 115 us -> 114 us (level)
  blocking collectives: 66.9 us -> 63.7 us
  starting transfers between devices: 17.9 us -> 21.1 us
    all_to_all x1, starting transfers between devices: 7.11 us -> 10.3 us  [traded(): lax.all_to_all(block, 'ep', 0, 0, axis_index_groups=groups, tiled=True)]
    all_to_all x3, blocking collectives: 57.9 us -> 54.7 us  [traded(): lax.all_to_all(block, 'ep', 0, 0, axis_index_groups=groups, tiled=True)]
where the time goes in v8:
time: 114 us
  blocking collectives  63.7 us (56%)
  starting transfers between devices  21.1 us (19%)
  waiting for transfers between devices  18.6 us (16%)
  Pallas kernels  8.22 us (7%)
  other arithmetic  1.3 us (1%)
    all_to_all x3, blocking collectives, traded(): lax.all_to_all(block, 'ep', 0, 0, axis_index_groups=groups, tiled=True)  54.7 us
    all_to_all x1, waiting for transfers between devices, traded(): lax.all_to_all(block, 'ep', 0, 0, axis_index_groups=groups, tiled=True)  11.5 us
    all_to_all x1, starting transfers between devices, traded(): lax.all_to_all(block, 'ep', 0, 0, axis_index_groups=groups, tiled=True)  10.3 us
    all_to_all x1, blocking collectives, body(): got = lax.all_to_all(leaving, ('section', 'tp'), 0, 0, tiled=True)  9.07 us
    pallas_call x7, Pallas kernels, local(): pl.pallas_call(kernel, out_shape=outs, in_specs=[pl.BlockSpec(memory_spac...  8.22 us
    ppermute x1, starting transfers between devices, body(): gain_other = lax.ppermute(out_gain, 'section', swap)  4.03 us
    ppermute x1, waiting for transfers between devices, body(): got = lax.ppermute(sent, 'tp', swap)  3.97 us
    ppermute x1, waiting for transfers between devices, body(): gain_other = lax.ppermute(out_gain, 'section', swap)  3.07 us
  transfers between devices with their start and end apart: 5, of which 3 were waited for; matrix products, arithmetic and copies ran while one was open for 1% of the time, Pallas kernels for 2%

profile of v8, /device:TPU:2, one launch (start us, length us, event | category | flops | bytes accessed | tf_op | source)
XLA Modules:
  0.0 113.8 jit_solution(13366417032323529623)
XLA Ops:
  0.6 1.6 %shard_map.86 = bf16[8,4,3712]{2,1,0:T(4,128)(2,1)} custom-call(bf16[4,3584]{1,0:T(4,128)(2,1)} %bitcast.17, s32[4,4]{1,0:T(4,128)} %bitcast.23, f32[4,4]{1,0:T(4,128)} %bitcast.24), custom_call_target="tpu_custom_call" | custom-call | tf_op jit(solution)/shard_map/pallas_call | solution.py:188
  2.2 17.3 %all_to_all.25 = bf16[8,4,3712]{2,1,0:T(4,128)(2,1)S(1)} all-to-all(bf16[8,4,3712]{2,1,0:T(4,128)(2,1)} %shard_map.86), channel_id=1, replica_groups={{2,6,10,14,18,22,26,30},{34,38,42,46,50,54,58,62},{66,70,74,78,82,86,90..., dimensions={0} | all-to-all | bytes 475136 | tf_op jit(solution)/shard_map/all_to_all | solution.py:32
  19.5 0.1 reshape.22.rows_ref
  19.6 1.7 %shard_map.87 = (bf16[192,3712]{1,0:T(8,128)(2,1)}, bf16[32,192]{1,0:T(8,128)(2,1)S(1)}) custom-call(bf16[32,3712]{1,0:T(8,128)(2,1)S(1)} %reshape.22.rows_ref), custom_call_target="tpu_custom_call" | custom-call | tf_op jit(solution)/shard_map/pallas_call | solution.py:188
  21.2 10.3 %all-to-all-start.1 = ((bf16[8,24,3712]{2,1,0:T(8,128)(2,1)}), bf16[8,24,3712]{2,1,0:T(8,128)(2,1)S(1)}, u32[]{:S(2)}, u32[]{:S(2)}) async-start(bf16[8,24,3712]{2,1,0:T(8,128)(2,1)} %bitcast.19), calls=%async_computation.1 | async-start | bytes 2850816 | tf_op jit(solution)/shard_map/all_to_all | solution.py:32
  31.6 1.9 %collective-permute-start.1 = (bf16[3584,256]{1,0:T(8,128)(2,1)S(1)}, bf16[3584,256]{1,0:T(8,128)(2,1)}, u32[]{:S(2)}, u32[]{:S(2)}) collective-permute-start(bf16[3584,256]{1,0:T(8,128)(2,1)S(1)} %bitcast.15), channel_id=1, source_target_pairs={{0,2},{2,0},{4,6},{6,4},{8,10},{10,8},{12,14},{14,12},{16,18},{18,... | collective-permute-start | bytes 5505032 | tf_op jit(solution)/shard_map/ppermute | solution.py:216
  33.5 2.4 %collective-permute-start.3 = (bf16[128,3584]{1,0:T(8,128)(2,1)}, bf16[128,3584]{1,0:T(8,128)(2,1)}, u32[]{:S(2)}, u32[]{:S(2)}) collective-permute-start(bf16[128,3584]{1,0:T(8,128)(2,1)} %bitcast.20), channel_id=1, source_target_pairs={{0,2},{2,0},{4,6},{6,4},{8,10},{10,8},{12,14},{14,12},{16,18},{18,... | collective-permute-start | bytes 2752520 | tf_op jit(solution)/shard_map/ppermute | solution.py:217
  35.9 4.0 %collective-permute-start = (bf16[1,3584]{1,0:T(2,128)(2,1)S(1)}, bf16[1,3584]{1,0:T(2,128)(2,1)S(1)}, u32[]{:S(2)}, u32[]{:S(2)}) collective-permute-start(bf16[1,3584]{1,0:T(2,128)(2,1)S(1)} %copy-done.4), channel_id=1, source_target_pairs={{0,256},{256,0},{1,257},{257,1},{2,258},{258,2},{3,259},{259,3},{4... | collective-permute-start | bytes 21512 | tf_op jit(solution)/shard_map/ppermute | solution.py:218
  40.0 3.1 %collective-permute-done.gain_ref = bf16[1,3584]{1,0:T(2,128)(2,1)S(1)} collective-permute-done((bf16[1,3584]{1,0:T(2,128)(2,1)S(1)}, bf16[1,3584]{1,0:T(2,128)(2,1)S(1)}, u32[]{:S(2)}, u32[]{:S(2)}) %collective-permute-start) | collective-permute-done | bytes 7200 | tf_op jit(solution)/shard_map/ppermute | solution.py:218
  43.0 11.5 %all-to-all-done.1 = bf16[8,24,3712]{2,1,0:T(8,128)(2,1)S(1)} async-done(((bf16[8,24,3712]{2,1,0:T(8,128)(2,1)}), bf16[8,24,3712]{2,1,0:T(8,128)(2,1)S(1)}, u32[]{:S(2)}, u32[]{:S(2)}) %all-to-all-start.1) | async-done | bytes 1425440 | tf_op jit(solution)/shard_map/all_to_all | solution.py:32
  54.6 0.0 collective-permute-done.1.other_hbm
  54.6 2.5 %shard_map.88 = (f32[192,512]{1,0:T(8,128)S(1)}, bf16[208,512]{1,0:T(8,128)(2,1)S(1)}, f32[192,128]{1,0:T(8,128)S(1)}) custom-call(bf16[192,3712]{1,0:T(8,128)(2,1)S(1)} %bitcast.11, bf16[1,3584]{1,0:T(2,128)(2,1)S(1)} %copy-done.2, bf16[3584,256]{1,0:T(8,128)(2,1)S(1)} %bitcast.16, bf16[3584,256]{1,0:T(8,128)(2,1)} %collective-permute-done.1.other_hbm), custom_call_target="tpu_custom_call" | custom-call | tf_op jit(solution)/shard_map/pallas_call | solution.py:188
  57.0 2.4 %collective-permute-start.2 = (bf16[208,512]{1,0:T(8,128)(2,1)S(1)}, bf16[208,512]{1,0:T(8,128)(2,1)S(1)}, u32[]{:S(2)}, u32[]{:S(2)}) collective-permute-start(bf16[208,512]{1,0:T(8,128)(2,1)S(1)} %get-tuple-element.16), channel_id=1, source_target_pairs={{0,1},{1,0},{2,3},{3,2},{4,5},{5,4},{6,7},{7,6},{8,9},{9,8},{10,11... | collective-permute-start | bytes 638984 | tf_op jit(solution)/shard_map/ppermute | solution.py:259
  59.5 0.0 collective-permute-done.3
  59.5 1.3 %pad_maximum_fusion.down_ref = bf16[256,3584]{1,0:T(8,128)(2,1)S(1)} fusion(bf16[128,3584]{1,0:T(8,128)(2,1)} %collective-permute-done.3, bf16[128,3584]{1,0:T(8,128)(2,1)S(1)} %bitcast.21), kind=kLoop, calls=%fused_computation | loop fusion | flops 3670016 | bytes 3670016 | tf_op jit(solution)/shard_map/concatenate | solution.py:220
  60.8 4.0 %collective-permute-done.2.got_ref = bf16[208,512]{1,0:T(8,128)(2,1)S(1)} collective-permute-done((bf16[208,512]{1,0:T(8,128)(2,1)S(1)}, bf16[208,512]{1,0:T(8,128)(2,1)S(1)}, u32[]{:S(2)}, u32[]{:S(2)}) %collective-permute-start.2) | collective-permute-done | bytes 213024 | tf_op jit(solution)/shard_map/ppermute | solution.py:259
  64.8 0.8 shard_map.89
  65.6 24.8 %all_to_all.26 = bf16[8,24,3584]{2,1,0:T(8,128)(2,1)S(1)} all-to-all(bf16[8,24,3584]{2,1,0:T(8,128)(2,1)S(1)} %bitcast.13), channel_id=1, replica_groups={{0,4,8,12,16,20,24,28},{32,36,40,44,48,52,56,60},{64,68,72,76,80,84,88,..., dimensions={0} | all-to-all | bytes 2752512 | tf_op jit(solution)/shard_map/all_to_all | solution.py:32
  90.4 0.3 shard_map.90
  90.7 0.1 reshape.27
  90.8 12.5 %all_to_all.27.parts_ref = bf16[8,4,3584]{2,1,0:T(4,128)(2,1)S(1)} all-to-all(bf16[8,4,3584]{2,1,0:T(4,128)(2,1)S(1)} %reshape.27), channel_id=1, replica_groups={{2,6,10,14,18,22,26,30},{34,38,42,46,50,54,58,62},{66,70,74,78,82,86,90..., dimensions={0} | all-to-all | bytes 458752 | tf_op jit(solution)/shard_map/all_to_all | solution.py:32
  103.4 0.7 shard_map.91
  104.0 9.1 %all_to_all.28.got_ref = bf16[4,4,3712]{2,1,0:T(4,128)(2,1)S(1)} all-to-all(bf16[4,4,3712]{2,1,0:T(4,128)(2,1)S(1)} %get-tuple-element.18), channel_id=1, replica_groups=mesh['section'=2,'ep'=128,'tp'=2] {'section','tp'}, dimensions={0} | all-to-all | bytes 237568 | tf_op jit(solution)/shard_map/all_to_all | solution.py:275
  113.1 0.7 shard_map.92
  (10 shorter events, 0.0 us)
Async XLA Ops:
  19.5 12.1 %copy-start = (bf16[1,1,3584,256]{3,2,1,0:T(8,128)(2,1)S(1)}, bf16[1,1,3584,256]{3,2,1,0:T(8,128)(2,1)}, u32[]{:S(2)}) copy-start(bf16[1,1,3584,256]{3,2,1,0:T(8,128)(2,1)} %param.11) | copy-start | bytes 5505028
  19.5 16.4 %copy-start.4 = (bf16[1,3584]{1,0:T(2,128)(2,1)S(1)}, bf16[1,3584]{1,0:T(2,128)(2,1)}, u32[]{:S(2)}) copy-start(bf16[1,3584]{1,0:T(2,128)(2,1)} %param.13) | copy-start | bytes 21508
  19.5 35.1 %copy-start.2 = (bf16[1,3584]{1,0:T(2,128)(2,1)S(1)}, bf16[1,3584]{1,0:T(2,128)(2,1)}, u32[]{:S(2)}) copy-start(bf16[1,3584]{1,0:T(2,128)(2,1)} %gain_ref.1) | copy-start | bytes 21508
  21.2 33.3 %all-to-all-start.1 = ((bf16[8,24,3712]{2,1,0:T(8,128)(2,1)}), bf16[8,24,3712]{2,1,0:T(8,128)(2,1)S(1)}, u32[]{:S(2)}, u32[]{:S(2)}) async-start(bf16[8,24,3712]{2,1,0:T(8,128)(2,1)} %bitcast.19), calls=%async_computation.1 | async-start | bytes 2850816 | tf_op jit(solution)/shard_map/all_to_all | solution.py:32
  31.6 23.0 %collective-permute-start.1 = (bf16[3584,256]{1,0:T(8,128)(2,1)S(1)}, bf16[3584,256]{1,0:T(8,128)(2,1)}, u32[]{:S(2)}, u32[]{:S(2)}) collective-permute-start(bf16[3584,256]{1,0:T(8,128)(2,1)S(1)} %bitcast.15), channel_id=1, source_target_pairs={{0,2},{2,0},{4,6},{6,4},{8,10},{10,8},{12,14},{14,12},{16,18},{18,... | collective-permute-start | bytes 5505032 | tf_op jit(solution)/shard_map/ppermute | solution.py:216
  33.5 26.0 %collective-permute-start.3 = (bf16[128,3584]{1,0:T(8,128)(2,1)}, bf16[128,3584]{1,0:T(8,128)(2,1)}, u32[]{:S(2)}, u32[]{:S(2)}) collective-permute-start(bf16[128,3584]{1,0:T(8,128)(2,1)} %bitcast.20), channel_id=1, source_target_pairs={{0,2},{2,0},{4,6},{6,4},{8,10},{10,8},{12,14},{14,12},{16,18},{18,... | collective-permute-start | bytes 2752520 | tf_op jit(solution)/shard_map/ppermute | solution.py:217
  35.9 7.1 %collective-permute-start = (bf16[1,3584]{1,0:T(2,128)(2,1)S(1)}, bf16[1,3584]{1,0:T(2,128)(2,1)S(1)}, u32[]{:S(2)}, u32[]{:S(2)}) collective-permute-start(bf16[1,3584]{1,0:T(2,128)(2,1)S(1)} %copy-done.4), channel_id=1, source_target_pairs={{0,256},{256,0},{1,257},{257,1},{2,258},{258,2},{3,259},{259,3},{4... | collective-permute-start | bytes 21512 | tf_op jit(solution)/shard_map/ppermute | solution.py:218
  54.6 4.9 %copy-start.3 = (bf16[1,1,128,3584]{3,2,1,0:T(8,128)(2,1)S(1)}, bf16[1,1,128,3584]{3,2,1,0:T(8,128)(2,1)}, u32[]{:S(2)}) copy-start(bf16[1,1,128,3584]{3,2,1,0:T(8,128)(2,1)} %param.12) | copy-start | bytes 2752516
  57.0 7.7 %collective-permute-start.2 = (bf16[208,512]{1,0:T(8,128)(2,1)S(1)}, bf16[208,512]{1,0:T(8,128)(2,1)S(1)}, u32[]{:S(2)}, u32[]{:S(2)}) collective-permute-start(bf16[208,512]{1,0:T(8,128)(2,1)S(1)} %get-tuple-element.16), channel_id=1, source_target_pairs={{0,1},{1,0},{2,3},{3,2},{4,5},{5,4},{6,7},{7,6},{8,9},{9,8},{10,11... | collective-permute-start | bytes 638984 | tf_op jit(solution)/shard_map/ppermute | solution.py:259
  90.4 13.0 %copy-start.1 = (bf16[1,4,3584]{2,1,0:T(4,128)(2,1)S(1)}, bf16[1,4,3584]{2,1,0:T(4,128)(2,1)}, u32[]{:S(2)}) copy-start(bf16[1,4,3584]{2,1,0:T(4,128)(2,1)} %param.7) | copy-start | bytes 86020

commit v9 on v8

--- a/solution.py
+++ b/solution.py
@@ -105,20 +105,21 @@
     for k in range(7):
         at = slice(k * deep, (k + 1) * deep)
         values = rows_ref[:, at].astype(F32)
-        part = jnp.sum(values * values, axis=1, keepdims=True)
-        squares_ref[...] = jnp.broadcast_to(part, squares_ref.shape) + (
-            squares_ref[...] if k else 0.0
-        )
+        for lo in range(0, deep, EXTRA):
+            piece = values[:, lo : lo + EXTRA]
+            squares = piece * piece + (squares if k or lo else 0.0)
         scaled = (values * gain_ref[:, at].astype(F32)).astype(BF16)
         scaled_ref[:, at] = scaled
         sums = jnp.dot(scaled, own_ref[at, :], preferred_element_type=F32)
         kept_ref[:, : cols // 2] = sums + (kept_ref[:, : cols // 2] if k else 0.0)
     copy.wait()
     kept_ref[:, cols // 2 :] = jnp.dot(scaled_ref[...], other_ref[...], preferred_element_type=F32)
+    squares = jnp.sum(squares, axis=1, keepdims=True)
+    squares_ref[...] = jnp.broadcast_to(squares, squares_ref.shape)
     sent_ref[:rows] = kept_ref[...].astype(BF16)
     across = lax.broadcasted_iota(jnp.int32, (rows, cols), 1)
     down = lax.broadcasted_iota(jnp.int32, (rows, cols), 0)
-    total = jnp.sum(jnp.where(across == down, squares_ref[:, :1], 0.0), axis=0, keepdims=True)
+    total = jnp.sum(jnp.where(across == down, squares, 0.0), axis=0, keepdims=True)
     high = total.astype(BF16).astype(F32)
     row = lax.broadcasted_iota(jnp.int32, (16, cols), 0)
     sent_ref[rows:] = jnp.where(row == 0, high, jnp.where(row == 1, total - high, 0.0)).astype(BF16)
@@ -152,7 +153,9 @@
 
 
 def gather_parts(back_ref, parts_ref, out_ref):
-    out_ref[...] = jnp.dot(back_ref[...], parts_ref[...], preferred_element_type=F32).astype(BF16)
+    sums = jnp.dot(back_ref[...], parts_ref[...], preferred_element_type=F32).astype(BF16)
+    for t in range(ALONG):
+        out_ref[t] = sums[t * ROWS : (t + 1) * ROWS]
 
 
 def finish(parts_ref, rows_ref, out_ref, sent_ref):
@@ -267,8 +270,8 @@
         down_all,
     )
     returned = traded(parts.reshape(ALONG, TIGHT, half_width), far).reshape(total, half_width)
-    (summed,) = local(gather_parts, [shape(WIDE, half_width)], far_back, returned)
-    home = traded(summed.reshape(ALONG, ROWS, half_width), near)
+    (summed,) = local(gather_parts, [shape(ALONG, ROWS, half_width)], far_back, returned)
+    home = traded(summed, near)
     layer_out, leaving = local(
         finish, [shape(ROWS, half_width), shape(4, ROWS, full)], home, rows
     )

time: 114 us -> 115 us (level)
  transfers between devices with their start and end apart: 5 -> 5, of which waited for: 3 -> 3; matrix products, arithmetic and copies ran while one was open for 1% -> 1% of each run, Pallas kernels for 2% -> 3%
where the time goes in v9:
time: 115 us; the launch traced here: 114 us
  blocking collectives  63.7 us (55%)
  starting transfers between devices  21.1 us (18%)
  waiting for transfers between devices  18.6 us (16%)
  Pallas kernels  8.82 us (8%)
  other arithmetic  1.3 us (1%)
    all_to_all x3, blocking collectives, traded(): lax.all_to_all(block, 'ep', 0, 0, axis_index_groups=groups, tiled=True)  54.7 us
    all_to_all x1, waiting for transfers between devices, traded(): lax.all_to_all(block, 'ep', 0, 0, axis_index_groups=groups, tiled=True)  11.5 us
    all_to_all x1, starting transfers between devices, traded(): lax.all_to_all(block, 'ep', 0, 0, axis_index_groups=groups, tiled=True)  10.3 us
    all_to_all x1, blocking collectives, body(): got = lax.all_to_all(leaving, ('section', 'tp'), 0, 0, tiled=True)  9.07 us
    pallas_call x7, Pallas kernels, local(): pl.pallas_call(kernel, out_shape=outs, in_specs=[pl.BlockSpec(memory_spac...  8.82 us
    ppermute x1, starting transfers between devices, body(): gain_other = lax.ppermute(out_gain, 'section', swap)  4.03 us
    ppermute x1, waiting for transfers between devices, body(): got = lax.ppermute(sent, 'tp', swap)  3.96 us
    ppermute x1, waiting for transfers between devices, body(): gain_other = lax.ppermute(out_gain, 'section', swap)  3.07 us
  transfers between devices with their start and end apart: 5, of which 3 were waited for; matrix products, arithmetic and copies ran while one was open for 1% of the time, Pallas kernels for 3%

profile of v9, /device:TPU:2, one launch (start us, length us, event | category | flops | bytes accessed | tf_op | source)
XLA Modules:
  0.0 114.4 jit_solution(6254664244693623587)
XLA Ops:
  0.6 1.6 %shard_map.86 = bf16[8,4,3712]{2,1,0:T(4,128)(2,1)} custom-call(bf16[4,3584]{1,0:T(4,128)(2,1)} %bitcast.17, s32[4,4]{1,0:T(4,128)} %bitcast.23, f32[4,4]{1,0:T(4,128)} %bitcast.24), custom_call_target="tpu_custom_call" | custom-call | tf_op jit(solution)/shard_map/pallas_call | solution.py:191
  2.2 17.3 %all_to_all.25 = bf16[8,4,3712]{2,1,0:T(4,128)(2,1)S(1)} all-to-all(bf16[8,4,3712]{2,1,0:T(4,128)(2,1)} %shard_map.86), channel_id=1, replica_groups={{2,6,10,14,18,22,26,30},{34,38,42,46,50,54,58,62},{66,70,74,78,82,86,90..., dimensions={0} | all-to-all | bytes 475136 | tf_op jit(solution)/shard_map/all_to_all | solution.py:32
  19.5 0.1 reshape.19.rows_ref
  19.6 1.7 %shard_map.87 = (bf16[192,3712]{1,0:T(8,128)(2,1)}, bf16[32,192]{1,0:T(8,128)(2,1)S(1)}) custom-call(bf16[32,3712]{1,0:T(8,128)(2,1)S(1)} %reshape.19.rows_ref), custom_call_target="tpu_custom_call" | custom-call | tf_op jit(solution)/shard_map/pallas_call | solution.py:191
  21.2 10.3 %all-to-all-start.1 = ((bf16[8,24,3712]{2,1,0:T(8,128)(2,1)}), bf16[8,24,3712]{2,1,0:T(8,128)(2,1)S(1)}, u32[]{:S(2)}, u32[]{:S(2)}) async-start(bf16[8,24,3712]{2,1,0:T(8,128)(2,1)} %bitcast.19), calls=%async_computation.1 | async-start | bytes 2850816 | tf_op jit(solution)/shard_map/all_to_all | solution.py:32
  31.6 1.9 %collective-permute-start.1 = (bf16[3584,256]{1,0:T(8,128)(2,1)S(1)}, bf16[3584,256]{1,0:T(8,128)(2,1)}, u32[]{:S(2)}, u32[]{:S(2)}) collective-permute-start(bf16[3584,256]{1,0:T(8,128)(2,1)S(1)} %bitcast.15), channel_id=1, source_target_pairs={{0,2},{2,0},{4,6},{6,4},{8,10},{10,8},{12,14},{14,12},{16,18},{18,... | collective-permute-start | bytes 5505032 | tf_op jit(solution)/shard_map/ppermute | solution.py:219
  33.5 2.4 %collective-permute-start.3 = (bf16[128,3584]{1,0:T(8,128)(2,1)}, bf16[128,3584]{1,0:T(8,128)(2,1)}, u32[]{:S(2)}, u32[]{:S(2)}) collective-permute-start(bf16[128,3584]{1,0:T(8,128)(2,1)} %bitcast.20), channel_id=1, source_target_pairs={{0,2},{2,0},{4,6},{6,4},{8,10},{10,8},{12,14},{14,12},{16,18},{18,... | collective-permute-start | bytes 2752520 | tf_op jit(solution)/shard_map/ppermute | solution.py:220
  35.9 4.0 %collective-permute-start = (bf16[1,3584]{1,0:T(2,128)(2,1)S(1)}, bf16[1,3584]{1,0:T(2,128)(2,1)S(1)}, u32[]{:S(2)}, u32[]{:S(2)}) collective-permute-start(bf16[1,3584]{1,0:T(2,128)(2,1)S(1)} %copy-done.4), channel_id=1, source_target_pairs={{0,256},{256,0},{1,257},{257,1},{2,258},{258,2},{3,259},{259,3},{4... | collective-permute-start | bytes 21512 | tf_op jit(solution)/shard_map/ppermute | solution.py:221
  40.0 3.1 %collective-permute-done.gain_ref = bf16[1,3584]{1,0:T(2,128)(2,1)S(1)} collective-permute-done((bf16[1,3584]{1,0:T(2,128)(2,1)S(1)}, bf16[1,3584]{1,0:T(2,128)(2,1)S(1)}, u32[]{:S(2)}, u32[]{:S(2)}) %collective-permute-start) | collective-permute-done | bytes 7200 | tf_op jit(solution)/shard_map/ppermute | solution.py:221
  43.0 11.5 %all-to-all-done.1 = bf16[8,24,3712]{2,1,0:T(8,128)(2,1)S(1)} async-done(((bf16[8,24,3712]{2,1,0:T(8,128)(2,1)}), bf16[8,24,3712]{2,1,0:T(8,128)(2,1)S(1)}, u32[]{:S(2)}, u32[]{:S(2)}) %all-to-all-start.1) | async-done | bytes 1425440 | tf_op jit(solution)/shard_map/all_to_all | solution.py:32
  54.6 0.0 collective-permute-done.1.other_hbm
  54.6 3.1 %shard_map.88 = (f32[192,512]{1,0:T(8,128)S(1)}, bf16[208,512]{1,0:T(8,128)(2,1)S(1)}, f32[192,128]{1,0:T(8,128)S(1)}) custom-call(bf16[192,3712]{1,0:T(8,128)(2,1)S(1)} %bitcast.11, bf16[1,3584]{1,0:T(2,128)(2,1)S(1)} %copy-done.2, bf16[3584,256]{1,0:T(8,128)(2,1)S(1)} %bitcast.16, bf16[3584,256]{1,0:T(8,128)(2,1)} %collective-permute-done.1.other_hbm), custom_call_target="tpu_custom_call" | custom-call | tf_op jit(solution)/shard_map/pallas_call | solution.py:191
  57.6 2.4 %collective-permute-start.2 = (bf16[208,512]{1,0:T(8,128)(2,1)S(1)}, bf16[208,512]{1,0:T(8,128)(2,1)S(1)}, u32[]{:S(2)}, u32[]{:S(2)}) collective-permute-start(bf16[208,512]{1,0:T(8,128)(2,1)S(1)} %get-tuple-element.16), channel_id=1, source_target_pairs={{0,1},{1,0},{2,3},{3,2},{4,5},{5,4},{6,7},{7,6},{8,9},{9,8},{10,11... | collective-permute-start | bytes 638984 | tf_op jit(solution)/shard_map/ppermute | solution.py:262
  60.1 0.0 collective-permute-done.3
  60.1 1.3 %pad_maximum_fusion.down_ref = bf16[256,3584]{1,0:T(8,128)(2,1)S(1)} fusion(bf16[128,3584]{1,0:T(8,128)(2,1)} %collective-permute-done.3, bf16[128,3584]{1,0:T(8,128)(2,1)S(1)} %bitcast.21), kind=kLoop, calls=%fused_computation | loop fusion | flops 3670016 | bytes 3670016 | tf_op jit(solution)/shard_map/concatenate | solution.py:223
  61.4 4.0 %collective-permute-done.2.got_ref = bf16[208,512]{1,0:T(8,128)(2,1)S(1)} collective-permute-done((bf16[208,512]{1,0:T(8,128)(2,1)S(1)}, bf16[208,512]{1,0:T(8,128)(2,1)S(1)}, u32[]{:S(2)}, u32[]{:S(2)}) %collective-permute-start.2) | collective-permute-done | bytes 213024 | tf_op jit(solution)/shard_map/ppermute | solution.py:262
  65.4 0.8 shard_map.89
  66.2 0.0 copy-start.1
  66.2 24.8 %all_to_all.26 = bf16[8,24,3584]{2,1,0:T(8,128)(2,1)S(1)} all-to-all(bf16[8,24,3584]{2,1,0:T(8,128)(2,1)S(1)} %bitcast.13), channel_id=1, replica_groups={{0,4,8,12,16,20,24,28},{32,36,40,44,48,52,56,60},{64,68,72,76,80,84,88,..., dimensions={0} | all-to-all | bytes 2752512 | tf_op jit(solution)/shard_map/all_to_all | solution.py:32
  91.0 0.4 shard_map.90
  91.4 12.5 %all_to_all.27.parts_ref = bf16[8,4,3584]{2,1,0:T(4,128)(2,1)S(1)} all-to-all(bf16[8,4,3584]{2,1,0:T(4,128)(2,1)S(1)} %shard_map.90), channel_id=1, replica_groups={{2,6,10,14,18,22,26,30},{34,38,42,46,50,54,58,62},{66,70,74,78,82,86,90..., dimensions={0} | all-to-all | bytes 458752 | tf_op jit(solution)/shard_map/all_to_all | solution.py:32
  103.9 0.7 shard_map.91
  104.5 9.1 %all_to_all.28.got_ref = bf16[4,4,3712]{2,1,0:T(4,128)(2,1)S(1)} all-to-all(bf16[4,4,3712]{2,1,0:T(4,128)(2,1)S(1)} %get-tuple-element.18), channel_id=1, replica_groups=mesh['section'=2,'ep'=128,'tp'=2] {'section','tp'}, dimensions={0} | all-to-all | bytes 237568 | tf_op jit(solution)/shard_map/all_to_all | solution.py:278
  113.6 0.7 shard_map.92
  (9 shorter events, 0.0 us)
Async XLA Ops:
  19.5 12.1 %copy-start = (bf16[1,1,3584,256]{3,2,1,0:T(8,128)(2,1)S(1)}, bf16[1,1,3584,256]{3,2,1,0:T(8,128)(2,1)}, u32[]{:S(2)}) copy-start(bf16[1,1,3584,256]{3,2,1,0:T(8,128)(2,1)} %param.11) | copy-start | bytes 5505028
  19.5 16.4 %copy-start.4 = (bf16[1,3584]{1,0:T(2,128)(2,1)S(1)}, bf16[1,3584]{1,0:T(2,128)(2,1)}, u32[]{:S(2)}) copy-start(bf16[1,3584]{1,0:T(2,128)(2,1)} %param.13) | copy-start | bytes 21508
  19.5 35.1 %copy-start.2 = (bf16[1,3584]{1,0:T(2,128)(2,1)S(1)}, bf16[1,3584]{1,0:T(2,128)(2,1)}, u32[]{:S(2)}) copy-start(bf16[1,3584]{1,0:T(2,128)(2,1)} %gain_ref.1) | copy-start | bytes 21508
  21.2 33.3 %all-to-all-start.1 = ((bf16[8,24,3712]{2,1,0:T(8,128)(2,1)}), bf16[8,24,3712]{2,1,0:T(8,128)(2,1)S(1)}, u32[]{:S(2)}, u32[]{:S(2)}) async-start(bf16[8,24,3712]{2,1,0:T(8,128)(2,1)} %bitcast.19), calls=%async_computation.1 | async-start | bytes 2850816 | tf_op jit(solution)/shard_map/all_to_all | solution.py:32
  31.6 23.0 %collective-permute-start.1 = (bf16[3584,256]{1,0:T(8,128)(2,1)S(1)}, bf16[3584,256]{1,0:T(8,128)(2,1)}, u32[]{:S(2)}, u32[]{:S(2)}) collective-permute-start(bf16[3584,256]{1,0:T(8,128)(2,1)S(1)} %bitcast.15), channel_id=1, source_target_pairs={{0,2},{2,0},{4,6},{6,4},{8,10},{10,8},{12,14},{14,12},{16,18},{18,... | collective-permute-start | bytes 5505032 | tf_op jit(solution)/shard_map/ppermute | solution.py:219
  33.5 26.6 %collective-permute-start.3 = (bf16[128,3584]{1,0:T(8,128)(2,1)}, bf16[128,3584]{1,0:T(8,128)(2,1)}, u32[]{:S(2)}, u32[]{:S(2)}) collective-permute-start(bf16[128,3584]{1,0:T(8,128)(2,1)} %bitcast.20), channel_id=1, source_target_pairs={{0,2},{2,0},{4,6},{6,4},{8,10},{10,8},{12,14},{14,12},{16,18},{18,... | collective-permute-start | bytes 2752520 | tf_op jit(solution)/shard_map/ppermute | solution.py:220
  35.9 7.1 %collective-permute-start = (bf16[1,3584]{1,0:T(2,128)(2,1)S(1)}, bf16[1,3584]{1,0:T(2,128)(2,1)S(1)}, u32[]{:S(2)}, u32[]{:S(2)}) collective-permute-start(bf16[1,3584]{1,0:T(2,128)(2,1)S(1)} %copy-done.4), channel_id=1, source_target_pairs={{0,256},{256,0},{1,257},{257,1},{2,258},{258,2},{3,259},{259,3},{4... | collective-permute-start | bytes 21512 | tf_op jit(solution)/shard_map/ppermute | solution.py:221
  54.6 5.5 %copy-start.3 = (bf16[1,1,128,3584]{3,2,1,0:T(8,128)(2,1)S(1)}, bf16[1,1,128,3584]{3,2,1,0:T(8,128)(2,1)}, u32[]{:S(2)}) copy-start(bf16[1,1,128,3584]{3,2,1,0:T(8,128)(2,1)} %param.12) | copy-start | bytes 2752516
  57.6 7.7 %collective-permute-start.2 = (bf16[208,512]{1,0:T(8,128)(2,1)S(1)}, bf16[208,512]{1,0:T(8,128)(2,1)S(1)}, u32[]{:S(2)}, u32[]{:S(2)}) collective-permute-start(bf16[208,512]{1,0:T(8,128)(2,1)S(1)} %get-tuple-element.16), channel_id=1, source_target_pairs={{0,1},{1,0},{2,3},{3,2},{4,5},{5,4},{6,7},{7,6},{8,9},{9,8},{10,11... | collective-permute-start | bytes 638984 | tf_op jit(solution)/shard_map/ppermute | solution.py:262
  66.2 37.7 %copy-start.1 = (bf16[1,4,3584]{2,1,0:T(4,128)(2,1)S(1)}, bf16[1,4,3584]{2,1,0:T(4,128)(2,1)}, u32[]{:S(2)}) copy-start(bf16[1,4,3584]{2,1,0:T(4,128)(2,1)} %param.7) | copy-start | bytes 86020

commit v10 on v8

--- a/solution.py
+++ b/solution.py
@@ -50,19 +50,30 @@
         name = routes[:, k : k + 1]
         dense += jnp.where((lane == name) | (lane == name + EXPERTS), weights[:, k : k + 1], 0.0)
     high = dense.astype(BF16).astype(F32)
-    extra = jnp.where(lane < EXPERTS, high, dense - high).astype(BF16)
-    rows = rows_ref[...]
+    extra = jnp.where(lane < EXPERTS, high, dense - high)
+    side = out_ref.shape[2]
+    rows = rows_ref[...].astype(F32)
+    rest = jnp.zeros((ROWS, 2 * side - half_width - EXTRA), F32)
+    lower = jnp.concatenate([rows[:, side:], extra, rest], axis=1)
+    block = jnp.concatenate([rows[:, :side], lower], axis=0).astype(BF16)
     for t in range(ALONG):
-        out_ref[t, :, :half_width] = rows
-        out_ref[t, :, half_width:] = extra
+        out_ref[t] = block
+
+
+def placed(half, flat):
+    shape = (WIDE, 2 * WIDE) if flat else (2 * WIDE, WIDE)
+    one, two = index(shape, 0 if flat else 1), index(shape, 1 if flat else 0)
+    block, row = split(one, ROWS)
+    return jnp.where(two == block * 2 * ROWS + half * ROWS + row, 1.0, 0.0).astype(BF16)
 
 
 def sort_rows(rows_ref, out_ref, back_ref, staged, sems):
     place = lax.axis_index("ep")
     crossing, which = place % 2 == 1, (place // SPAN).astype(F32)
-    half_width = rows_ref.shape[1] - EXTRA
+    full, side = out_ref.shape[1], rows_ref.shape[1]
     total = ALONG * TIGHT
-    tail = rows_ref[:, half_width:].astype(F32)
+    tail = rows_ref[:, full - EXTRA - side : full - side]
+    tail = jnp.dot(placed(1, True), tail, preferred_element_type=F32)
     named = jnp.where((tail > 0.0) & (index((WIDE, EXTRA), 1) < EXPERTS - 0.5), 1.0, 0.0)
     one, two = index((WIDE, WIDE), 0), index((WIDE, WIDE), 1)
     ahead = jnp.where((split(one, ROWS)[0] == split(two, ROWS)[0]) & (two < one), 1.0, 0.0)
@@ -82,11 +93,15 @@
     found = lax.dot_general(chosen, code, (((1,), (1,)), ((), ())), preferred_element_type=F32)
     forth = matrix(found, index((total, 1), 0), index((1, WIDE), 1))
     copies = []
-    for k, lo in enumerate(range(0, half_width + EXTRA, CHUNK)):
-        at = pl.ds(lo, min(CHUNK, half_width + EXTRA - lo))
-        staged[:, at] = jnp.dot(forth, rows_ref[:, at], preferred_element_type=F32).astype(BF16)
-        copies.append(pltpu.make_async_copy(staged.at[:, at], out_ref.at[:, at], sems.at[k]))
-        copies[k].start()
+    for half, (start, end) in enumerate(((0, side), (side, full))):
+        mine = jnp.dot(forth, placed(half, True), preferred_element_type=F32).astype(BF16)
+        for lo in range(start, end, CHUNK):
+            size = min(CHUNK, end - lo)
+            at, piece = pl.ds(lo, size), rows_ref[:, pl.ds(lo - start, size)]
+            staged[:, at] = jnp.dot(mine, piece, preferred_element_type=F32).astype(BF16)
+            k = len(copies)
+            copies.append(pltpu.make_async_copy(staged.at[:, at], out_ref.at[:, at], sems.at[k]))
+            copies[k].start()
     chosen = pick(index((1, total), 1), index((EXTRA, total), 0))
     found = jnp.dot(code, chosen, preferred_element_type=F32)
     back_ref[...] = matrix(found, index((1, total), 1), index((WIDE, 1), 0))
@@ -152,7 +167,13 @@
 
 
 def gather_parts(back_ref, parts_ref, out_ref):
-    out_ref[...] = jnp.dot(back_ref[...], parts_ref[...], preferred_element_type=F32).astype(BF16)
+    side = out_ref.shape[1]
+    for half in range(2):
+        at = slice(half * side, (half + 1) * side)
+        sums = jnp.dot(back_ref[...], parts_ref[:, at], preferred_element_type=F32).astype(BF16)
+        part = jnp.dot(placed(half, False), sums, preferred_element_type=F32)
+        both = part if half == 0 else both + part
+    out_ref[...] = both.astype(BF16)
 
 
 def finish(parts_ref, rows_ref, out_ref, sent_ref):
@@ -160,6 +181,7 @@
     mixture = parts_ref[0].astype(F32)
     for t in range(1, ALONG):
         mixture += parts_ref[t].astype(F32)
+    mixture = jnp.concatenate([mixture[:ROWS], mixture[ROWS:]], axis=1)
     layer = (rows_ref[...].astype(F32) + mixture).astype(BF16)
     out_ref[...] = layer
     values = layer.astype(F32)
@@ -211,6 +233,7 @@
     swap = [(0, 1), (1, 0)]
     full = half_width + EXTRA
     total = ALONG * TIGHT
+    side = -(-full // (2 * EXTRA)) * EXTRA
 
     gate_own, down_own = gate_up[0, 0], down[0, 0]
     gate_other = lax.ppermute(gate_own, "ep", other_core)
@@ -221,19 +244,19 @@
 
     (leaving,) = local(
         announce,
-        [shape(ALONG, ROWS, full)],
+        [shape(ALONG, 2 * ROWS, side)],
         rows,
         routes[0],
         route_weights[0],
         vmem=60 * MIB,
     )
-    met = traded(leaving, near).reshape(WIDE, full)
+    met = traded(leaving, near).reshape(2 * WIDE, side)
     sorted_rows, far_back = local(
         sort_rows,
         [shape(total, full), shape(WIDE, total)],
         met,
         out_spaces=[pltpu.HBM, pltpu.VMEM],
-        scratch=[pltpu.VMEM((total, full), BF16), pltpu.SemaphoreType.DMA((-(-full // CHUNK),))],
+        scratch=[pltpu.VMEM((total, full), BF16), pltpu.SemaphoreType.DMA((2 * -(-side // CHUNK),))],
         vmem=53 * MIB,
     )
     gathered = traded(sorted_rows.reshape(ALONG, TIGHT, full), far).reshape(total, full)
@@ -267,8 +290,8 @@
         down_all,
     )
     returned = traded(parts.reshape(ALONG, TIGHT, half_width), far).reshape(total, half_width)
-    (summed,) = local(gather_parts, [shape(WIDE, half_width)], far_back, returned)
-    home = traded(summed.reshape(ALONG, ROWS, half_width), near)
+    (summed,) = local(gather_parts, [shape(2 * WIDE, half_width // 2)], far_back, returned)
+    home = traded(summed.reshape(ALONG, 2 * ROWS, half_width // 2), near)
     layer_out, leaving = local(
         finish, [shape(ROWS, half_width), shape(4, ROWS, full)], home, rows
     )

time: 114 us -> 115 us (level)
  no operation moved by 1% of the time
where the time goes in v10:
time: 115 us
  blocking collectives  63.9 us (56%)
  starting transfers between devices  21.1 us (18%)
  waiting for transfers between devices  18.6 us (16%)
  Pallas kernels  8.82 us (8%)
  other arithmetic  1.3 us (1%)
    all_to_all x3, blocking collectives, traded(): lax.all_to_all(block, 'ep', 0, 0, axis_index_groups=groups, tiled=True)  54.9 us
    all_to_all x1, waiting for transfers between devices, traded(): lax.all_to_all(block, 'ep', 0, 0, axis_index_groups=groups, tiled=True)  11.5 us
    all_to_all x1, starting transfers between devices, traded(): lax.all_to_all(block, 'ep', 0, 0, axis_index_groups=groups, tiled=True)  10.3 us
    all_to_all x1, blocking collectives, body(): got = lax.all_to_all(leaving, ('section', 'tp'), 0, 0, tiled=True)  9.07 us
    pallas_call x7, Pallas kernels, local(): pl.pallas_call(kernel, out_shape=outs, in_specs=[pl.BlockSpec(memory_spac...  8.82 us
    ppermute x1, starting transfers between devices, body(): gain_other = lax.ppermute(out_gain, 'section', swap)  4.03 us
    ppermute x1, waiting for transfers between devices, body(): got = lax.ppermute(sent, 'tp', swap)  3.96 us
    ppermute x1, waiting for transfers between devices, body(): gain_other = lax.ppermute(out_gain, 'section', swap)  3.07 us
  transfers between devices with their start and end apart: 5, of which 3 were waited for; matrix products, arithmetic and copies ran while one was open for 1% of the time, Pallas kernels for 2%

profile of v10, /device:TPU:2, one launch (start us, length us, event | category | flops | bytes accessed | tf_op | source)
XLA Modules:
  0.0 114.5 jit_solution(9922398624645436257)
XLA Ops:
  0.6 1.6 %shard_map.86 = bf16[8,8,1920]{2,1,0:T(8,128)(2,1)} custom-call(bf16[4,3584]{1,0:T(4,128)(2,1)} %bitcast.21, s32[4,4]{1,0:T(4,128)} %bitcast.27, f32[4,4]{1,0:T(4,128)} %bitcast.28), custom_call_target="tpu_custom_call" | custom-call | tf_op jit(solution)/shard_map/pallas_call | solution.py:210
  2.2 17.5 %all_to_all.25 = bf16[8,8,1920]{2,1,0:T(8,128)(2,1)S(1)} all-to-all(bf16[8,8,1920]{2,1,0:T(8,128)(2,1)} %shard_map.86), channel_id=1, replica_groups={{2,6,10,14,18,22,26,30},{34,38,42,46,50,54,58,62},{66,70,74,78,82,86,90..., dimensions={0} | all-to-all | bytes 491520 | tf_op jit(solution)/shard_map/all_to_all | solution.py:32
  19.7 2.0 %shard_map.87 = (bf16[192,3712]{1,0:T(8,128)(2,1)}, bf16[32,192]{1,0:T(8,128)(2,1)S(1)}) custom-call(bf16[64,1920]{1,0:T(8,128)(2,1)S(1)} %bitcast.19), custom_call_target="tpu_custom_call" | custom-call | tf_op jit(solution)/shard_map/pallas_call | solution.py:210
  21.8 10.3 %all-to-all-start.1 = ((bf16[8,24,3712]{2,1,0:T(8,128)(2,1)}), bf16[8,24,3712]{2,1,0:T(8,128)(2,1)S(1)}, u32[]{:S(2)}, u32[]{:S(2)}) async-start(bf16[8,24,3712]{2,1,0:T(8,128)(2,1)} %bitcast.23), calls=%async_computation.1 | async-start | bytes 2850816 | tf_op jit(solution)/shard_map/all_to_all | solution.py:32
  32.1 1.9 %collective-permute-start.1 = (bf16[3584,256]{1,0:T(8,128)(2,1)S(1)}, bf16[3584,256]{1,0:T(8,128)(2,1)}, u32[]{:S(2)}, u32[]{:S(2)}) collective-permute-start(bf16[3584,256]{1,0:T(8,128)(2,1)S(1)} %bitcast.17), channel_id=1, source_target_pairs={{0,2},{2,0},{4,6},{6,4},{8,10},{10,8},{12,14},{14,12},{16,18},{18,... | collective-permute-start | bytes 5505032 | tf_op jit(solution)/shard_map/ppermute | solution.py:239
  34.0 2.4 %collective-permute-start.3 = (bf16[128,3584]{1,0:T(8,128)(2,1)}, bf16[128,3584]{1,0:T(8,128)(2,1)}, u32[]{:S(2)}, u32[]{:S(2)}) collective-permute-start(bf16[128,3584]{1,0:T(8,128)(2,1)} %bitcast.24), channel_id=1, source_target_pairs={{0,2},{2,0},{4,6},{6,4},{8,10},{10,8},{12,14},{14,12},{16,18},{18,... | collective-permute-start | bytes 2752520 | tf_op jit(solution)/shard_map/ppermute | solution.py:240
  36.4 4.0 %collective-permute-start = (bf16[1,3584]{1,0:T(2,128)(2,1)S(1)}, bf16[1,3584]{1,0:T(2,128)(2,1)S(1)}, u32[]{:S(2)}, u32[]{:S(2)}) collective-permute-start(bf16[1,3584]{1,0:T(2,128)(2,1)S(1)} %copy-done.4), channel_id=1, source_target_pairs={{0,256},{256,0},{1,257},{257,1},{2,258},{258,2},{3,259},{259,3},{4... | collective-permute-start | bytes 21512 | tf_op jit(solution)/shard_map/ppermute | solution.py:241
  40.5 3.1 %collective-permute-done.gain_ref = bf16[1,3584]{1,0:T(2,128)(2,1)S(1)} collective-permute-done((bf16[1,3584]{1,0:T(2,128)(2,1)S(1)}, bf16[1,3584]{1,0:T(2,128)(2,1)S(1)}, u32[]{:S(2)}, u32[]{:S(2)}) %collective-permute-start) | collective-permute-done | bytes 7200 | tf_op jit(solution)/shard_map/ppermute | solution.py:241
  43.6 11.5 %all-to-all-done.1 = bf16[8,24,3712]{2,1,0:T(8,128)(2,1)S(1)} async-done(((bf16[8,24,3712]{2,1,0:T(8,128)(2,1)}), bf16[8,24,3712]{2,1,0:T(8,128)(2,1)S(1)}, u32[]{:S(2)}, u32[]{:S(2)}) %all-to-all-start.1) | async-done | bytes 1425440 | tf_op jit(solution)/shard_map/all_to_all | solution.py:32
  55.1 0.0 collective-permute-done.1.other_hbm
  55.1 0.0 copy-done.2
  55.1 2.5 %shard_map.88 = (f32[192,512]{1,0:T(8,128)S(1)}, bf16[208,512]{1,0:T(8,128)(2,1)S(1)}, f32[192,128]{1,0:T(8,128)S(1)}) custom-call(bf16[192,3712]{1,0:T(8,128)(2,1)S(1)} %bitcast.13, bf16[1,3584]{1,0:T(2,128)(2,1)S(1)} %copy-done.2, bf16[3584,256]{1,0:T(8,128)(2,1)S(1)} %bitcast.18, bf16[3584,256]{1,0:T(8,128)(2,1)} %collective-permute-done.1.other_hbm), custom_call_target="tpu_custom_call" | custom-call | tf_op jit(solution)/shard_map/pallas_call | solution.py:210
  57.6 2.4 %collective-permute-start.2 = (bf16[208,512]{1,0:T(8,128)(2,1)S(1)}, bf16[208,512]{1,0:T(8,128)(2,1)S(1)}, u32[]{:S(2)}, u32[]{:S(2)}) collective-permute-start(bf16[208,512]{1,0:T(8,128)(2,1)S(1)} %get-tuple-element.16), channel_id=1, source_target_pairs={{0,1},{1,0},{2,3},{3,2},{4,5},{5,4},{6,7},{7,6},{8,9},{9,8},{10,11... | collective-permute-start | bytes 638984 | tf_op jit(solution)/shard_map/ppermute | solution.py:282
  60.0 0.0 collective-permute-done.3
  60.0 1.3 %pad_maximum_fusion.down_ref = bf16[256,3584]{1,0:T(8,128)(2,1)S(1)} fusion(bf16[128,3584]{1,0:T(8,128)(2,1)} %collective-permute-done.3, bf16[128,3584]{1,0:T(8,128)(2,1)S(1)} %bitcast.25), kind=kLoop, calls=%fused_computation | loop fusion | flops 3670016 | bytes 3670016 | tf_op jit(solution)/shard_map/concatenate | solution.py:243
  61.3 4.0 %collective-permute-done.2.got_ref = bf16[208,512]{1,0:T(8,128)(2,1)S(1)} collective-permute-done((bf16[208,512]{1,0:T(8,128)(2,1)S(1)}, bf16[208,512]{1,0:T(8,128)(2,1)S(1)}, u32[]{:S(2)}, u32[]{:S(2)}) %collective-permute-start.2) | collective-permute-done | bytes 213024 | tf_op jit(solution)/shard_map/ppermute | solution.py:282
  65.3 0.8 shard_map.89
  66.1 0.0 copy-start.1
  66.1 24.8 %all_to_all.26 = bf16[8,24,3584]{2,1,0:T(8,128)(2,1)S(1)} all-to-all(bf16[8,24,3584]{2,1,0:T(8,128)(2,1)S(1)} %bitcast.15), channel_id=1, replica_groups={{0,4,8,12,16,20,24,28},{32,36,40,44,48,52,56,60},{64,68,72,76,80,84,88,..., dimensions={0} | all-to-all | bytes 2752512 | tf_op jit(solution)/shard_map/all_to_all | solution.py:32
  90.9 0.6 shard_map.90
  91.5 12.5 %all_to_all.27.parts_ref = bf16[8,8,1792]{2,1,0:T(8,128)(2,1)S(1)} all-to-all(bf16[8,8,1792]{2,1,0:T(8,128)(2,1)S(1)} %bitcast.20), channel_id=1, replica_groups={{2,6,10,14,18,22,26,30},{34,38,42,46,50,54,58,62},{66,70,74,78,82,86,90..., dimensions={0} | all-to-all | bytes 458752 | tf_op jit(solution)/shard_map/all_to_all | solution.py:32
  104.0 0.7 shard_map.91
  104.7 9.1 %all_to_all.28.got_ref = bf16[4,4,3712]{2,1,0:T(4,128)(2,1)S(1)} all-to-all(bf16[4,4,3712]{2,1,0:T(4,128)(2,1)S(1)} %get-tuple-element.18), channel_id=1, replica_groups=mesh['section'=2,'ep'=128,'tp'=2] {'section','tp'}, dimensions={0} | all-to-all | bytes 237568 | tf_op jit(solution)/shard_map/all_to_all | solution.py:298
  113.8 0.7 shard_map.92
  (8 shorter events, 0.0 us)
Async XLA Ops:
  2.2 29.9 %copy-start = (bf16[1,1,3584,256]{3,2,1,0:T(8,128)(2,1)S(1)}, bf16[1,1,3584,256]{3,2,1,0:T(8,128)(2,1)}, u32[]{:S(2)}) copy-start(bf16[1,1,3584,256]{3,2,1,0:T(8,128)(2,1)} %param.11) | copy-start | bytes 5505028
  2.2 34.2 %copy-start.4 = (bf16[1,3584]{1,0:T(2,128)(2,1)S(1)}, bf16[1,3584]{1,0:T(2,128)(2,1)}, u32[]{:S(2)}) copy-start(bf16[1,3584]{1,0:T(2,128)(2,1)} %param.13) | copy-start | bytes 21508
  2.2 52.9 %copy-start.2 = (bf16[1,3584]{1,0:T(2,128)(2,1)S(1)}, bf16[1,3584]{1,0:T(2,128)(2,1)}, u32[]{:S(2)}) copy-start(bf16[1,3584]{1,0:T(2,128)(2,1)} %gain_ref.1) | copy-start | bytes 21508
  21.8 33.3 %all-to-all-start.1 = ((bf16[8,24,3712]{2,1,0:T(8,128)(2,1)}), bf16[8,24,3712]{2,1,0:T(8,128)(2,1)S(1)}, u32[]{:S(2)}, u32[]{:S(2)}) async-start(bf16[8,24,3712]{2,1,0:T(8,128)(2,1)} %bitcast.23), calls=%async_computation.1 | async-start | bytes 2850816 | tf_op jit(solution)/shard_map/all_to_all | solution.py:32
  32.1 23.0 %collective-permute-start.1 = (bf16[3584,256]{1,0:T(8,128)(2,1)S(1)}, bf16[3584,256]{1,0:T(8,128)(2,1)}, u32[]{:S(2)}, u32[]{:S(2)}) collective-permute-start(bf16[3584,256]{1,0:T(8,128)(2,1)S(1)} %bitcast.17), channel_id=1, source_target_pairs={{0,2},{2,0},{4,6},{6,4},{8,10},{10,8},{12,14},{14,12},{16,18},{18,... | collective-permute-start | bytes 5505032 | tf_op jit(solution)/shard_map/ppermute | solution.py:239
  34.0 26.0 %collective-permute-start.3 = (bf16[128,3584]{1,0:T(8,128)(2,1)}, bf16[128,3584]{1,0:T(8,128)(2,1)}, u32[]{:S(2)}, u32[]{:S(2)}) collective-permute-start(bf16[128,3584]{1,0:T(8,128)(2,1)} %bitcast.24), channel_id=1, source_target_pairs={{0,2},{2,0},{4,6},{6,4},{8,10},{10,8},{12,14},{14,12},{16,18},{18,... | collective-permute-start | bytes 2752520 | tf_op jit(solution)/shard_map/ppermute | solution.py:240
  36.4 7.1 %collective-permute-start = (bf16[1,3584]{1,0:T(2,128)(2,1)S(1)}, bf16[1,3584]{1,0:T(2,128)(2,1)S(1)}, u32[]{:S(2)}, u32[]{:S(2)}) collective-permute-start(bf16[1,3584]{1,0:T(2,128)(2,1)S(1)} %copy-done.4), channel_id=1, source_target_pairs={{0,256},{256,0},{1,257},{257,1},{2,258},{258,2},{3,259},{259,3},{4... | collective-permute-start | bytes 21512 | tf_op jit(solution)/shard_map/ppermute | solution.py:241
  55.1 4.9 %copy-start.3 = (bf16[1,1,128,3584]{3,2,1,0:T(8,128)(2,1)S(1)}, bf16[1,1,128,3584]{3,2,1,0:T(8,128)(2,1)}, u32[]{:S(2)}) copy-start(bf16[1,1,128,3584]{3,2,1,0:T(8,128)(2,1)} %param.12) | copy-start | bytes 2752516
  57.6 7.7 %collective-permute-start.2 = (bf16[208,512]{1,0:T(8,128)(2,1)S(1)}, bf16[208,512]{1,0:T(8,128)(2,1)S(1)}, u32[]{:S(2)}, u32[]{:S(2)}) collective-permute-start(bf16[208,512]{1,0:T(8,128)(2,1)S(1)} %get-tuple-element.16), channel_id=1, source_target_pairs={{0,1},{1,0},{2,3},{3,2},{4,5},{5,4},{6,7},{7,6},{8,9},{9,8},{10,11... | collective-permute-start | bytes 638984 | tf_op jit(solution)/shard_map/ppermute | solution.py:282
  66.1 37.9 %copy-start.1 = (bf16[1,4,3584]{2,1,0:T(4,128)(2,1)S(1)}, bf16[1,4,3584]{2,1,0:T(4,128)(2,1)}, u32[]{:S(2)}) copy-start(bf16[1,4,3584]{2,1,0:T(4,128)(2,1)} %param.7) | copy-start | bytes 86020

commit v11 on v8

--- a/solution.py
+++ b/solution.py
@@ -82,14 +82,20 @@
     found = lax.dot_general(chosen, code, (((1,), (1,)), ((), ())), preferred_element_type=F32)
     forth = matrix(found, index((total, 1), 0), index((1, WIDE), 1))
     copies = []
-    for k, lo in enumerate(range(0, half_width + EXTRA, CHUNK)):
-        at = pl.ds(lo, min(CHUNK, half_width + EXTRA - lo))
+    for k, lo in enumerate(range(0, half_width, CHUNK)):
+        at = pl.ds(lo, min(CHUNK, half_width - lo))
         staged[:, at] = jnp.dot(forth, rows_ref[:, at], preferred_element_type=F32).astype(BF16)
         copies.append(pltpu.make_async_copy(staged.at[:, at], out_ref.at[:, at], sems.at[k]))
         copies[k].start()
     chosen = pick(index((1, total), 1), index((EXTRA, total), 0))
     found = jnp.dot(code, chosen, preferred_element_type=F32)
-    back_ref[...] = matrix(found, index((1, total), 1), index((WIDE, 1), 0))
+    here = matrix(found, index((1, total), 1), index((WIDE, 1), 0)).astype(F32)
+    exact = rows_ref[:, half_width:]
+    high = jnp.dot(exact, chosen, preferred_element_type=F32)
+    chosen = pick(index((1, total), 1), index((EXTRA, total), 0) - EXPERTS)
+    low = jnp.dot(exact, chosen, preferred_element_type=F32)
+    back_ref[:WIDE] = (here * high).astype(BF16)
+    back_ref[WIDE:] = (here * low).astype(BF16)
     for copy in copies:
         copy.wait()
 
@@ -124,13 +130,8 @@
     sent_ref[rows:] = jnp.where(row == 0, high, jnp.where(row == 1, total - high, 0.0)).astype(BF16)
 
 
-def expert(width, rows_ref, kept_ref, squares_ref, got_ref, down_ref, out_ref):
+def expert(width, kept_ref, squares_ref, got_ref, down_ref, out_ref):
     units, half_width = down_ref.shape[0] // 2, down_ref.shape[1]
-    which = lax.axis_index("ep") // SPAN
-    tail = rows_ref[:, half_width:].astype(F32)
-    lane = lax.broadcasted_iota(jnp.int32, tail.shape, 1)
-    mine = (lane == which) | (lane == which + EXPERTS)
-    weight = jnp.sum(jnp.where(mine, tail, 0.0), axis=1, keepdims=True)
     rows = kept_ref.shape[0]
     far = jnp.sum(got_ref[rows:].astype(F32), axis=0, keepdims=True)
     across = lax.broadcasted_iota(jnp.int32, (rows, far.shape[1]), 1)
@@ -143,7 +144,7 @@
         a = (kept_ref[:, lo : lo + units] + got_ref[:rows, lo : lo + units].astype(F32)) * scale
         lo += units
         b = (kept_ref[:, lo : lo + units] + got_ref[:rows, lo : lo + units].astype(F32)) * scale
-        hidden.append((a / (1.0 + jnp.exp(-a)) * b * weight).astype(BF16))
+        hidden.append((a / (1.0 + jnp.exp(-a)) * b).astype(BF16))
     both = jnp.concatenate(hidden, axis=1)
     deep = half_width // 4
     for k in range(4):
@@ -152,7 +153,8 @@
 
 
 def gather_parts(back_ref, parts_ref, out_ref):
-    out_ref[...] = jnp.dot(back_ref[...], parts_ref[...], preferred_element_type=F32).astype(BF16)
+    sums = jnp.dot(back_ref[...], parts_ref[...], preferred_element_type=F32)
+    out_ref[...] = (sums[:WIDE] + sums[WIDE:]).astype(BF16)
 
 
 def finish(parts_ref, rows_ref, out_ref, sent_ref):
@@ -230,13 +232,17 @@
     met = traded(leaving, near).reshape(WIDE, full)
     sorted_rows, far_back = local(
         sort_rows,
-        [shape(total, full), shape(WIDE, total)],
+        [shape(total, half_width), shape(2 * WIDE, total)],
         met,
         out_spaces=[pltpu.HBM, pltpu.VMEM],
-        scratch=[pltpu.VMEM((total, full), BF16), pltpu.SemaphoreType.DMA((-(-full // CHUNK),))],
+        scratch=[
+            pltpu.VMEM((total, half_width), BF16),
+            pltpu.SemaphoreType.DMA((-(-half_width // CHUNK),)),
+        ],
         vmem=53 * MIB,
     )
-    gathered = traded(sorted_rows.reshape(ALONG, TIGHT, full), far).reshape(total, full)
+    gathered = traded(sorted_rows.reshape(ALONG, TIGHT, half_width), far)
+    gathered = gathered.reshape(total, half_width)
     gathered, gain_other = lax.optimization_barrier((gathered, gain_other))
     kept, sent, squares = local(
         gate,
@@ -260,7 +266,6 @@
     (parts,) = local(
         functools.partial(expert, width),
         [shape(total, half_width)],
-        gathered,
         kept,
         squares,
         got,

time: 114 us -> 114 us (level)
  no operation moved by 1% of the time
where the time goes in v11:
time: 114 us; the launch traced here: 113 us
  blocking collectives  63.7 us (56%)
  starting transfers between devices  21.1 us (19%)
  waiting for transfers between devices  18 us (16%)
  Pallas kernels  8.16 us (7%)
  other arithmetic  1.3 us (1%)
    all_to_all x3, blocking collectives, traded(): lax.all_to_all(block, 'ep', 0, 0, axis_index_groups=groups, tiled=True)  54.7 us
    all_to_all x1, waiting for transfers between devices, traded(): lax.all_to_all(block, 'ep', 0, 0, axis_index_groups=groups, tiled=True)  11 us
    all_to_all x1, starting transfers between devices, traded(): lax.all_to_all(block, 'ep', 0, 0, axis_index_groups=groups, tiled=True)  10.3 us
    all_to_all x1, blocking collectives, body(): got = lax.all_to_all(leaving, ('section', 'tp'), 0, 0, tiled=True)  9.08 us
    pallas_call x7, Pallas kernels, local(): pl.pallas_call(kernel, out_shape=outs, in_specs=[pl.BlockSpec(memory_spac...  8.16 us
    ppermute x1, starting transfers between devices, body(): gain_other = lax.ppermute(out_gain, 'section', swap)  4.04 us
    ppermute x1, waiting for transfers between devices, body(): got = lax.ppermute(sent, 'tp', swap)  3.96 us
    ppermute x1, waiting for transfers between devices, body(): gain_other = lax.ppermute(out_gain, 'section', swap)  3.07 us
  transfers between devices with their start and end apart: 5, of which 3 were waited for; matrix products, arithmetic and copies ran while one was open for 1% of the time, Pallas kernels for 2%

profile of v11, /device:TPU:2, one launch (start us, length us, event | category | flops | bytes accessed | tf_op | source)
XLA Modules:
  0.0 113.2 jit_solution(10390075212620180610)
XLA Ops:
  0.6 1.6 %shard_map.86 = bf16[8,4,3712]{2,1,0:T(4,128)(2,1)} custom-call(bf16[4,3584]{1,0:T(4,128)(2,1)} %bitcast.16, s32[4,4]{1,0:T(4,128)} %bitcast.22, f32[4,4]{1,0:T(4,128)} %bitcast.23), custom_call_target="tpu_custom_call" | custom-call | tf_op jit(solution)/shard_map/pallas_call | solution.py:190
  2.2 17.3 %all_to_all.25 = bf16[8,4,3712]{2,1,0:T(4,128)(2,1)S(1)} all-to-all(bf16[8,4,3712]{2,1,0:T(4,128)(2,1)} %shard_map.86), channel_id=1, replica_groups={{2,6,10,14,18,22,26,30},{34,38,42,46,50,54,58,62},{66,70,74,78,82,86,90..., dimensions={0} | all-to-all | bytes 475136 | tf_op jit(solution)/shard_map/all_to_all | solution.py:32
  19.5 0.1 reshape.22.rows_ref
  19.6 1.6 %shard_map.87 = (bf16[192,3584]{1,0:T(8,128)(2,1)}, bf16[64,192]{1,0:T(8,128)(2,1)S(1)}) custom-call(bf16[32,3712]{1,0:T(8,128)(2,1)S(1)} %reshape.22.rows_ref), custom_call_target="tpu_custom_call" | custom-call | tf_op jit(solution)/shard_map/pallas_call | solution.py:190
  21.2 10.3 %all-to-all-start.1 = ((bf16[8,24,3584]{2,1,0:T(8,128)(2,1)}), bf16[8,24,3584]{2,1,0:T(8,128)(2,1)S(1)}, u32[]{:S(2)}, u32[]{:S(2)}) async-start(bf16[8,24,3584]{2,1,0:T(8,128)(2,1)} %bitcast.18), calls=%async_computation.1 | async-start | bytes 2752512 | tf_op jit(solution)/shard_map/all_to_all | solution.py:32
  31.5 1.9 %collective-permute-start.1 = (bf16[3584,256]{1,0:T(8,128)(2,1)S(1)}, bf16[3584,256]{1,0:T(8,128)(2,1)}, u32[]{:S(2)}, u32[]{:S(2)}) collective-permute-start(bf16[3584,256]{1,0:T(8,128)(2,1)S(1)} %bitcast.14), channel_id=1, source_target_pairs={{0,2},{2,0},{4,6},{6,4},{8,10},{10,8},{12,14},{14,12},{16,18},{18,... | collective-permute-start | bytes 5505032 | tf_op jit(solution)/shard_map/ppermute | solution.py:218
  33.5 2.4 %collective-permute-start.3 = (bf16[128,3584]{1,0:T(8,128)(2,1)}, bf16[128,3584]{1,0:T(8,128)(2,1)}, u32[]{:S(2)}, u32[]{:S(2)}) collective-permute-start(bf16[128,3584]{1,0:T(8,128)(2,1)} %bitcast.19), channel_id=1, source_target_pairs={{0,2},{2,0},{4,6},{6,4},{8,10},{10,8},{12,14},{14,12},{16,18},{18,... | collective-permute-start | bytes 2752520 | tf_op jit(solution)/shard_map/ppermute | solution.py:219
  35.9 4.0 %collective-permute-start = (bf16[1,3584]{1,0:T(2,128)(2,1)S(1)}, bf16[1,3584]{1,0:T(2,128)(2,1)S(1)}, u32[]{:S(2)}, u32[]{:S(2)}) collective-permute-start(bf16[1,3584]{1,0:T(2,128)(2,1)S(1)} %copy-done.4), channel_id=1, source_target_pairs={{0,256},{256,0},{1,257},{257,1},{2,258},{258,2},{3,259},{259,3},{4... | collective-permute-start | bytes 21512 | tf_op jit(solution)/shard_map/ppermute | solution.py:220
  39.9 3.1 %collective-permute-done.gain_ref = bf16[1,3584]{1,0:T(2,128)(2,1)S(1)} collective-permute-done((bf16[1,3584]{1,0:T(2,128)(2,1)S(1)}, bf16[1,3584]{1,0:T(2,128)(2,1)S(1)}, u32[]{:S(2)}, u32[]{:S(2)}) %collective-permute-start) | collective-permute-done | bytes 7200 | tf_op jit(solution)/shard_map/ppermute | solution.py:220
  43.0 11.0 %all-to-all-done.1 = bf16[8,24,3584]{2,1,0:T(8,128)(2,1)S(1)} async-done(((bf16[8,24,3584]{2,1,0:T(8,128)(2,1)}), bf16[8,24,3584]{2,1,0:T(8,128)(2,1)S(1)}, u32[]{:S(2)}, u32[]{:S(2)}) %all-to-all-start.1) | async-done | bytes 1376288 | tf_op jit(solution)/shard_map/all_to_all | solution.py:32
  54.0 0.0 collective-permute-done.1.other_hbm
  54.0 2.5 %shard_map.88 = (f32[192,512]{1,0:T(8,128)S(1)}, bf16[208,512]{1,0:T(8,128)(2,1)S(1)}, f32[192,128]{1,0:T(8,128)S(1)}) custom-call(bf16[192,3584]{1,0:T(8,128)(2,1)S(1)} %bitcast.11, bf16[1,3584]{1,0:T(2,128)(2,1)S(1)} %copy-done.2, bf16[3584,256]{1,0:T(8,128)(2,1)S(1)} %bitcast.15, bf16[3584,256]{1,0:T(8,128)(2,1)} %collective-permute-done.1.other_hbm), custom_call_target="tpu_custom_call" | custom-call | tf_op jit(solution)/shard_map/pallas_call | solution.py:190
  56.5 2.4 %collective-permute-start.2 = (bf16[208,512]{1,0:T(8,128)(2,1)S(1)}, bf16[208,512]{1,0:T(8,128)(2,1)S(1)}, u32[]{:S(2)}, u32[]{:S(2)}) collective-permute-start(bf16[208,512]{1,0:T(8,128)(2,1)S(1)} %get-tuple-element.16), channel_id=1, source_target_pairs={{0,1},{1,0},{2,3},{3,2},{4,5},{5,4},{6,7},{7,6},{8,9},{9,8},{10,11... | collective-permute-start | bytes 638984 | tf_op jit(solution)/shard_map/ppermute | solution.py:265
  58.9 0.0 collective-permute-done.3
  58.9 1.3 %pad_maximum_fusion.down_ref = bf16[256,3584]{1,0:T(8,128)(2,1)S(1)} fusion(bf16[128,3584]{1,0:T(8,128)(2,1)} %collective-permute-done.3, bf16[128,3584]{1,0:T(8,128)(2,1)S(1)} %bitcast.20), kind=kLoop, calls=%fused_computation | loop fusion | flops 3670016 | bytes 3670016 | tf_op jit(solution)/shard_map/concatenate | solution.py:222
  60.2 4.0 %collective-permute-done.2.got_ref = bf16[208,512]{1,0:T(8,128)(2,1)S(1)} collective-permute-done((bf16[208,512]{1,0:T(8,128)(2,1)S(1)}, bf16[208,512]{1,0:T(8,128)(2,1)S(1)}, u32[]{:S(2)}, u32[]{:S(2)}) %collective-permute-start.2) | collective-permute-done | bytes 213024 | tf_op jit(solution)/shard_map/ppermute | solution.py:265
  64.2 0.8 shard_map.89
  65.0 24.8 %all_to_all.26 = bf16[8,24,3584]{2,1,0:T(8,128)(2,1)S(1)} all-to-all(bf16[8,24,3584]{2,1,0:T(8,128)(2,1)S(1)} %bitcast.13), channel_id=1, replica_groups={{0,4,8,12,16,20,24,28},{32,36,40,44,48,52,56,60},{64,68,72,76,80,84,88,..., dimensions={0} | all-to-all | bytes 2752512 | tf_op jit(solution)/shard_map/all_to_all | solution.py:32
  89.8 0.4 shard_map.90
  90.2 0.1 reshape.27
  90.2 12.5 %all_to_all.27.parts_ref = bf16[8,4,3584]{2,1,0:T(4,128)(2,1)S(1)} all-to-all(bf16[8,4,3584]{2,1,0:T(4,128)(2,1)S(1)} %reshape.27), channel_id=1, replica_groups={{2,6,10,14,18,22,26,30},{34,38,42,46,50,54,58,62},{66,70,74,78,82,86,90..., dimensions={0} | all-to-all | bytes 458752 | tf_op jit(solution)/shard_map/all_to_all | solution.py:32
  102.8 0.7 shard_map.91
  103.4 9.1 %all_to_all.28.got_ref = bf16[4,4,3712]{2,1,0:T(4,128)(2,1)S(1)} all-to-all(bf16[4,4,3712]{2,1,0:T(4,128)(2,1)S(1)} %get-tuple-element.18), channel_id=1, replica_groups=mesh['section'=2,'ep'=128,'tp'=2] {'section','tp'}, dimensions={0} | all-to-all | bytes 237568 | tf_op jit(solution)/shard_map/all_to_all | solution.py:280
  112.5 0.7 shard_map.92
  (10 shorter events, 0.0 us)
Async XLA Ops:
  19.5 12.0 %copy-start = (bf16[1,1,3584,256]{3,2,1,0:T(8,128)(2,1)S(1)}, bf16[1,1,3584,256]{3,2,1,0:T(8,128)(2,1)}, u32[]{:S(2)}) copy-start(bf16[1,1,3584,256]{3,2,1,0:T(8,128)(2,1)} %param.11) | copy-start | bytes 5505028
  19.5 16.4 %copy-start.4 = (bf16[1,3584]{1,0:T(2,128)(2,1)S(1)}, bf16[1,3584]{1,0:T(2,128)(2,1)}, u32[]{:S(2)}) copy-start(bf16[1,3584]{1,0:T(2,128)(2,1)} %param.13) | copy-start | bytes 21508
  19.5 34.5 %copy-start.2 = (bf16[1,3584]{1,0:T(2,128)(2,1)S(1)}, bf16[1,3584]{1,0:T(2,128)(2,1)}, u32[]{:S(2)}) copy-start(bf16[1,3584]{1,0:T(2,128)(2,1)} %gain_ref.1) | copy-start | bytes 21508
  21.2 32.8 %all-to-all-start.1 = ((bf16[8,24,3584]{2,1,0:T(8,128)(2,1)}), bf16[8,24,3584]{2,1,0:T(8,128)(2,1)S(1)}, u32[]{:S(2)}, u32[]{:S(2)}) async-start(bf16[8,24,3584]{2,1,0:T(8,128)(2,1)} %bitcast.18), calls=%async_computation.1 | async-start | bytes 2752512 | tf_op jit(solution)/shard_map/all_to_all | solution.py:32
  31.5 22.5 %collective-permute-start.1 = (bf16[3584,256]{1,0:T(8,128)(2,1)S(1)}, bf16[3584,256]{1,0:T(8,128)(2,1)}, u32[]{:S(2)}, u32[]{:S(2)}) collective-permute-start(bf16[3584,256]{1,0:T(8,128)(2,1)S(1)} %bitcast.14), channel_id=1, source_target_pairs={{0,2},{2,0},{4,6},{6,4},{8,10},{10,8},{12,14},{14,12},{16,18},{18,... | collective-permute-start | bytes 5505032 | tf_op jit(solution)/shard_map/ppermute | solution.py:218
  33.5 25.5 %collective-permute-start.3 = (bf16[128,3584]{1,0:T(8,128)(2,1)}, bf16[128,3584]{1,0:T(8,128)(2,1)}, u32[]{:S(2)}, u32[]{:S(2)}) collective-permute-start(bf16[128,3584]{1,0:T(8,128)(2,1)} %bitcast.19), channel_id=1, source_target_pairs={{0,2},{2,0},{4,6},{6,4},{8,10},{10,8},{12,14},{14,12},{16,18},{18,... | collective-permute-start | bytes 2752520 | tf_op jit(solution)/shard_map/ppermute | solution.py:219
  35.9 7.1 %collective-permute-start = (bf16[1,3584]{1,0:T(2,128)(2,1)S(1)}, bf16[1,3584]{1,0:T(2,128)(2,1)S(1)}, u32[]{:S(2)}, u32[]{:S(2)}) collective-permute-start(bf16[1,3584]{1,0:T(2,128)(2,1)S(1)} %copy-done.4), channel_id=1, source_target_pairs={{0,256},{256,0},{1,257},{257,1},{2,258},{258,2},{3,259},{259,3},{4... | collective-permute-start | bytes 21512 | tf_op jit(solution)/shard_map/ppermute | solution.py:220
  54.0 4.9 %copy-start.3 = (bf16[1,1,128,3584]{3,2,1,0:T(8,128)(2,1)S(1)}, bf16[1,1,128,3584]{3,2,1,0:T(8,128)(2,1)}, u32[]{:S(2)}) copy-start(bf16[1,1,128,3584]{3,2,1,0:T(8,128)(2,1)} %param.12) | copy-start | bytes 2752516
  56.5 7.7 %collective-permute-start.2 = (bf16[208,512]{1,0:T(8,128)(2,1)S(1)}, bf16[208,512]{1,0:T(8,128)(2,1)S(1)}, u32[]{:S(2)}, u32[]{:S(2)}) collective-permute-start(bf16[208,512]{1,0:T(8,128)(2,1)S(1)} %get-tuple-element.16), channel_id=1, source_target_pairs={{0,1},{1,0},{2,3},{3,2},{4,5},{5,4},{6,7},{7,6},{8,9},{9,8},{10,11... | collective-permute-start | bytes 638984 | tf_op jit(solution)/shard_map/ppermute | solution.py:265
  89.8 13.0 %copy-start.1 = (bf16[1,4,3584]{2,1,0:T(4,128)(2,1)S(1)}, bf16[1,4,3584]{2,1,0:T(4,128)(2,1)}, u32[]{:S(2)}) copy-start(bf16[1,4,3584]{2,1,0:T(4,128)(2,1)} %param.7) | copy-start | bytes 86020

commit v12 on v11

--- a/solution.py
+++ b/solution.py
@@ -18,6 +18,7 @@
 TIGHT = ALONG * MOST
 MIB = 1024 * 1024
 CHUNK = 1024
+PIECES = 7
 
 
 def crossed_groups(ep, first):
@@ -101,30 +102,36 @@
 
 
 def gate(
-    rows_ref, gain_ref, own_ref, other_hbm, kept_ref, sent_ref, squares_ref, scaled_ref, other_ref, sem
+    rows_ref, gain_ref, own_ref, other_hbm, kept_ref, sent_ref, squares_ref, other_ref, sems
 ):
-    copy = pltpu.make_async_copy(other_hbm, other_ref, sem)
-    copy.start()
     half_width, cols = own_ref.shape[0], kept_ref.shape[1]
     rows = rows_ref.shape[0]
-    deep = half_width // 7
-    for k in range(7):
+    deep = half_width // PIECES
+    copies = []
+    for k in range(PIECES):
+        at = pl.ds(k * deep, deep)
+        copies.append(pltpu.make_async_copy(other_hbm.at[at], other_ref.at[at], sems.at[k]))
+        copies[k].start()
+    for k in range(PIECES):
         at = slice(k * deep, (k + 1) * deep)
         values = rows_ref[:, at].astype(F32)
-        part = jnp.sum(values * values, axis=1, keepdims=True)
-        squares_ref[...] = jnp.broadcast_to(part, squares_ref.shape) + (
-            squares_ref[...] if k else 0.0
-        )
+        pieces = values * values
+        part = pieces[:, :EXTRA]
+        for lo in range(EXTRA, deep, EXTRA):
+            part = part + pieces[:, lo : lo + EXTRA]
+        squares_ref[...] = part + (squares_ref[...] if k else 0.0)
         scaled = (values * gain_ref[:, at].astype(F32)).astype(BF16)
-        scaled_ref[:, at] = scaled
         sums = jnp.dot(scaled, own_ref[at, :], preferred_element_type=F32)
         kept_ref[:, : cols // 2] = sums + (kept_ref[:, : cols // 2] if k else 0.0)
-    copy.wait()
-    kept_ref[:, cols // 2 :] = jnp.dot(scaled_ref[...], other_ref[...], preferred_element_type=F32)
+        copies[k].wait()
+        sums = jnp.dot(scaled, other_ref[at, :], preferred_element_type=F32)
+        kept_ref[:, cols // 2 :] = sums + (kept_ref[:, cols // 2 :] if k else 0.0)
+    squares = jnp.sum(squares_ref[...], axis=1, keepdims=True)
+    squares_ref[...] = jnp.broadcast_to(squares, squares_ref.shape)
     sent_ref[:rows] = kept_ref[...].astype(BF16)
     across = lax.broadcasted_iota(jnp.int32, (rows, cols), 1)
     down = lax.broadcasted_iota(jnp.int32, (rows, cols), 0)
-    total = jnp.sum(jnp.where(across == down, squares_ref[:, :1], 0.0), axis=0, keepdims=True)
+    total = jnp.sum(jnp.where(across == down, squares, 0.0), axis=0, keepdims=True)
     high = total.astype(BF16).astype(F32)
     row = lax.broadcasted_iota(jnp.int32, (16, cols), 0)
     sent_ref[rows:] = jnp.where(row == 0, high, jnp.where(row == 1, total - high, 0.0)).astype(BF16)
@@ -154,7 +161,9 @@
 
 def gather_parts(back_ref, parts_ref, out_ref):
     sums = jnp.dot(back_ref[...], parts_ref[...], preferred_element_type=F32)
-    out_ref[...] = (sums[:WIDE] + sums[WIDE:]).astype(BF16)
+    sums = (sums[:WIDE] + sums[WIDE:]).astype(BF16)
+    for t in range(ALONG):
+        out_ref[t] = sums[t * ROWS : (t + 1) * ROWS]
 
 
 def finish(parts_ref, rows_ref, out_ref, sent_ref):
@@ -257,9 +266,8 @@
         gate_other,
         spaces=[pltpu.VMEM] * 3 + [pl.ANY],
         scratch=[
-            pltpu.VMEM((total, half_width), BF16),
             pltpu.VMEM((half_width, cols), BF16),
-            pltpu.SemaphoreType.DMA,
+            pltpu.SemaphoreType.DMA((PIECES,)),
         ],
     )
     got = lax.ppermute(sent, "tp", swap)
@@ -272,8 +280,8 @@
         down_all,
     )
     returned = traded(parts.reshape(ALONG, TIGHT, half_width), far).reshape(total, half_width)
-    (summed,) = local(gather_parts, [shape(WIDE, half_width)], far_back, returned)
-    home = traded(summed.reshape(ALONG, ROWS, half_width), near)
+    (summed,) = local(gather_parts, [shape(ALONG, ROWS, half_width)], far_back, returned)
+    home = traded(summed, near)
     layer_out, leaving = local(
         finish, [shape(ROWS, half_width), shape(4, ROWS, full)], home, rows
     )

time: 114 us -> 114 us (level)
  no operation moved by 1% of the time
where the time goes in v12:
time: 114 us; the launch traced here: 113 us
  blocking collectives  63.7 us (56%)
  starting transfers between devices  21.1 us (19%)
  waiting for transfers between devices  18 us (16%)
  Pallas kernels  8.09 us (7%)
  other arithmetic  1.3 us (1%)
    all_to_all x3, blocking collectives, traded(): lax.all_to_all(block, 'ep', 0, 0, axis_index_groups=groups, tiled=True)  54.7 us
    all_to_all x1, waiting for transfers between devices, traded(): lax.all_to_all(block, 'ep', 0, 0, axis_index_groups=groups, tiled=True)  11 us
    all_to_all x1, starting transfers between devices, traded(): lax.all_to_all(block, 'ep', 0, 0, axis_index_groups=groups, tiled=True)  10.3 us
    all_to_all x1, blocking collectives, body(): got = lax.all_to_all(leaving, ('section', 'tp'), 0, 0, tiled=True)  9.07 us
    pallas_call x7, Pallas kernels, local(): pl.pallas_call(kernel, out_shape=outs, in_specs=[pl.BlockSpec(memory_spac...  8.09 us
    ppermute x1, starting transfers between devices, body(): gain_other = lax.ppermute(out_gain, 'section', swap)  4.04 us
    ppermute x1, waiting for transfers between devices, body(): got = lax.ppermute(sent, 'tp', swap)  3.96 us
    ppermute x1, waiting for transfers between devices, body(): gain_other = lax.ppermute(out_gain, 'section', swap)  3.07 us
  transfers between devices with their start and end apart: 5, of which 3 were waited for; matrix products, arithmetic and copies ran while one was open for 1% of the time, Pallas kernels for 2%

profile of v12, /device:TPU:2, one launch (start us, length us, event | category | flops | bytes accessed | tf_op | source)
XLA Modules:
  0.0 113.1 jit_solution(7143504315772848204)
XLA Ops:
  0.6 1.6 %shard_map.86 = bf16[8,4,3712]{2,1,0:T(4,128)(2,1)} custom-call(bf16[4,3584]{1,0:T(4,128)(2,1)} %bitcast.16, s32[4,4]{1,0:T(4,128)} %bitcast.22, f32[4,4]{1,0:T(4,128)} %bitcast.23), custom_call_target="tpu_custom_call" | custom-call | tf_op jit(solution)/shard_map/pallas_call | solution.py:199
  2.2 17.3 %all_to_all.25 = bf16[8,4,3712]{2,1,0:T(4,128)(2,1)S(1)} all-to-all(bf16[8,4,3712]{2,1,0:T(4,128)(2,1)} %shard_map.86), channel_id=1, replica_groups={{2,6,10,14,18,22,26,30},{34,38,42,46,50,54,58,62},{66,70,74,78,82,86,90..., dimensions={0} | all-to-all | bytes 475136 | tf_op jit(solution)/shard_map/all_to_all | solution.py:33
  19.5 0.1 reshape.19.rows_ref
  19.6 1.6 %shard_map.87 = (bf16[192,3584]{1,0:T(8,128)(2,1)}, bf16[64,192]{1,0:T(8,128)(2,1)S(1)}) custom-call(bf16[32,3712]{1,0:T(8,128)(2,1)S(1)} %reshape.19.rows_ref), custom_call_target="tpu_custom_call" | custom-call | tf_op jit(solution)/shard_map/pallas_call | solution.py:199
  21.2 10.3 %all-to-all-start.1 = ((bf16[8,24,3584]{2,1,0:T(8,128)(2,1)}), bf16[8,24,3584]{2,1,0:T(8,128)(2,1)S(1)}, u32[]{:S(2)}, u32[]{:S(2)}) async-start(bf16[8,24,3584]{2,1,0:T(8,128)(2,1)} %bitcast.18), calls=%async_computation.1 | async-start | bytes 2752512 | tf_op jit(solution)/shard_map/all_to_all | solution.py:33
  31.5 1.9 %collective-permute-start.1 = (bf16[3584,256]{1,0:T(8,128)(2,1)S(1)}, bf16[3584,256]{1,0:T(8,128)(2,1)}, u32[]{:S(2)}, u32[]{:S(2)}) collective-permute-start(bf16[3584,256]{1,0:T(8,128)(2,1)S(1)} %bitcast.14), channel_id=1, source_target_pairs={{0,2},{2,0},{4,6},{6,4},{8,10},{10,8},{12,14},{14,12},{16,18},{18,... | collective-permute-start | bytes 5505032 | tf_op jit(solution)/shard_map/ppermute | solution.py:227
  33.5 2.4 %collective-permute-start.3 = (bf16[128,3584]{1,0:T(8,128)(2,1)}, bf16[128,3584]{1,0:T(8,128)(2,1)}, u32[]{:S(2)}, u32[]{:S(2)}) collective-permute-start(bf16[128,3584]{1,0:T(8,128)(2,1)} %bitcast.19), channel_id=1, source_target_pairs={{0,2},{2,0},{4,6},{6,4},{8,10},{10,8},{12,14},{14,12},{16,18},{18,... | collective-permute-start | bytes 2752520 | tf_op jit(solution)/shard_map/ppermute | solution.py:228
  35.9 4.0 %collective-permute-start = (bf16[1,3584]{1,0:T(2,128)(2,1)S(1)}, bf16[1,3584]{1,0:T(2,128)(2,1)S(1)}, u32[]{:S(2)}, u32[]{:S(2)}) collective-permute-start(bf16[1,3584]{1,0:T(2,128)(2,1)S(1)} %copy-done.4), channel_id=1, source_target_pairs={{0,256},{256,0},{1,257},{257,1},{2,258},{258,2},{3,259},{259,3},{4... | collective-permute-start | bytes 21512 | tf_op jit(solution)/shard_map/ppermute | solution.py:229
  39.9 3.1 %collective-permute-done.gain_ref = bf16[1,3584]{1,0:T(2,128)(2,1)S(1)} collective-permute-done((bf16[1,3584]{1,0:T(2,128)(2,1)S(1)}, bf16[1,3584]{1,0:T(2,128)(2,1)S(1)}, u32[]{:S(2)}, u32[]{:S(2)}) %collective-permute-start) | collective-permute-done | bytes 7200 | tf_op jit(solution)/shard_map/ppermute | solution.py:229
  43.0 11.0 %all-to-all-done.1 = bf16[8,24,3584]{2,1,0:T(8,128)(2,1)S(1)} async-done(((bf16[8,24,3584]{2,1,0:T(8,128)(2,1)}), bf16[8,24,3584]{2,1,0:T(8,128)(2,1)S(1)}, u32[]{:S(2)}, u32[]{:S(2)}) %all-to-all-start.1) | async-done | bytes 1376288 | tf_op jit(solution)/shard_map/all_to_all | solution.py:33
  54.0 0.0 collective-permute-done.1.other_hbm
  54.0 2.4 %shard_map.88 = (f32[192,512]{1,0:T(8,128)S(1)}, bf16[208,512]{1,0:T(8,128)(2,1)S(1)}, f32[192,128]{1,0:T(8,128)S(1)}) custom-call(bf16[192,3584]{1,0:T(8,128)(2,1)S(1)} %bitcast.11, bf16[1,3584]{1,0:T(2,128)(2,1)S(1)} %copy-done.2, bf16[3584,256]{1,0:T(8,128)(2,1)S(1)} %bitcast.15, bf16[3584,256]{1,0:T(8,128)(2,1)} %collective-permute-done.1.other_hbm), custom_call_target="tpu_custom_call" | custom-call | tf_op jit(solution)/shard_map/pallas_call | solution.py:199
  56.4 2.4 %collective-permute-start.2 = (bf16[208,512]{1,0:T(8,128)(2,1)S(1)}, bf16[208,512]{1,0:T(8,128)(2,1)S(1)}, u32[]{:S(2)}, u32[]{:S(2)}) collective-permute-start(bf16[208,512]{1,0:T(8,128)(2,1)S(1)} %get-tuple-element.16), channel_id=1, source_target_pairs={{0,1},{1,0},{2,3},{3,2},{4,5},{5,4},{6,7},{7,6},{8,9},{9,8},{10,11... | collective-permute-start | bytes 638984 | tf_op jit(solution)/shard_map/ppermute | solution.py:273
  58.9 0.0 collective-permute-done.3
  58.9 1.3 %pad_maximum_fusion.down_ref = bf16[256,3584]{1,0:T(8,128)(2,1)S(1)} fusion(bf16[128,3584]{1,0:T(8,128)(2,1)} %collective-permute-done.3, bf16[128,3584]{1,0:T(8,128)(2,1)S(1)} %bitcast.20), kind=kLoop, calls=%fused_computation | loop fusion | flops 3670016 | bytes 3670016 | tf_op jit(solution)/shard_map/concatenate | solution.py:231
  60.2 4.0 %collective-permute-done.2.got_ref = bf16[208,512]{1,0:T(8,128)(2,1)S(1)} collective-permute-done((bf16[208,512]{1,0:T(8,128)(2,1)S(1)}, bf16[208,512]{1,0:T(8,128)(2,1)S(1)}, u32[]{:S(2)}, u32[]{:S(2)}) %collective-permute-start.2) | collective-permute-done | bytes 213024 | tf_op jit(solution)/shard_map/ppermute | solution.py:273
  64.1 0.8 shard_map.89
  64.9 0.0 copy-start.1
  64.9 24.8 %all_to_all.26 = bf16[8,24,3584]{2,1,0:T(8,128)(2,1)S(1)} all-to-all(bf16[8,24,3584]{2,1,0:T(8,128)(2,1)S(1)} %bitcast.13), channel_id=1, replica_groups={{0,4,8,12,16,20,24,28},{32,36,40,44,48,52,56,60},{64,68,72,76,80,84,88,..., dimensions={0} | all-to-all | bytes 2752512 | tf_op jit(solution)/shard_map/all_to_all | solution.py:33
  89.7 0.4 shard_map.90
  90.1 12.5 %all_to_all.27.parts_ref = bf16[8,4,3584]{2,1,0:T(4,128)(2,1)S(1)} all-to-all(bf16[8,4,3584]{2,1,0:T(4,128)(2,1)S(1)} %shard_map.90), channel_id=1, replica_groups={{2,6,10,14,18,22,26,30},{34,38,42,46,50,54,58,62},{66,70,74,78,82,86,90..., dimensions={0} | all-to-all | bytes 458752 | tf_op jit(solution)/shard_map/all_to_all | solution.py:33
  102.6 0.7 shard_map.91
  103.3 9.1 %all_to_all.28.got_ref = bf16[4,4,3712]{2,1,0:T(4,128)(2,1)S(1)} all-to-all(bf16[4,4,3712]{2,1,0:T(4,128)(2,1)S(1)} %get-tuple-element.18), channel_id=1, replica_groups=mesh['section'=2,'ep'=128,'tp'=2] {'section','tp'}, dimensions={0} | all-to-all | bytes 237568 | tf_op jit(solution)/shard_map/all_to_all | solution.py:288
  112.4 0.7 shard_map.92
  (9 shorter events, 0.0 us)
Async XLA Ops:
  19.5 12.0 %copy-start = (bf16[1,1,3584,256]{3,2,1,0:T(8,128)(2,1)S(1)}, bf16[1,1,3584,256]{3,2,1,0:T(8,128)(2,1)}, u32[]{:S(2)}) copy-start(bf16[1,1,3584,256]{3,2,1,0:T(8,128)(2,1)} %param.11) | copy-start | bytes 5505028
  19.5 16.4 %copy-start.4 = (bf16[1,3584]{1,0:T(2,128)(2,1)S(1)}, bf16[1,3584]{1,0:T(2,128)(2,1)}, u32[]{:S(2)}) copy-start(bf16[1,3584]{1,0:T(2,128)(2,1)} %param.13) | copy-start | bytes 21508
  19.5 34.5 %copy-start.2 = (bf16[1,3584]{1,0:T(2,128)(2,1)S(1)}, bf16[1,3584]{1,0:T(2,128)(2,1)}, u32[]{:S(2)}) copy-start(bf16[1,3584]{1,0:T(2,128)(2,1)} %gain_ref.1) | copy-start | bytes 21508
  21.2 32.8 %all-to-all-start.1 = ((bf16[8,24,3584]{2,1,0:T(8,128)(2,1)}), bf16[8,24,3584]{2,1,0:T(8,128)(2,1)S(1)}, u32[]{:S(2)}, u32[]{:S(2)}) async-start(bf16[8,24,3584]{2,1,0:T(8,128)(2,1)} %bitcast.18), calls=%async_computation.1 | async-start | bytes 2752512 | tf_op jit(solution)/shard_map/all_to_all | solution.py:33
  31.5 22.5 %collective-permute-start.1 = (bf16[3584,256]{1,0:T(8,128)(2,1)S(1)}, bf16[3584,256]{1,0:T(8,128)(2,1)}, u32[]{:S(2)}, u32[]{:S(2)}) collective-permute-start(bf16[3584,256]{1,0:T(8,128)(2,1)S(1)} %bitcast.14), channel_id=1, source_target_pairs={{0,2},{2,0},{4,6},{6,4},{8,10},{10,8},{12,14},{14,12},{16,18},{18,... | collective-permute-start | bytes 5505032 | tf_op jit(solution)/shard_map/ppermute | solution.py:227
  33.5 25.4 %collective-permute-start.3 = (bf16[128,3584]{1,0:T(8,128)(2,1)}, bf16[128,3584]{1,0:T(8,128)(2,1)}, u32[]{:S(2)}, u32[]{:S(2)}) collective-permute-start(bf16[128,3584]{1,0:T(8,128)(2,1)} %bitcast.19), channel_id=1, source_target_pairs={{0,2},{2,0},{4,6},{6,4},{8,10},{10,8},{12,14},{14,12},{16,18},{18,... | collective-permute-start | bytes 2752520 | tf_op jit(solution)/shard_map/ppermute | solution.py:228
  35.9 7.1 %collective-permute-start = (bf16[1,3584]{1,0:T(2,128)(2,1)S(1)}, bf16[1,3584]{1,0:T(2,128)(2,1)S(1)}, u32[]{:S(2)}, u32[]{:S(2)}) collective-permute-start(bf16[1,3584]{1,0:T(2,128)(2,1)S(1)} %copy-done.4), channel_id=1, source_target_pairs={{0,256},{256,0},{1,257},{257,1},{2,258},{258,2},{3,259},{259,3},{4... | collective-permute-start | bytes 21512 | tf_op jit(solution)/shard_map/ppermute | solution.py:229
  54.0 4.9 %copy-start.3 = (bf16[1,1,128,3584]{3,2,1,0:T(8,128)(2,1)S(1)}, bf16[1,1,128,3584]{3,2,1,0:T(8,128)(2,1)}, u32[]{:S(2)}) copy-start(bf16[1,1,128,3584]{3,2,1,0:T(8,128)(2,1)} %param.12) | copy-start | bytes 2752516
  56.4 7.7 %collective-permute-start.2 = (bf16[208,512]{1,0:T(8,128)(2,1)S(1)}, bf16[208,512]{1,0:T(8,128)(2,1)S(1)}, u32[]{:S(2)}, u32[]{:S(2)}) collective-permute-start(bf16[208,512]{1,0:T(8,128)(2,1)S(1)} %get-tuple-element.16), channel_id=1, source_target_pairs={{0,1},{1,0},{2,3},{3,2},{4,5},{5,4},{6,7},{7,6},{8,9},{9,8},{10,11... | collective-permute-start | bytes 638984 | tf_op jit(solution)/shard_map/ppermute | solution.py:273
  64.9 37.7 %copy-start.1 = (bf16[1,4,3584]{2,1,0:T(4,128)(2,1)S(1)}, bf16[1,4,3584]{2,1,0:T(4,128)(2,1)}, u32[]{:S(2)}) copy-start(bf16[1,4,3584]{2,1,0:T(4,128)(2,1)} %param.7) | copy-start | bytes 86020

commit v13 on v12

--- a/solution.py
+++ b/solution.py
@@ -17,7 +17,7 @@
 WIDE = ALONG * ROWS
 TIGHT = ALONG * MOST
 MIB = 1024 * 1024
-CHUNK = 1024
+CHUNK = 512
 PIECES = 7
 
 

time: 114 us -> 114 us (level)
  no operation moved by 1% of the time
where the time goes in v13:
time: 114 us; the launch traced here: 113 us
  blocking collectives  63.7 us (56%)
  starting transfers between devices  21.1 us (19%)
  waiting for transfers between devices  18 us (16%)
  Pallas kernels  8.08 us (7%)
  other arithmetic  1.3 us (1%)
    all_to_all x3, blocking collectives, traded(): lax.all_to_all(block, 'ep', 0, 0, axis_index_groups=groups, tiled=True)  54.7 us
    all_to_all x1, waiting for transfers between devices, traded(): lax.all_to_all(block, 'ep', 0, 0, axis_index_groups=groups, tiled=True)  11 us
    all_to_all x1, starting transfers between devices, traded(): lax.all_to_all(block, 'ep', 0, 0, axis_index_groups=groups, tiled=True)  10.3 us
    all_to_all x1, blocking collectives, body(): got = lax.all_to_all(leaving, ('section', 'tp'), 0, 0, tiled=True)  9.07 us
    pallas_call x7, Pallas kernels, local(): pl.pallas_call(kernel, out_shape=outs, in_specs=[pl.BlockSpec(memory_spac...  8.08 us
    ppermute x1, starting transfers between devices, body(): gain_other = lax.ppermute(out_gain, 'section', swap)  4.04 us
    ppermute x1, waiting for transfers between devices, body(): got = lax.ppermute(sent, 'tp', swap)  3.96 us
    ppermute x1, waiting for transfers between devices, body(): gain_other = lax.ppermute(out_gain, 'section', swap)  3.07 us
  transfers between devices with their start and end apart: 5, of which 3 were waited for; matrix products, arithmetic and copies ran while one was open for 1% of the time, Pallas kernels for 2%

profile of v13, /device:TPU:2, one launch (start us, length us, event | category | flops | bytes accessed | tf_op | source)
XLA Modules:
  0.0 113.1 jit_solution(14855347516231650433)
XLA Ops:
  0.6 1.6 %shard_map.86 = bf16[8,4,3712]{2,1,0:T(4,128)(2,1)} custom-call(bf16[4,3584]{1,0:T(4,128)(2,1)} %bitcast.16, s32[4,4]{1,0:T(4,128)} %bitcast.22, f32[4,4]{1,0:T(4,128)} %bitcast.23), custom_call_target="tpu_custom_call" | custom-call | tf_op jit(solution)/shard_map/pallas_call | solution.py:199
  2.2 17.3 %all_to_all.25 = bf16[8,4,3712]{2,1,0:T(4,128)(2,1)S(1)} all-to-all(bf16[8,4,3712]{2,1,0:T(4,128)(2,1)} %shard_map.86), channel_id=1, replica_groups={{2,6,10,14,18,22,26,30},{34,38,42,46,50,54,58,62},{66,70,74,78,82,86,90..., dimensions={0} | all-to-all | bytes 475136 | tf_op jit(solution)/shard_map/all_to_all | solution.py:33
  19.5 0.1 reshape.19.rows_ref
  19.6 1.6 %shard_map.87 = (bf16[192,3584]{1,0:T(8,128)(2,1)}, bf16[64,192]{1,0:T(8,128)(2,1)S(1)}) custom-call(bf16[32,3712]{1,0:T(8,128)(2,1)S(1)} %reshape.19.rows_ref), custom_call_target="tpu_custom_call" | custom-call | tf_op jit(solution)/shard_map/pallas_call | solution.py:199
  21.2 10.3 %all-to-all-start.1 = ((bf16[8,24,3584]{2,1,0:T(8,128)(2,1)}), bf16[8,24,3584]{2,1,0:T(8,128)(2,1)S(1)}, u32[]{:S(2)}, u32[]{:S(2)}) async-start(bf16[8,24,3584]{2,1,0:T(8,128)(2,1)} %bitcast.18), calls=%async_computation.1 | async-start | bytes 2752512 | tf_op jit(solution)/shard_map/all_to_all | solution.py:33
  31.5 1.9 %collective-permute-start.1 = (bf16[3584,256]{1,0:T(8,128)(2,1)S(1)}, bf16[3584,256]{1,0:T(8,128)(2,1)}, u32[]{:S(2)}, u32[]{:S(2)}) collective-permute-start(bf16[3584,256]{1,0:T(8,128)(2,1)S(1)} %bitcast.14), channel_id=1, source_target_pairs={{0,2},{2,0},{4,6},{6,4},{8,10},{10,8},{12,14},{14,12},{16,18},{18,... | collective-permute-start | bytes 5505032 | tf_op jit(solution)/shard_map/ppermute | solution.py:227
  33.4 2.4 %collective-permute-start.3 = (bf16[128,3584]{1,0:T(8,128)(2,1)}, bf16[128,3584]{1,0:T(8,128)(2,1)}, u32[]{:S(2)}, u32[]{:S(2)}) collective-permute-start(bf16[128,3584]{1,0:T(8,128)(2,1)} %bitcast.19), channel_id=1, source_target_pairs={{0,2},{2,0},{4,6},{6,4},{8,10},{10,8},{12,14},{14,12},{16,18},{18,... | collective-permute-start | bytes 2752520 | tf_op jit(solution)/shard_map/ppermute | solution.py:228
  35.9 4.0 %collective-permute-start = (bf16[1,3584]{1,0:T(2,128)(2,1)S(1)}, bf16[1,3584]{1,0:T(2,128)(2,1)S(1)}, u32[]{:S(2)}, u32[]{:S(2)}) collective-permute-start(bf16[1,3584]{1,0:T(2,128)(2,1)S(1)} %copy-done.4), channel_id=1, source_target_pairs={{0,256},{256,0},{1,257},{257,1},{2,258},{258,2},{3,259},{259,3},{4... | collective-permute-start | bytes 21512 | tf_op jit(solution)/shard_map/ppermute | solution.py:229
  39.9 3.1 %collective-permute-done.gain_ref = bf16[1,3584]{1,0:T(2,128)(2,1)S(1)} collective-permute-done((bf16[1,3584]{1,0:T(2,128)(2,1)S(1)}, bf16[1,3584]{1,0:T(2,128)(2,1)S(1)}, u32[]{:S(2)}, u32[]{:S(2)}) %collective-permute-start) | collective-permute-done | bytes 7200 | tf_op jit(solution)/shard_map/ppermute | solution.py:229
  43.0 11.0 %all-to-all-done.1 = bf16[8,24,3584]{2,1,0:T(8,128)(2,1)S(1)} async-done(((bf16[8,24,3584]{2,1,0:T(8,128)(2,1)}), bf16[8,24,3584]{2,1,0:T(8,128)(2,1)S(1)}, u32[]{:S(2)}, u32[]{:S(2)}) %all-to-all-start.1) | async-done | bytes 1376288 | tf_op jit(solution)/shard_map/all_to_all | solution.py:33
  54.0 0.0 collective-permute-done.1.other_hbm
  54.0 2.4 %shard_map.88 = (f32[192,512]{1,0:T(8,128)S(1)}, bf16[208,512]{1,0:T(8,128)(2,1)S(1)}, f32[192,128]{1,0:T(8,128)S(1)}) custom-call(bf16[192,3584]{1,0:T(8,128)(2,1)S(1)} %bitcast.11, bf16[1,3584]{1,0:T(2,128)(2,1)S(1)} %copy-done.2, bf16[3584,256]{1,0:T(8,128)(2,1)S(1)} %bitcast.15, bf16[3584,256]{1,0:T(8,128)(2,1)} %collective-permute-done.1.other_hbm), custom_call_target="tpu_custom_call" | custom-call | tf_op jit(solution)/shard_map/pallas_call | solution.py:199
  56.4 2.4 %collective-permute-start.2 = (bf16[208,512]{1,0:T(8,128)(2,1)S(1)}, bf16[208,512]{1,0:T(8,128)(2,1)S(1)}, u32[]{:S(2)}, u32[]{:S(2)}) collective-permute-start(bf16[208,512]{1,0:T(8,128)(2,1)S(1)} %get-tuple-element.16), channel_id=1, source_target_pairs={{0,1},{1,0},{2,3},{3,2},{4,5},{5,4},{6,7},{7,6},{8,9},{9,8},{10,11... | collective-permute-start | bytes 638984 | tf_op jit(solution)/shard_map/ppermute | solution.py:273
  58.8 0.0 collective-permute-done.3
  58.9 1.3 %pad_maximum_fusion.down_ref = bf16[256,3584]{1,0:T(8,128)(2,1)S(1)} fusion(bf16[128,3584]{1,0:T(8,128)(2,1)} %collective-permute-done.3, bf16[128,3584]{1,0:T(8,128)(2,1)S(1)} %bitcast.20), kind=kLoop, calls=%fused_computation | loop fusion | flops 3670016 | bytes 3670016 | tf_op jit(solution)/shard_map/concatenate | solution.py:231
  60.2 4.0 %collective-permute-done.2.got_ref = bf16[208,512]{1,0:T(8,128)(2,1)S(1)} collective-permute-done((bf16[208,512]{1,0:T(8,128)(2,1)S(1)}, bf16[208,512]{1,0:T(8,128)(2,1)S(1)}, u32[]{:S(2)}, u32[]{:S(2)}) %collective-permute-start.2) | collective-permute-done | bytes 213024 | tf_op jit(solution)/shard_map/ppermute | solution.py:273
  64.1 0.8 shard_map.89
  64.9 0.0 copy-start.1
  64.9 24.8 %all_to_all.26 = bf16[8,24,3584]{2,1,0:T(8,128)(2,1)S(1)} all-to-all(bf16[8,24,3584]{2,1,0:T(8,128)(2,1)S(1)} %bitcast.13), channel_id=1, replica_groups={{0,4,8,12,16,20,24,28},{32,36,40,44,48,52,56,60},{64,68,72,76,80,84,88,..., dimensions={0} | all-to-all | bytes 2752512 | tf_op jit(solution)/shard_map/all_to_all | solution.py:33
  89.7 0.4 shard_map.90
  90.1 12.5 %all_to_all.27.parts_ref = bf16[8,4,3584]{2,1,0:T(4,128)(2,1)S(1)} all-to-all(bf16[8,4,3584]{2,1,0:T(4,128)(2,1)S(1)} %shard_map.90), channel_id=1, replica_groups={{2,6,10,14,18,22,26,30},{34,38,42,46,50,54,58,62},{66,70,74,78,82,86,90..., dimensions={0} | all-to-all | bytes 458752 | tf_op jit(solution)/shard_map/all_to_all | solution.py:33
  102.6 0.7 shard_map.91
  103.3 9.1 %all_to_all.28.got_ref = bf16[4,4,3712]{2,1,0:T(4,128)(2,1)S(1)} all-to-all(bf16[4,4,3712]{2,1,0:T(4,128)(2,1)S(1)} %get-tuple-element.18), channel_id=1, replica_groups=mesh['section'=2,'ep'=128,'tp'=2] {'section','tp'}, dimensions={0} | all-to-all | bytes 237568 | tf_op jit(solution)/shard_map/all_to_all | solution.py:288
  112.4 0.7 shard_map.92
  (9 shorter events, 0.0 us)
Async XLA Ops:
  19.5 12.0 %copy-start = (bf16[1,1,3584,256]{3,2,1,0:T(8,128)(2,1)S(1)}, bf16[1,1,3584,256]{3,2,1,0:T(8,128)(2,1)}, u32[]{:S(2)}) copy-start(bf16[1,1,3584,256]{3,2,1,0:T(8,128)(2,1)} %param.11) | copy-start | bytes 5505028
  19.5 16.4 %copy-start.4 = (bf16[1,3584]{1,0:T(2,128)(2,1)S(1)}, bf16[1,3584]{1,0:T(2,128)(2,1)}, u32[]{:S(2)}) copy-start(bf16[1,3584]{1,0:T(2,128)(2,1)} %param.13) | copy-start | bytes 21508
  19.5 34.5 %copy-start.2 = (bf16[1,3584]{1,0:T(2,128)(2,1)S(1)}, bf16[1,3584]{1,0:T(2,128)(2,1)}, u32[]{:S(2)}) copy-start(bf16[1,3584]{1,0:T(2,128)(2,1)} %gain_ref.1) | copy-start | bytes 21508
  21.2 32.8 %all-to-all-start.1 = ((bf16[8,24,3584]{2,1,0:T(8,128)(2,1)}), bf16[8,24,3584]{2,1,0:T(8,128)(2,1)S(1)}, u32[]{:S(2)}, u32[]{:S(2)}) async-start(bf16[8,24,3584]{2,1,0:T(8,128)(2,1)} %bitcast.18), calls=%async_computation.1 | async-start | bytes 2752512 | tf_op jit(solution)/shard_map/all_to_all | solution.py:33
  31.5 22.5 %collective-permute-start.1 = (bf16[3584,256]{1,0:T(8,128)(2,1)S(1)}, bf16[3584,256]{1,0:T(8,128)(2,1)}, u32[]{:S(2)}, u32[]{:S(2)}) collective-permute-start(bf16[3584,256]{1,0:T(8,128)(2,1)S(1)} %bitcast.14), channel_id=1, source_target_pairs={{0,2},{2,0},{4,6},{6,4},{8,10},{10,8},{12,14},{14,12},{16,18},{18,... | collective-permute-start | bytes 5505032 | tf_op jit(solution)/shard_map/ppermute | solution.py:227
  33.4 25.4 %collective-permute-start.3 = (bf16[128,3584]{1,0:T(8,128)(2,1)}, bf16[128,3584]{1,0:T(8,128)(2,1)}, u32[]{:S(2)}, u32[]{:S(2)}) collective-permute-start(bf16[128,3584]{1,0:T(8,128)(2,1)} %bitcast.19), channel_id=1, source_target_pairs={{0,2},{2,0},{4,6},{6,4},{8,10},{10,8},{12,14},{14,12},{16,18},{18,... | collective-permute-start | bytes 2752520 | tf_op jit(solution)/shard_map/ppermute | solution.py:228
  35.9 7.1 %collective-permute-start = (bf16[1,3584]{1,0:T(2,128)(2,1)S(1)}, bf16[1,3584]{1,0:T(2,128)(2,1)S(1)}, u32[]{:S(2)}, u32[]{:S(2)}) collective-permute-start(bf16[1,3584]{1,0:T(2,128)(2,1)S(1)} %copy-done.4), channel_id=1, source_target_pairs={{0,256},{256,0},{1,257},{257,1},{2,258},{258,2},{3,259},{259,3},{4... | collective-permute-start | bytes 21512 | tf_op jit(solution)/shard_map/ppermute | solution.py:229
  54.0 4.9 %copy-start.3 = (bf16[1,1,128,3584]{3,2,1,0:T(8,128)(2,1)S(1)}, bf16[1,1,128,3584]{3,2,1,0:T(8,128)(2,1)}, u32[]{:S(2)}) copy-start(bf16[1,1,128,3584]{3,2,1,0:T(8,128)(2,1)} %param.12) | copy-start | bytes 2752516
  56.4 7.7 %collective-permute-start.2 = (bf16[208,512]{1,0:T(8,128)(2,1)S(1)}, bf16[208,512]{1,0:T(8,128)(2,1)S(1)}, u32[]{:S(2)}, u32[]{:S(2)}) collective-permute-start(bf16[208,512]{1,0:T(8,128)(2,1)S(1)} %get-tuple-element.16), channel_id=1, source_target_pairs={{0,1},{1,0},{2,3},{3,2},{4,5},{5,4},{6,7},{7,6},{8,9},{9,8},{10,11... | collective-permute-start | bytes 638984 | tf_op jit(solution)/shard_map/ppermute | solution.py:273
  64.9 37.7 %copy-start.1 = (bf16[1,4,3584]{2,1,0:T(4,128)(2,1)S(1)}, bf16[1,4,3584]{2,1,0:T(4,128)(2,1)}, u32[]{:S(2)}) copy-start(bf16[1,4,3584]{2,1,0:T(4,128)(2,1)} %param.7) | copy-start | bytes 86020

commit v14 on v12

--- a/solution.py
+++ b/solution.py
@@ -153,8 +153,8 @@
         b = (kept_ref[:, lo : lo + units] + got_ref[:rows, lo : lo + units].astype(F32)) * scale
         hidden.append((a / (1.0 + jnp.exp(-a)) * b).astype(BF16))
     both = jnp.concatenate(hidden, axis=1)
-    deep = half_width // 4
-    for k in range(4):
+    deep = half_width // 2
+    for k in range(2):
         at = slice(k * deep, (k + 1) * deep)
         out_ref[:, at] = jnp.dot(both, down_ref[:, at], preferred_element_type=F32).astype(BF16)
 

time: 114 us -> 114 us (level)
  no operation moved by 1% of the time
where the time goes in v14:
time: 114 us; the launch traced here: 113 us
  blocking collectives  63.7 us (56%)
  starting transfers between devices  21.1 us (19%)
  waiting for transfers between devices  18 us (16%)
  Pallas kernels  8.03 us (7%)
  other arithmetic  1.3 us (1%)
    all_to_all x3, blocking collectives, traded(): lax.all_to_all(block, 'ep', 0, 0, axis_index_groups=groups, tiled=True)  54.7 us
    all_to_all x1, waiting for transfers between devices, traded(): lax.all_to_all(block, 'ep', 0, 0, axis_index_groups=groups, tiled=True)  11 us
    all_to_all x1, starting transfers between devices, traded(): lax.all_to_all(block, 'ep', 0, 0, axis_index_groups=groups, tiled=True)  10.3 us
    all_to_all x1, blocking collectives, body(): got = lax.all_to_all(leaving, ('section', 'tp'), 0, 0, tiled=True)  9.07 us
    pallas_call x7, Pallas kernels, local(): pl.pallas_call(kernel, out_shape=outs, in_specs=[pl.BlockSpec(memory_spac...  8.03 us
    ppermute x1, starting transfers between devices, body(): gain_other = lax.ppermute(out_gain, 'section', swap)  4.04 us
    ppermute x1, waiting for transfers between devices, body(): got = lax.ppermute(sent, 'tp', swap)  3.96 us
    ppermute x1, waiting for transfers between devices, body(): gain_other = lax.ppermute(out_gain, 'section', swap)  3.07 us
  transfers between devices with their start and end apart: 5, of which 3 were waited for; matrix products, arithmetic and copies ran while one was open for 1% of the time, Pallas kernels for 2%

profile of v14, /device:TPU:2, one launch (start us, length us, event | category | flops | bytes accessed | tf_op | source)
XLA Modules:
  0.0 113.0 jit_solution(14658727308826040681)
XLA Ops:
  0.6 1.6 %shard_map.86 = bf16[8,4,3712]{2,1,0:T(4,128)(2,1)} custom-call(bf16[4,3584]{1,0:T(4,128)(2,1)} %bitcast.16, s32[4,4]{1,0:T(4,128)} %bitcast.22, f32[4,4]{1,0:T(4,128)} %bitcast.23), custom_call_target="tpu_custom_call" | custom-call | tf_op jit(solution)/shard_map/pallas_call | solution.py:199
  2.2 17.3 %all_to_all.25 = bf16[8,4,3712]{2,1,0:T(4,128)(2,1)S(1)} all-to-all(bf16[8,4,3712]{2,1,0:T(4,128)(2,1)} %shard_map.86), channel_id=1, replica_groups={{2,6,10,14,18,22,26,30},{34,38,42,46,50,54,58,62},{66,70,74,78,82,86,90..., dimensions={0} | all-to-all | bytes 475136 | tf_op jit(solution)/shard_map/all_to_all | solution.py:33
  19.5 0.1 reshape.19.rows_ref
  19.6 1.6 %shard_map.87 = (bf16[192,3584]{1,0:T(8,128)(2,1)}, bf16[64,192]{1,0:T(8,128)(2,1)S(1)}) custom-call(bf16[32,3712]{1,0:T(8,128)(2,1)S(1)} %reshape.19.rows_ref), custom_call_target="tpu_custom_call" | custom-call | tf_op jit(solution)/shard_map/pallas_call | solution.py:199
  21.2 10.3 %all-to-all-start.1 = ((bf16[8,24,3584]{2,1,0:T(8,128)(2,1)}), bf16[8,24,3584]{2,1,0:T(8,128)(2,1)S(1)}, u32[]{:S(2)}, u32[]{:S(2)}) async-start(bf16[8,24,3584]{2,1,0:T(8,128)(2,1)} %bitcast.18), calls=%async_computation.1 | async-start | bytes 2752512 | tf_op jit(solution)/shard_map/all_to_all | solution.py:33
  31.5 1.9 %collective-permute-start.1 = (bf16[3584,256]{1,0:T(8,128)(2,1)S(1)}, bf16[3584,256]{1,0:T(8,128)(2,1)}, u32[]{:S(2)}, u32[]{:S(2)}) collective-permute-start(bf16[3584,256]{1,0:T(8,128)(2,1)S(1)} %bitcast.14), channel_id=1, source_target_pairs={{0,2},{2,0},{4,6},{6,4},{8,10},{10,8},{12,14},{14,12},{16,18},{18,... | collective-permute-start | bytes 5505032 | tf_op jit(solution)/shard_map/ppermute | solution.py:227
  33.5 2.4 %collective-permute-start.3 = (bf16[128,3584]{1,0:T(8,128)(2,1)}, bf16[128,3584]{1,0:T(8,128)(2,1)}, u32[]{:S(2)}, u32[]{:S(2)}) collective-permute-start(bf16[128,3584]{1,0:T(8,128)(2,1)} %bitcast.19), channel_id=1, source_target_pairs={{0,2},{2,0},{4,6},{6,4},{8,10},{10,8},{12,14},{14,12},{16,18},{18,... | collective-permute-start | bytes 2752520 | tf_op jit(solution)/shard_map/ppermute | solution.py:228
  35.9 4.0 %collective-permute-start = (bf16[1,3584]{1,0:T(2,128)(2,1)S(1)}, bf16[1,3584]{1,0:T(2,128)(2,1)S(1)}, u32[]{:S(2)}, u32[]{:S(2)}) collective-permute-start(bf16[1,3584]{1,0:T(2,128)(2,1)S(1)} %copy-done.4), channel_id=1, source_target_pairs={{0,256},{256,0},{1,257},{257,1},{2,258},{258,2},{3,259},{259,3},{4... | collective-permute-start | bytes 21512 | tf_op jit(solution)/shard_map/ppermute | solution.py:229
  39.9 3.1 %collective-permute-done.gain_ref = bf16[1,3584]{1,0:T(2,128)(2,1)S(1)} collective-permute-done((bf16[1,3584]{1,0:T(2,128)(2,1)S(1)}, bf16[1,3584]{1,0:T(2,128)(2,1)S(1)}, u32[]{:S(2)}, u32[]{:S(2)}) %collective-permute-start) | collective-permute-done | bytes 7200 | tf_op jit(solution)/shard_map/ppermute | solution.py:229
  43.0 11.0 %all-to-all-done.1 = bf16[8,24,3584]{2,1,0:T(8,128)(2,1)S(1)} async-done(((bf16[8,24,3584]{2,1,0:T(8,128)(2,1)}), bf16[8,24,3584]{2,1,0:T(8,128)(2,1)S(1)}, u32[]{:S(2)}, u32[]{:S(2)}) %all-to-all-start.1) | async-done | bytes 1376288 | tf_op jit(solution)/shard_map/all_to_all | solution.py:33
  54.0 0.0 collective-permute-done.1.other_hbm
  54.0 2.4 %shard_map.88 = (f32[192,512]{1,0:T(8,128)S(1)}, bf16[208,512]{1,0:T(8,128)(2,1)S(1)}, f32[192,128]{1,0:T(8,128)S(1)}) custom-call(bf16[192,3584]{1,0:T(8,128)(2,1)S(1)} %bitcast.11, bf16[1,3584]{1,0:T(2,128)(2,1)S(1)} %copy-done.2, bf16[3584,256]{1,0:T(8,128)(2,1)S(1)} %bitcast.15, bf16[3584,256]{1,0:T(8,128)(2,1)} %collective-permute-done.1.other_hbm), custom_call_target="tpu_custom_call" | custom-call | tf_op jit(solution)/shard_map/pallas_call | solution.py:199
  56.4 2.4 %collective-permute-start.2 = (bf16[208,512]{1,0:T(8,128)(2,1)S(1)}, bf16[208,512]{1,0:T(8,128)(2,1)S(1)}, u32[]{:S(2)}, u32[]{:S(2)}) collective-permute-start(bf16[208,512]{1,0:T(8,128)(2,1)S(1)} %get-tuple-element.16), channel_id=1, source_target_pairs={{0,1},{1,0},{2,3},{3,2},{4,5},{5,4},{6,7},{7,6},{8,9},{9,8},{10,11... | collective-permute-start | bytes 638984 | tf_op jit(solution)/shard_map/ppermute | solution.py:273
  58.9 0.0 collective-permute-done.3
  58.9 1.3 %pad_maximum_fusion.down_ref = bf16[256,3584]{1,0:T(8,128)(2,1)S(1)} fusion(bf16[128,3584]{1,0:T(8,128)(2,1)} %collective-permute-done.3, bf16[128,3584]{1,0:T(8,128)(2,1)S(1)} %bitcast.20), kind=kLoop, calls=%fused_computation | loop fusion | flops 3670016 | bytes 3670016 | tf_op jit(solution)/shard_map/concatenate | solution.py:231
  60.2 4.0 %collective-permute-done.2.got_ref = bf16[208,512]{1,0:T(8,128)(2,1)S(1)} collective-permute-done((bf16[208,512]{1,0:T(8,128)(2,1)S(1)}, bf16[208,512]{1,0:T(8,128)(2,1)S(1)}, u32[]{:S(2)}, u32[]{:S(2)}) %collective-permute-start.2) | collective-permute-done | bytes 213024 | tf_op jit(solution)/shard_map/ppermute | solution.py:273
  64.1 0.7 shard_map.89
  64.9 0.0 copy-start.1
  64.9 24.8 %all_to_all.26 = bf16[8,24,3584]{2,1,0:T(8,128)(2,1)S(1)} all-to-all(bf16[8,24,3584]{2,1,0:T(8,128)(2,1)S(1)} %bitcast.13), channel_id=1, replica_groups={{0,4,8,12,16,20,24,28},{32,36,40,44,48,52,56,60},{64,68,72,76,80,84,88,..., dimensions={0} | all-to-all | bytes 2752512 | tf_op jit(solution)/shard_map/all_to_all | solution.py:33
  89.7 0.4 shard_map.90
  90.0 12.5 %all_to_all.27.parts_ref = bf16[8,4,3584]{2,1,0:T(4,128)(2,1)S(1)} all-to-all(bf16[8,4,3584]{2,1,0:T(4,128)(2,1)S(1)} %shard_map.90), channel_id=1, replica_groups={{2,6,10,14,18,22,26,30},{34,38,42,46,50,54,58,62},{66,70,74,78,82,86,90..., dimensions={0} | all-to-all | bytes 458752 | tf_op jit(solution)/shard_map/all_to_all | solution.py:33
  102.6 0.7 shard_map.91
  103.2 9.1 %all_to_all.28.got_ref = bf16[4,4,3712]{2,1,0:T(4,128)(2,1)S(1)} all-to-all(bf16[4,4,3712]{2,1,0:T(4,128)(2,1)S(1)} %get-tuple-element.18), channel_id=1, replica_groups=mesh['section'=2,'ep'=128,'tp'=2] {'section','tp'}, dimensions={0} | all-to-all | bytes 237568 | tf_op jit(solution)/shard_map/all_to_all | solution.py:288
  112.3 0.7 shard_map.92
  (9 shorter events, 0.0 us)
Async XLA Ops:
  19.5 12.0 %copy-start = (bf16[1,1,3584,256]{3,2,1,0:T(8,128)(2,1)S(1)}, bf16[1,1,3584,256]{3,2,1,0:T(8,128)(2,1)}, u32[]{:S(2)}) copy-start(bf16[1,1,3584,256]{3,2,1,0:T(8,128)(2,1)} %param.11) | copy-start | bytes 5505028
  19.5 16.4 %copy-start.4 = (bf16[1,3584]{1,0:T(2,128)(2,1)S(1)}, bf16[1,3584]{1,0:T(2,128)(2,1)}, u32[]{:S(2)}) copy-start(bf16[1,3584]{1,0:T(2,128)(2,1)} %param.13) | copy-start | bytes 21508
  19.5 34.5 %copy-start.2 = (bf16[1,3584]{1,0:T(2,128)(2,1)S(1)}, bf16[1,3584]{1,0:T(2,128)(2,1)}, u32[]{:S(2)}) copy-start(bf16[1,3584]{1,0:T(2,128)(2,1)} %gain_ref.1) | copy-start | bytes 21508
  21.2 32.8 %all-to-all-start.1 = ((bf16[8,24,3584]{2,1,0:T(8,128)(2,1)}), bf16[8,24,3584]{2,1,0:T(8,128)(2,1)S(1)}, u32[]{:S(2)}, u32[]{:S(2)}) async-start(bf16[8,24,3584]{2,1,0:T(8,128)(2,1)} %bitcast.18), calls=%async_computation.1 | async-start | bytes 2752512 | tf_op jit(solution)/shard_map/all_to_all | solution.py:33
  31.5 22.5 %collective-permute-start.1 = (bf16[3584,256]{1,0:T(8,128)(2,1)S(1)}, bf16[3584,256]{1,0:T(8,128)(2,1)}, u32[]{:S(2)}, u32[]{:S(2)}) collective-permute-start(bf16[3584,256]{1,0:T(8,128)(2,1)S(1)} %bitcast.14), channel_id=1, source_target_pairs={{0,2},{2,0},{4,6},{6,4},{8,10},{10,8},{12,14},{14,12},{16,18},{18,... | collective-permute-start | bytes 5505032 | tf_op jit(solution)/shard_map/ppermute | solution.py:227
  33.5 25.4 %collective-permute-start.3 = (bf16[128,3584]{1,0:T(8,128)(2,1)}, bf16[128,3584]{1,0:T(8,128)(2,1)}, u32[]{:S(2)}, u32[]{:S(2)}) collective-permute-start(bf16[128,3584]{1,0:T(8,128)(2,1)} %bitcast.19), channel_id=1, source_target_pairs={{0,2},{2,0},{4,6},{6,4},{8,10},{10,8},{12,14},{14,12},{16,18},{18,... | collective-permute-start | bytes 2752520 | tf_op jit(solution)/shard_map/ppermute | solution.py:228
  35.9 7.1 %collective-permute-start = (bf16[1,3584]{1,0:T(2,128)(2,1)S(1)}, bf16[1,3584]{1,0:T(2,128)(2,1)S(1)}, u32[]{:S(2)}, u32[]{:S(2)}) collective-permute-start(bf16[1,3584]{1,0:T(2,128)(2,1)S(1)} %copy-done.4), channel_id=1, source_target_pairs={{0,256},{256,0},{1,257},{257,1},{2,258},{258,2},{3,259},{259,3},{4... | collective-permute-start | bytes 21512 | tf_op jit(solution)/shard_map/ppermute | solution.py:229
  54.0 4.9 %copy-start.3 = (bf16[1,1,128,3584]{3,2,1,0:T(8,128)(2,1)S(1)}, bf16[1,1,128,3584]{3,2,1,0:T(8,128)(2,1)}, u32[]{:S(2)}) copy-start(bf16[1,1,128,3584]{3,2,1,0:T(8,128)(2,1)} %param.12) | copy-start | bytes 2752516
  56.4 7.7 %collective-permute-start.2 = (bf16[208,512]{1,0:T(8,128)(2,1)S(1)}, bf16[208,512]{1,0:T(8,128)(2,1)S(1)}, u32[]{:S(2)}, u32[]{:S(2)}) collective-permute-start(bf16[208,512]{1,0:T(8,128)(2,1)S(1)} %get-tuple-element.16), channel_id=1, source_target_pairs={{0,1},{1,0},{2,3},{3,2},{4,5},{5,4},{6,7},{7,6},{8,9},{9,8},{10,11... | collective-permute-start | bytes 638984 | tf_op jit(solution)/shard_map/ppermute | solution.py:273
  64.9 37.7 %copy-start.1 = (bf16[1,4,3584]{2,1,0:T(4,128)(2,1)S(1)}, bf16[1,4,3584]{2,1,0:T(4,128)(2,1)}, u32[]{:S(2)}) copy-start(bf16[1,4,3584]{2,1,0:T(4,128)(2,1)} %param.7) | copy-start | bytes 86020
